TPU v7x, 1024 devices: a whole 8x8x8 slice. The times are simulated.
1024 devices in a mesh: dom: 256 (over z_hi, x, y, core), rep: 4 (over z_lo).
Axes of the slice: x: 8, y: 8, z: 8 (z_hi: 2, z_lo: 4; z = z_hi * 4 + z_lo), core: 2. Of those that a mesh axis runs over, the one named last changes fastest.
Arguments:
- features: bfloat16 [262144, 256], P(('dom', 'rep')), may hold values from -6 to 6
- tile_values: bfloat16 [2048, 20, 128, 128], P(('dom', 'rep')), may hold values from -0.4375 to 0.4375
- tile_cols: int32 [2048, 20], P(('dom', 'rep')), may hold values from 0 to 39
- tile_counts: int32 [2048], P(('dom', 'rep')), may hold values from 1 to 20, as said below
- weight: bfloat16 [256, 256], replicated, may hold values from -0.375 to 0.375
- cotangent: bfloat16 [262144, 256], P(('dom', 'rep')), may hold values from -6 to 6
Outputs:
- layer_out: bfloat16 [262144, 256], P(('dom', 'rep'))
- feat_grad: float32 [262144, 256], P(('dom', 'rep'))
- weight_grad: float32 [256, 256], replicated
Inputs may be any that keep to these rules, and one draw needn't show every extreme that they name: `tile_counts`: in every aligned block of 4 rows of tiles at least one row holds 20 live slots; other rows are skewed towards few slots.
All inputs are finite; a program needn't handle non-finite values.
Results may differ from a plain program's by a relative error of at most 0.0065.
Values may be sent and summed in bfloat16 or wider, within the bound.
No kernel may reach another device: no remote copies, remote signals or barrier semaphores. Data moves between devices by JAX's collectives and lax.ppermute only.
A program may use at most 64 MiB of HBM per device.

v0:
```python
import math

import jax
import jax.numpy as jnp
from jax import lax
from jax.sharding import PartitionSpec as P

REACH = 2


def from_behind(value, axis, by):
    length = lax.axis_size(axis)
    return lax.ppermute(value, axis, [(i, (i + by) % length) for i in range(length)])


def per_device(features, tile_values, tile_cols, tile_counts, weight, cotangent):
    rows = features.shape[0]
    width = features.shape[1]
    groups = lax.axis_size("dom")
    members = lax.axis_size("rep")
    offsets = list(range(-REACH, REACH + 1))
    group_rows = lax.all_gather(features, "rep", axis=0, tiled=True)
    pieces = []
    for offset in offsets:
        if offset == 0:
            pieces.append(group_rows)
        else:
            pieces.append(from_behind(group_rows, "dom", -offset))
    band = jnp.concatenate(pieces, 0)
    band_tiles = band.reshape(-1, 128, width)
    band_count = band_tiles.shape[0]
    slots = tile_cols.shape[1]
    live = jnp.arange(slots, dtype=jnp.int32)[None, :] < tile_counts[:, None]
    masked = jnp.where(live[:, :, None, None], tile_values, jnp.zeros_like(tile_values))
    picked = band_tiles[tile_cols]
    aggregated = jnp.einsum("tsij,tsjf->tif", masked, picked, preferred_element_type=jnp.float32)
    aggregated = aggregated.reshape(rows, width).astype(jnp.bfloat16)
    layer_out = jnp.dot(aggregated, weight, preferred_element_type=jnp.float32).astype(jnp.bfloat16)
    local_weight = jnp.dot(aggregated.T, cotangent, preferred_element_type=jnp.float32)
    back = jnp.dot(cotangent, weight.T, preferred_element_type=jnp.float32).astype(jnp.bfloat16)
    back_tiles = back.reshape(-1, 128, width)
    spread = jnp.einsum("tsji,tjf->tsif", masked, back_tiles, preferred_element_type=jnp.float32)
    onehot = (
        tile_cols[:, :, None] == jnp.arange(band_count, dtype=jnp.int32)[None, None, :]
    ).astype(jnp.float32)
    partial_sums = jnp.einsum("tsc,tsif->cif", onehot, spread)
    partial_sums = partial_sums.reshape(len(offsets), rows * members, width)
    total = jnp.zeros((rows * members, width), jnp.float32)
    for index, offset in enumerate(offsets):
        if offset == 0:
            total = total + partial_sums[index]
        else:
            total = total + from_behind(partial_sums[index], "dom", offset)
    feat_grad = lax.psum_scatter(total, "rep", scatter_dimension=0, tiled=True)
    summed = lax.psum(local_weight, ("dom", "rep"))
    weight_grad = summed / math.sqrt(rows * groups * members)
    return (layer_out, feat_grad, weight_grad)


def solution(mesh):
    placed = (
        P(("dom", "rep"), None),
        P(("dom", "rep"), None, None, None),
        P(("dom", "rep"), None),
        P(("dom", "rep")),
        P(),
        P(("dom", "rep"), None),
    )
    return jax.shard_map(
        per_device,
        mesh=mesh,
        in_specs=placed,
        out_specs=(P(("dom", "rep"), None), P(("dom", "rep"), None), P()),
        check_vma=False,
    )
```

profile of v0, /device:TPU:1, one launch (start us, length us, event | category | flops | bytes accessed | tf_op | source)
XLA Modules:
  0.0 432.2 jit_solution(2631853329825838327)
XLA Ops:
  8.1 21.2 %all_gather.3 = bf16[1024,256]{1,0:T(8,128)(2,1)} all-gather(bf16[256,256]{1,0:T(8,128)(2,1)} %param.6), channel_id=1, replica_groups=mesh['dom'=256,'rep'=4] {'rep'}, dimensions={0}, use_global_device_ids=true | all-gather | bytes 655360 | tf_op jit(solution)/shard_map/all_gather | solution.py:22
  29.3 3.8 collective-permute-start
  33.1 6.5 %collective-permute-start.1 = (bf16[1024,256]{1,0:T(8,128)(2,1)}, bf16[1024,256]{1,0:T(8,128)(2,1)}, u32[]{:S(2)}, u32[]{:S(2)}) collective-permute-start(bf16[1024,256]{1,0:T(8,128)(2,1)} %all_gather.3), channel_id=1, source_target_pairs={{0,4},{4,8},{8,12},{12,16},{16,20},{20,24},{24,28},{28,32},{32,36}... | collective-permute-start | bytes 1572872 | tf_op jit(solution)/shard_map/ppermute | solution.py:13
  39.5 5.0 %collective-permute-start.2 = (bf16[1024,256]{1,0:T(8,128)(2,1)}, bf16[1024,256]{1,0:T(8,128)(2,1)}, u32[]{:S(2)}, u32[]{:S(2)}) collective-permute-start(bf16[1024,256]{1,0:T(8,128)(2,1)} %all_gather.3), channel_id=1, source_target_pairs={{0,1020},{4,0},{8,4},{12,8},{16,12},{20,16},{24,20},{28,24},{32,28... | collective-permute-start | bytes 1572872 | tf_op jit(solution)/shard_map/ppermute | solution.py:13
  44.5 11.8 %collective-permute-start.3 = (bf16[1024,256]{1,0:T(8,128)(2,1)}, bf16[1024,256]{1,0:T(8,128)(2,1)}, u32[]{:S(2)}, u32[]{:S(2)}) collective-permute-start(bf16[1024,256]{1,0:T(8,128)(2,1)} %all_gather.3), channel_id=1, source_target_pairs={{0,1016},{4,1020},{8,0},{12,4},{16,8},{20,12},{24,16},{28,20},{32,... | collective-permute-start | bytes 1572872 | tf_op jit(solution)/shard_map/ppermute | solution.py:13
  56.3 0.7 iota_compare_fusion.1
  57.0 1.1 convolution_convert_fusion
  58.1 2.6 fusion.5
  60.8 2.1 fusion.2
  62.9 1.4 fusion.16
  64.3 1.3 copy.9
  65.6 3.4 collective-permute-start.4
  69.1 2.6 copy.10
  71.7 1.3 copy.12
  73.7 7.3 %collective-permute-start.5 = (f32[1024,256]{1,0:T(8,128)}, f32[1024,256]{1,0:T(8,128)}, u32[]{:S(2)}, u32[]{:S(2)}) collective-permute-start(f32[1024,256]{1,0:T(8,128)} %bitcast.12), channel_id=1, source_target_pairs={{0,1020},{4,0},{8,4},{12,8},{16,12},{20,16},{24,20},{28,24},{32,28... | collective-permute-start | bytes 3145736 | tf_op jit(solution)/shard_map/ppermute | solution.py:13
  81.1 1.9 constant_dynamic-update-slice_fusion.4
  82.9 1.9 collective-permute-start.6
  84.9 1.9 collective-permute-start.7
  86.8 1.9 constant_dynamic-update-slice_fusion.3
  88.7 1.9 constant_dynamic-update-slice_fusion.2
  90.6 1.9 constant_dynamic-update-slice_fusion.1
  92.5 1.9 constant_dynamic-update-slice_fusion
  94.4 4.2 gather_fusion
  98.6 2.3 fusion.6
  100.9 0.6 copy-done.3
  101.6 0.9 fusion.17
  102.6 20.3 %collective-permute-done.4 = f32[1024,256]{1,0:T(8,128)} collective-permute-done((f32[1024,256]{1,0:T(8,128)}, f32[1024,256]{1,0:T(8,128)}, u32[]{:S(2)}, u32[]{:S(2)}) %collective-permute-start.4) | collective-permute-done | bytes 1048608 | tf_op jit(solution)/shard_map/ppermute | solution.py:13
  122.9 41.3 %collective-permute-done.7 = f32[1024,256]{1,0:T(8,128)} collective-permute-done((f32[1024,256]{1,0:T(8,128)S(1)}, f32[1024,256]{1,0:T(8,128)}, u32[]{:S(2)}, u32[]{:S(2)}) %collective-permute-start.7) | collective-permute-done | bytes 1048608 | tf_op jit(solution)/shard_map/ppermute | solution.py:13
  164.2 3.5 fusion.8
  167.7 0.8 convolution_convert_fusion.1
  168.6 254.5 %all-reduce.2.cloned.1.call-done = f32[256,256]{1,0:T(8,128)} async-done(((f32[256,256]{1,0:T(8,128)}), f32[256,256]{1,0:T(8,128)}) %all-reduce.2.cloned.1.call-update) | async-done | bytes 262160 | tf_op jit(solution)/shard_map/psum | solution.py:55
  423.1 1.7 broadcast_multiply_fusion
  (27 shorter events, 0.9 us)
Async XLA Ops:
  8.0 49.0 %copy-start = (bf16[256,256]{1,0:T(8,128)(2,1)S(1)}, bf16[256,256]{1,0:T(8,128)(2,1)}, u32[]{:S(2)}) copy-start(bf16[256,256]{1,0:T(8,128)(2,1)} %param.11) | copy-start | bytes 393220
  8.0 52.8 %copy-start.5 = (s32[2,20]{1,0:T(2,128)S(1)}, s32[2,20]{1,0:T(2,128)}, u32[]{:S(2)}) copy-start(s32[2,20]{1,0:T(2,128)} %param.8) | copy-start | bytes 484
  8.0 415.1 %all-reduce.2.cloned.1.call-start = ((), (), s32[]{:S(2)}) async-start(), calls=%async_computation.2 | async-start | bytes 524288 | tf_op jit(solution)/shard_map/psum | solution.py:55
  29.3 44.5 %collective-permute-start = (bf16[1024,256]{1,0:T(8,128)(2,1)}, bf16[1024,256]{1,0:T(8,128)(2,1)}, u32[]{:S(2)}, u32[]{:S(2)}) collective-permute-start(bf16[1024,256]{1,0:T(8,128)(2,1)} %all_gather.3), channel_id=1, source_target_pairs={{0,8},{4,12},{8,16},{12,20},{16,24},{20,28},{24,32},{28,36},{32,40... | collective-permute-start | bytes 1572872 | tf_op jit(solution)/shard_map/ppermute | solution.py:13
  33.1 49.9 %collective-permute-start.1 = (bf16[1024,256]{1,0:T(8,128)(2,1)}, bf16[1024,256]{1,0:T(8,128)(2,1)}, u32[]{:S(2)}, u32[]{:S(2)}) collective-permute-start(bf16[1024,256]{1,0:T(8,128)(2,1)} %all_gather.3), channel_id=1, source_target_pairs={{0,4},{4,8},{8,12},{12,16},{16,20},{20,24},{24,28},{28,32},{32,36}... | collective-permute-start | bytes 1572872 | tf_op jit(solution)/shard_map/ppermute | solution.py:13
  39.5 45.3 %collective-permute-start.2 = (bf16[1024,256]{1,0:T(8,128)(2,1)}, bf16[1024,256]{1,0:T(8,128)(2,1)}, u32[]{:S(2)}, u32[]{:S(2)}) collective-permute-start(bf16[1024,256]{1,0:T(8,128)(2,1)} %all_gather.3), channel_id=1, source_target_pairs={{0,1020},{4,0},{8,4},{12,8},{16,12},{20,16},{24,20},{28,24},{32,28... | collective-permute-start | bytes 1572872 | tf_op jit(solution)/shard_map/ppermute | solution.py:13
  44.5 48.0 %collective-permute-start.3 = (bf16[1024,256]{1,0:T(8,128)(2,1)}, bf16[1024,256]{1,0:T(8,128)(2,1)}, u32[]{:S(2)}, u32[]{:S(2)}) collective-permute-start(bf16[1024,256]{1,0:T(8,128)(2,1)} %all_gather.3), channel_id=1, source_target_pairs={{0,1016},{4,1020},{8,0},{12,4},{16,8},{20,12},{24,16},{28,20},{32,... | collective-permute-start | bytes 1572872 | tf_op jit(solution)/shard_map/ppermute | solution.py:13
  65.6 57.3 %collective-permute-start.4 = (f32[1024,256]{1,0:T(8,128)}, f32[1024,256]{1,0:T(8,128)}, u32[]{:S(2)}, u32[]{:S(2)}) collective-permute-start(f32[1024,256]{1,0:T(8,128)} %bitcast.11), channel_id=1, source_target_pairs={{0,1016},{4,1020},{8,0},{12,4},{16,8},{20,12},{24,16},{28,20},{32,... | collective-permute-start | bytes 3145736 | tf_op jit(solution)/shard_map/ppermute | solution.py:13
  73.7 49.1 %collective-permute-start.5 = (f32[1024,256]{1,0:T(8,128)}, f32[1024,256]{1,0:T(8,128)}, u32[]{:S(2)}, u32[]{:S(2)}) collective-permute-start(f32[1024,256]{1,0:T(8,128)} %bitcast.12), channel_id=1, source_target_pairs={{0,1020},{4,0},{8,4},{12,8},{16,12},{20,16},{24,20},{28,24},{32,28... | collective-permute-start | bytes 3145736 | tf_op jit(solution)/shard_map/ppermute | solution.py:13
  82.9 39.9 %collective-permute-start.6 = (f32[1024,256]{1,0:T(8,128)}, f32[1024,256]{1,0:T(8,128)}, u32[]{:S(2)}, u32[]{:S(2)}) collective-permute-start(f32[1024,256]{1,0:T(8,128)} %bitcast.14), channel_id=1, source_target_pairs={{0,4},{4,8},{8,12},{12,16},{16,20},{20,24},{24,28},{28,32},{32,36}... | collective-permute-start | bytes 3145736 | tf_op jit(solution)/shard_map/ppermute | solution.py:13
  84.9 79.3 %collective-permute-start.7 = (f32[1024,256]{1,0:T(8,128)S(1)}, f32[1024,256]{1,0:T(8,128)}, u32[]{:S(2)}, u32[]{:S(2)}) collective-permute-start(f32[1024,256]{1,0:T(8,128)S(1)} %bitcast.38), channel_id=1, source_target_pairs={{0,8},{4,12},{8,16},{12,20},{16,24},{20,28},{24,32},{28,36},{32,40... | collective-permute-start | bytes 3145736 | tf_op jit(solution)/shard_map/ppermute | solution.py:13
  94.4 4.2 copy-start.1
  100.9 0.7 copy-start.3
  102.5 65.2 %copy-start.2 = (bf16[256,256]{1,0:T(8,128)(2,1)S(1)}, bf16[256,256]{1,0:T(8,128)(2,1)}, u32[]{:S(2)}) copy-start(bf16[256,256]{1,0:T(8,128)(2,1)} %param.10) | copy-start | bytes 393220
  102.5 65.2 %copy-start.4 = (bf16[2,128,256]{2,1,0:T(8,128)(2,1)S(1)}, bf16[2,128,256]{2,1,0:T(8,128)(2,1)}, u32[]{:S(2)}) copy-start(bf16[2,128,256]{2,1,0:T(8,128)(2,1)} %copy-done.3) | copy-start | bytes 393220
  102.5 322.2 %reduce-scatter.2.cloned.1.call-start = ((), (), s32[]{:S(2)}) async-start(), calls=%async_computation.1 | async-start | bytes 1310720 | tf_op jit(solution)/shard_map/reduce_scatter | solution.py:54
Sparse Core Ops, SparseCore 0:
  102.6 320.3 all-reduce.1
Sparse Core Ops, SparseCore 1:
  167.8 27.7 reduce-scatter.1
where the time goes:
time: 433 us; the launch traced here: 432 us
  waiting for transfers between devices  316 us (73%)
  starting transfers between devices  41.6 us (10%)
  local copies, waits for them, and re-layouts  21.7 us (5%)
  blocking collectives  21.2 us (5%)
  between operations  15.7 us (4%)
  matrix products  9.89 us (2%)
  other arithmetic  5.89 us (1%)
    psum x1, waiting for transfers between devices, per_device(): summed = lax.psum(local_weight, ('dom', 'rep'))  255 us
    ppermute x8, waiting for transfers between devices, from_behind(): lax.ppermute(value, axis, [(i, (i + by) % length) for i in range(length)])  61.6 us
    ppermute x8, starting transfers between devices, from_behind(): lax.ppermute(value, axis, [(i, (i + by) % length) for i in range(length)])  41.6 us
    all_gather x1, blocking collectives, per_device(): group_rows = lax.all_gather(features, 'rep', axis=0, tiled=True)  21.2 us
  transfers between devices with their start and end apart: 10, of which 3 were waited for; matrix products, arithmetic and copies ran while one was open for 9% of the time, Pallas kernels for 0%

commit v1 on v0

v1 whole, which is shorter than its diff:
```python
import functools
import math

import jax
import jax.numpy as jnp
from jax import lax
from jax.experimental import pallas as pl
from jax.experimental.pallas import tpu as pltpu
from jax.sharding import Mesh, PartitionSpec as P

TILE = 128
ALL = ("zh", "x", "y", "c", "zl")
DOM = ("zh", "x", "y", "c")
PLANE = ("x", "y")
COLUMN = ("zh", "zl", "c")
VMEM_LIMIT = 24 * 1024 * 1024


def near_pairs(groups):
    pairs = []
    for d in range(groups):
        k, c = d // 2, d % 2
        pairs.append((d, (2 * (k - 1) + 1 if c == 0 else 2 * (k + 1)) % groups))
    return pairs


def far_pairs(groups, outward):
    pairs = []
    for d in range(groups):
        step = 2 if (d % 2 == 1) == outward else -2
        pairs.append((d, (d + step) % groups))
    return pairs


def tile_of(col, core, per_group):
    band = col // per_group
    band = jnp.where(core == 0, 4 - band, band)
    place = jnp.where(band >= 2, band - 2, 4 - band)
    return place * per_group + col % per_group


def forward_kernel(core_ref, counts, cols, tiles, weight, cotangent, x0, x1, x2, x3, x4, out, local, band, sems):
    sources = (x0, x1, x2, x3, x4)
    rows = x0.shape[0]
    per_group = rows // TILE
    copies = []
    for index, source in enumerate(sources):
        copy = pltpu.make_async_copy(source, band.at[pl.ds(index * rows, rows)], sems.at[index])
        copy.start()
        copies.append(copy)
    for copy in copies:
        copy.wait()
    core = core_ref[0]
    slots = tiles.shape[1]
    sums = []
    for t in range(tiles.shape[0]):
        count = counts[t]
        total = jnp.zeros((TILE, x0.shape[1]), jnp.float32)
        for s in range(0, slots, 2):
            left, right = [], []
            for one in (s, s + 1):
                start = pl.multiple_of(tile_of(cols[t, one], core, per_group) * TILE, TILE)
                value = tiles[t, one]
                left.append(jnp.where(one < count, value, jnp.zeros_like(value)))
                right.append(band[pl.ds(start, TILE), :])
            total = total + jnp.dot(
                jnp.concatenate(left, 1), jnp.concatenate(right, 0), preferred_element_type=jnp.float32
            )
        sums.append(total.astype(jnp.bfloat16))
    aggregated = jnp.concatenate(sums, 0)
    out[...] = jnp.dot(aggregated, weight[...], preferred_element_type=jnp.float32).astype(jnp.bfloat16)
    grad = lax.dot_general(
        aggregated, cotangent[...], (((0,), (0,)), ((), ())), preferred_element_type=jnp.float32
    ).astype(jnp.bfloat16)
    height = grad.shape[0]
    local[0:height, :] = grad[:, 0:TILE]
    local[height : 2 * height, :] = grad[:, TILE : 2 * TILE]


def scatter_tiles(core, counts, cols, tiles, cotangent, total, least, most, per_group):
    for t in range(tiles.shape[0]):
        grads = cotangent[t * TILE : (t + 1) * TILE, :]

        def step(s, carry):
            place = tile_of(cols[t, s], core, per_group)

            @pl.when((place >= least) & (place < most))
            def _():
                start = pl.multiple_of((place - least) * TILE, TILE)
                total[pl.ds(start, TILE), :] += lax.dot_general(
                    tiles[t, s], grads, (((0,), (0,)), ((), ())), preferred_element_type=jnp.float32
                )

            return carry

        lax.fori_loop(0, counts[t], step, 0)


def send_kernel(core_ref, counts, cols, tiles, cotangent, out, total):
    per_group = out.shape[0] // TILE // 2
    total[...] = jnp.zeros_like(total)
    scatter_tiles(core_ref[0], counts, cols, tiles, cotangent, total, 3 * per_group, 5 * per_group, per_group)
    out[...] = total[...].astype(jnp.bfloat16)


def keep_kernel(core_ref, counts, cols, tiles, cotangent, received, own, near, far, total):
    rows = own.shape[0]
    per_group = rows // TILE
    total[0 : 2 * rows, :] = received[...].astype(jnp.float32)
    total[2 * rows : 3 * rows, :] = jnp.zeros_like(total[2 * rows : 3 * rows, :])
    scatter_tiles(core_ref[0], counts, cols, tiles, cotangent, total, 0, 3 * per_group, per_group)
    own[...] = total[0:rows, :]
    near[...] = total[rows : 2 * rows, :].astype(jnp.bfloat16)
    far[...] = total[2 * rows : 3 * rows, :].astype(jnp.bfloat16)


def params():
    return pltpu.CompilerParams(vmem_limit_bytes=VMEM_LIMIT)


def per_device(features, tile_values, tile_cols, tile_counts, weight, cotangent):
    rows, width = features.shape
    slots = tile_cols.shape[1]
    groups = math.prod(lax.axis_size(axis) for axis in DOM)
    members = lax.axis_size("zl")
    group_rows = rows * members
    core = lax.axis_index("c").astype(jnp.int32).reshape(1)
    near = near_pairs(groups)
    swap = [(0, 1), (1, 0)]
    smem = pl.BlockSpec(memory_space=pltpu.SMEM)
    vmem = pl.BlockSpec(memory_space=pltpu.VMEM)
    anywhere = pl.BlockSpec(memory_space=pl.ANY)
    flops = 2 * 2 * slots * TILE * TILE * width

    x0 = lax.all_gather(features, "zl", axis=0, tiled=True)
    x1 = lax.ppermute(x0, DOM, near)
    x2 = lax.ppermute(x0, DOM, far_pairs(groups, False))
    x3 = lax.ppermute(x0, "c", swap)
    x4 = lax.ppermute(x1, "c", swap)

    sent = pl.pallas_call(
        send_kernel,
        out_shape=jax.ShapeDtypeStruct((2 * group_rows, width), jnp.bfloat16),
        in_specs=[smem, smem, smem, vmem, vmem],
        out_specs=vmem,
        scratch_shapes=[pltpu.VMEM((2 * group_rows, width), jnp.float32)],
        compiler_params=params(),
        cost_estimate=pl.CostEstimate(flops=flops, bytes_accessed=4 << 20, transcendentals=0),
        name="send",
    )(core, tile_counts, tile_cols, tile_values, cotangent)
    received = lax.ppermute(sent, "c", swap)
    own, near_sum, far_sum = pl.pallas_call(
        keep_kernel,
        out_shape=(
            jax.ShapeDtypeStruct((group_rows, width), jnp.float32),
            jax.ShapeDtypeStruct((group_rows, width), jnp.bfloat16),
            jax.ShapeDtypeStruct((group_rows, width), jnp.bfloat16),
        ),
        in_specs=[smem, smem, smem, vmem, vmem, vmem],
        out_specs=(vmem, vmem, vmem),
        scratch_shapes=[pltpu.VMEM((3 * group_rows, width), jnp.float32)],
        compiler_params=params(),
        cost_estimate=pl.CostEstimate(flops=flops, bytes_accessed=8 << 20, transcendentals=0),
        name="keep",
    )(core, tile_counts, tile_cols, tile_values, cotangent, received)
    near_in = lax.ppermute(near_sum, DOM, near)
    far_in = lax.ppermute(far_sum, DOM, far_pairs(groups, True))

    layer_out, local = pl.pallas_call(
        forward_kernel,
        out_shape=(
            jax.ShapeDtypeStruct((rows, width), jnp.bfloat16),
            jax.ShapeDtypeStruct((2 * width, TILE), jnp.bfloat16),
        ),
        in_specs=[smem, smem, smem, vmem, vmem, vmem] + [anywhere] * 5,
        out_specs=(vmem, vmem),
        scratch_shapes=[
            pltpu.VMEM((5 * group_rows, width), jnp.bfloat16),
            pltpu.SemaphoreType.DMA((5,)),
        ],
        compiler_params=params(),
        cost_estimate=pl.CostEstimate(flops=flops, bytes_accessed=6 << 20, transcendentals=0),
        name="forward",
    )(core, tile_counts, tile_cols, tile_values, weight, cotangent, x0, x1, x2, x3, x4)

    plane = math.prod(lax.axis_size(axis) for axis in PLANE)
    column = math.prod(lax.axis_size(axis) for axis in COLUMN)
    parts = lax.all_to_all(local.reshape(plane, -1, TILE), PLANE, 0, 0)
    part = jnp.sum(parts.astype(jnp.float32), 0)
    parts = lax.all_to_all(jnp.broadcast_to(part[None], (column,) + part.shape), COLUMN, 0, 0)
    part = jnp.sum(parts, 0) / math.sqrt(rows * groups * members)
    part = part.astype(jnp.bfloat16)
    parts = lax.all_to_all(jnp.broadcast_to(part[None], (plane,) + part.shape), PLANE, 0, 0)
    parts = parts.reshape(2, width, TILE).astype(jnp.float32)
    weight_grad = jnp.concatenate([parts[0], parts[1]], 1)

    total = (own + near_in.astype(jnp.float32) + far_in.astype(jnp.float32)).astype(jnp.bfloat16)
    mine = lax.psum_scatter(total, "zl", scatter_dimension=0, tiled=True)
    feat_grad = lax.dot_general(mine, weight, (((1,), (1,)), ((), ())), preferred_element_type=jnp.float32)
    return (layer_out, feat_grad, weight_grad)


def solution(mesh):
    split = Mesh(mesh.devices.reshape(2, 8, 8, 2, 4), ALL)
    rows = P(ALL)
    return jax.shard_map(
        per_device,
        mesh=split,
        in_specs=(rows, rows, rows, rows, P(), rows),
        out_specs=(rows, rows, P()),
        check_vma=False,
    )
```

time: 433 us -> 165 us (0.38)
  waiting for transfers between devices: 316 us -> 15.9 us
  blocking collectives: 21.2 us -> 59.5 us
  local copies, waits for them, and re-layouts: 21.7 us -> 3.61 us
  starting transfers between devices: 41.6 us -> 57.8 us
  Pallas kernels: 0 us -> 9.35 us
  matrix products: 9.89 us -> 1.83 us
    psum x1 -> x0, waiting for transfers between devices: 255 us -> none  [per_device(): summed = lax.psum(local_weight, ('dom', 'rep'))]
    all_to_all x0 -> x2, blocking collectives: none -> 45.8 us  [the longest x1 27.1 us: per_device(): lax.all_to_all(jnp.broadcast_to(part[None], (column,) + part.shape), COLU...]
    ppermute x8 -> x7, waiting for transfers between devices: 61.6 us -> 15.9 us  [the longest x1 15.9 us: per_device(): far_in = lax.ppermute(far_sum, DOM, far_pairs(groups, True))]
    ppermute x8 -> x7, starting transfers between devices: 41.6 us -> 51.4 us  [the longest x1 15.9 us: per_device(): received = lax.ppermute(sent, 'c', swap)]
    pallas_call x0 -> x3, Pallas kernels: none -> 9.35 us  [the longest x1 3.9 us: per_device(): pl.pallas_call(keep_kernel, out_shape=(jax.ShapeDtypeStruct((group_rows,...]
    dot_general x6 -> x1, matrix products: 9.89 us -> 1.83 us  [per_device(): lax.dot_general(mine, weight, (((1,), (1,)), ((), ())), preferred_element...]
    all_gather x1, blocking collectives: 21.2 us -> 13.7 us  [per_device(): x0 = lax.all_gather(features, 'zl', axis=0, tiled=True)]
    slice x6 -> x0, local copies, waits for them, and re-layouts: 7.32 us -> none  [the longest x5 6.98 us: per_device(): total = total + from_behind(partial_sums[index], 'dom', offset)]
  transfers between devices with their start and end apart: 10 -> 9, of which waited for: 3 -> 1; matrix products, arithmetic and copies ran while one was open for 9% -> 1% of each run, Pallas kernels for 0% -> 4%
where the time goes in v1:
time: 165 us; the launch traced here: 164 us
  blocking collectives  59.5 us (36%)
  starting transfers between devices  57.8 us (35%)
  waiting for transfers between devices  15.9 us (10%)
  between operations  14.2 us (9%)
  Pallas kernels  9.35 us (6%)
  local copies, waits for them, and re-layouts  3.61 us (2%)
  matrix products  1.83 us (1%)
  other arithmetic  1.79 us (1%)
    all_to_all x1, blocking collectives, per_device(): lax.all_to_all(jnp.broadcast_to(part[None], (column,) + part.shape), COLU...  27.1 us
    all_to_all x1, blocking collectives, per_device(): lax.all_to_all(jnp.broadcast_to(part[None], (plane,) + part.shape), PLANE...  18.7 us
    ppermute x1, waiting for transfers between devices, per_device(): far_in = lax.ppermute(far_sum, DOM, far_pairs(groups, True))  15.9 us
    ppermute x1, starting transfers between devices, per_device(): received = lax.ppermute(sent, 'c', swap)  15.9 us
    ppermute x1, starting transfers between devices, per_device(): x2 = lax.ppermute(x0, DOM, far_pairs(groups, False))  13.9 us
    all_gather x1, blocking collectives, per_device(): x0 = lax.all_gather(features, 'zl', axis=0, tiled=True)  13.7 us
    ppermute x1, starting transfers between devices, per_device(): x4 = lax.ppermute(x1, 'c', swap)  12.1 us
    all_to_all x1, starting transfers between devices, per_device(): parts = lax.all_to_all(local.reshape(plane, -1, TILE), PLANE, 0, 0)  6.35 us
  transfers between devices with their start and end apart: 9, of which 1 were waited for; matrix products, arithmetic and copies ran while one was open for 1% of the time, Pallas kernels for 4%

profile of v1, /device:TPU:1, one launch (start us, length us, event | category | flops | bytes accessed | tf_op | source)
XLA Modules:
  0.0 164.0 jit_solution(8779971206938524023)
XLA Ops:
  7.2 1.3 copy-done
  8.5 0.9 copy-done.1
  9.4 0.7 copy-done.4
  10.1 0.7 copy-done.5
  10.7 3.2 %send.1 = bf16[2048,256]{1,0:T(8,128)(2,1)S(1)} custom-call(s32[1]{0:T(128)} %bitcast.core_ref, s32[2]{0:T(128)S(1)} %copy-done.5, s32[2,20]{1,0:T(2,128)S(1)} %copy-done.4, bf16[2,20,128,128]{3,2,1,0:T(8,128)(2,1)S(1)} %copy-done, bf16[256,256]{1,0:T(8,128)(2,1)S(1)} %copy-done.1), custom_call_target="tpu_custom_call" | custom-call | flops 335544320 | bytes 4194304 | tf_op jit(solution)/shard_map/send/pallas_call | solution.py:141
  14.0 15.9 %collective-permute-start.4 = (bf16[2048,256]{1,0:T(8,128)(2,1)S(1)}, bf16[2048,256]{1,0:T(8,128)(2,1)S(1)}, u32[]{:S(2)}, u32[]{:S(2)}) collective-permute-start(bf16[2048,256]{1,0:T(8,128)(2,1)S(1)} %send.1), channel_id=1, source_target_pairs={{0,4},{4,0},{1,5},{5,1},{2,6},{6,2},{3,7},{7,3},{8,12},{12,8},{9,1... | collective-permute-start | bytes 3145736 | tf_op jit(solution)/shard_map/ppermute | solution.py:151
  29.8 13.7 %all_gather.3.x0 = bf16[1024,256]{1,0:T(8,128)(2,1)S(1)} all-gather(bf16[256,256]{1,0:T(8,128)(2,1)S(1)} %copy-done.6), channel_id=1, replica_groups=mesh['zh'=2,'x'=8,'y'=8,'c'=2,'zl'=4] {'zl'}, dimensions={0}, use_global_device_ids=true | all-gather | bytes 655360 | tf_op jit(solution)/shard_map/all_gather | solution.py:135
  43.5 2.0 %collective-permute-start = (bf16[1024,256]{1,0:T(8,128)(2,1)S(1)}, bf16[1024,256]{1,0:T(8,128)(2,1)S(1)}, u32[]{:S(2)}, u32[]{:S(2)}) collective-permute-start(bf16[1024,256]{1,0:T(8,128)(2,1)S(1)} %all_gather.3.x0), channel_id=1, source_target_pairs={{0,1020},{4,8},{8,4},{12,16},{16,12},{20,24},{24,20},{28,32},{32,2... | collective-permute-start | bytes 1572872 | tf_op jit(solution)/shard_map/ppermute | solution.py:136
  45.6 13.9 %collective-permute-start.1 = (bf16[1024,256]{1,0:T(8,128)(2,1)S(1)}, bf16[1024,256]{1,0:T(8,128)(2,1)S(1)}, u32[]{:S(2)}, u32[]{:S(2)}) collective-permute-start(bf16[1024,256]{1,0:T(8,128)(2,1)S(1)} %all_gather.3.x0), channel_id=1, source_target_pairs={{0,8},{4,1020},{8,16},{12,4},{16,24},{20,12},{24,32},{28,20},{32,4... | collective-permute-start | bytes 1572872 | tf_op jit(solution)/shard_map/ppermute | solution.py:137
  59.4 1.9 %collective-permute-start.2 = (bf16[1024,256]{1,0:T(8,128)(2,1)S(1)}, bf16[1024,256]{1,0:T(8,128)(2,1)S(1)}, u32[]{:S(2)}, u32[]{:S(2)}) collective-permute-start(bf16[1024,256]{1,0:T(8,128)(2,1)S(1)} %all_gather.3.x0), channel_id=1, source_target_pairs={{0,4},{4,0},{1,5},{5,1},{2,6},{6,2},{3,7},{7,3},{8,12},{12,8},{9,1... | collective-permute-start | bytes 1572872 | tf_op jit(solution)/shard_map/ppermute | solution.py:138
  61.4 0.0 collective-permute-done.x1
  61.4 12.1 %collective-permute-start.3 = (bf16[1024,256]{1,0:T(8,128)(2,1)S(1)}, bf16[1024,256]{1,0:T(8,128)(2,1)S(1)}, u32[]{:S(2)}, u32[]{:S(2)}) collective-permute-start(bf16[1024,256]{1,0:T(8,128)(2,1)S(1)} %collective-permute-done.x1), channel_id=1, source_target_pairs={{0,4},{4,0},{1,5},{5,1},{2,6},{6,2},{3,7},{7,3},{8,12},{12,8},{9,1... | collective-permute-start | bytes 1572872 | tf_op jit(solution)/shard_map/ppermute | solution.py:139
  73.5 0.0 collective-permute-done.4.received
  73.5 3.9 %keep.1 = (f32[1024,256]{1,0:T(8,128)S(1)}, bf16[1024,256]{1,0:T(8,128)(2,1)S(1)}, bf16[1024,256]{1,0:T(8,128)(2,1)S(1)}) custom-call(s32[1]{0:T(128)} %bitcast.core_ref, s32[2]{0:T(128)S(1)} %copy-done.5, s32[2,20]{1,0:T(2,128)S(1)} %copy-done.4, bf16[2,20,128,128]{3,2,1,0:T(8,128)(2,1)S(1)} %copy-done, bf16[256,256]{1,0:T(8,128)(2,1)S(1)} %copy-done.1, ...), custom_call_target="tpu_custom_call" | custom-call | flops 335544320 | bytes 8388608 | tf_op jit(solution)/shard_map/keep/pallas_call | solution.py:152
  77.4 1.9 %collective-permute-start.6 = (bf16[1024,256]{1,0:T(8,128)(2,1)S(1)}, bf16[1024,256]{1,0:T(8,128)(2,1)S(1)}, u32[]{:S(2)}, u32[]{:S(2)}) collective-permute-start(bf16[1024,256]{1,0:T(8,128)(2,1)S(1)} %get-tuple-element.11), channel_id=1, source_target_pairs={{0,1016},{4,12},{8,0},{12,20},{16,8},{20,28},{24,16},{28,36},{32,2... | collective-permute-start | bytes 1572872 | tf_op jit(solution)/shard_map/ppermute | solution.py:167
  79.3 3.7 %collective-permute-start.5 = (bf16[1024,256]{1,0:T(8,128)(2,1)S(1)}, bf16[1024,256]{1,0:T(8,128)(2,1)S(1)}, u32[]{:S(2)}, u32[]{:S(2)}) collective-permute-start(bf16[1024,256]{1,0:T(8,128)(2,1)S(1)} %get-tuple-element.10), channel_id=1, source_target_pairs={{0,1020},{4,8},{8,4},{12,16},{16,12},{20,24},{24,20},{28,32},{32,2... | collective-permute-start | bytes 1572872 | tf_op jit(solution)/shard_map/ppermute | solution.py:166
  83.0 0.0 collective-permute-done.1.x2
  83.0 0.0 collective-permute-done.2.x3
  83.1 0.0 collective-permute-done.3.x4
  83.1 2.2 %forward.1 = (bf16[256,256]{1,0:T(8,128)(2,1)}, bf16[512,128]{1,0:T(8,128)(2,1)}) custom-call(s32[1]{0:T(128)} %bitcast.core_ref, s32[2]{0:T(128)S(1)} %copy-done.5, s32[2,20]{1,0:T(2,128)S(1)} %copy-done.4, bf16[2,20,128,128]{3,2,1,0:T(8,128)(2,1)S(1)} %copy-done, bf16[256,256]{1,0:T(8,128)(2,1)S(1)} %copy-done.3, bf16[256,256]{1,0:T(8,128)(2,1)S(1)} %copy-done.2, ...), custom_call_target="tpu_custom_call" | custom-call | flops 335544320 | bytes 6291456 | tf_op jit(solution)/shard_map/forward/pallas_call | solution.py:169
  85.3 6.4 %all-to-all-start = ((bf16[64,8,128]{2,1,0:T(8,128)(2,1)}), bf16[64,8,128]{2,1,0:T(8,128)(2,1)S(1)}, u32[]{:S(2)}, u32[]{:S(2)}) async-start(bf16[64,8,128]{2,1,0:T(8,128)(2,1)} %bitcast.1), calls=%async_computation.1 | async-start | bytes 262144 | tf_op jit(solution)/shard_map/all_to_all | solution.py:188
  91.7 0.0 reduce-scatter.2.cloned.1.call-start
  91.7 15.9 %collective-permute-done.6 = bf16[1024,256]{1,0:T(8,128)(2,1)S(1)} collective-permute-done((bf16[1024,256]{1,0:T(8,128)(2,1)S(1)}, bf16[1024,256]{1,0:T(8,128)(2,1)S(1)}, u32[]{:S(2)}, u32[]{:S(2)}) %collective-permute-start.6) | collective-permute-done | bytes 524320 | tf_op jit(solution)/shard_map/ppermute | solution.py:167
  107.6 0.0 collective-permute-done.5
  107.6 1.0 add_convert_fusion
  108.6 0.0 reduce-scatter.2.cloned.1.call-update
  108.6 0.0 all-to-all-done
  108.6 0.1 convert_reduce_fusion
  108.7 27.1 %all_to_all.15 = f32[16,8,128]{2,1,0:T(8,128)S(1)} all-to-all(f32[16,8,128]{2,1,0:T(8,128)S(1)} %broadcast_in_dim.4), channel_id=1, replica_groups=mesh['zh'=2,'x'=8,'y'=8,'c'=2,'zl'=4] {'zh','zl','c'}, dimensions={0} | all-to-all | bytes 131072 | tf_op jit(solution)/shard_map/all_to_all | solution.py:190
  135.8 18.7 %all_to_all.16 = bf16[64,8,128]{2,1,0:T(8,128)(2,1)S(1)} all-to-all(bf16[64,8,128]{2,1,0:T(8,128)(2,1)S(1)} %broadcast_in_dim.5), channel_id=1, replica_groups=mesh['zh'=2,'x'=8,'y'=8,'c'=2,'zl'=4] {'x','y'}, dimensions={0} | all-to-all | bytes 262144 | tf_op jit(solution)/shard_map/all_to_all | solution.py:193
  154.6 0.7 pad_maximum_fusion
  155.3 1.8 %fusion = f32[256,256]{1,0:T(8,128)} fusion(bf16[256,256]{1,0:T(8,128)(2,1)} %reduce-scatter.2.cloned.1.call-done, bf16[256,256]{1,0:T(8,128)(2,1)S(1)} %copy-done.3), kind=kOutput, calls=%fused_computation.6 | convolution fusion | flops 33554432 | bytes 524288 | tf_op jit(solution)/shard_map/dot_general | solution.py:199
  (17 shorter events, 0.1 us)
Async XLA Ops:
  7.2 1.3 copy-start
  8.5 0.9 copy-start.1
  9.4 0.7 copy-start.4
  10.1 0.7 copy-start.5
  10.7 19.1 %copy-start.6 = (bf16[256,256]{1,0:T(8,128)(2,1)S(1)}, bf16[256,256]{1,0:T(8,128)(2,1)}, u32[]{:S(2)}) copy-start(bf16[256,256]{1,0:T(8,128)(2,1)} %param.6) | copy-start | bytes 393220
  14.0 59.5 %collective-permute-start.4 = (bf16[2048,256]{1,0:T(8,128)(2,1)S(1)}, bf16[2048,256]{1,0:T(8,128)(2,1)S(1)}, u32[]{:S(2)}, u32[]{:S(2)}) collective-permute-start(bf16[2048,256]{1,0:T(8,128)(2,1)S(1)} %send.1), channel_id=1, source_target_pairs={{0,4},{4,0},{1,5},{5,1},{2,6},{6,2},{3,7},{7,3},{8,12},{12,8},{9,1... | collective-permute-start | bytes 3145736 | tf_op jit(solution)/shard_map/ppermute | solution.py:151
  43.5 39.6 %copy-start.2 = (bf16[256,256]{1,0:T(8,128)(2,1)S(1)}, bf16[256,256]{1,0:T(8,128)(2,1)}, u32[]{:S(2)}) copy-start(bf16[256,256]{1,0:T(8,128)(2,1)} %cotangent.5) | copy-start | bytes 393220
  43.5 39.6 %copy-start.3 = (bf16[256,256]{1,0:T(8,128)(2,1)S(1)}, bf16[256,256]{1,0:T(8,128)(2,1)}, u32[]{:S(2)}) copy-start(bf16[256,256]{1,0:T(8,128)(2,1)} %weight.1) | copy-start | bytes 393220
  43.5 17.9 %collective-permute-start = (bf16[1024,256]{1,0:T(8,128)(2,1)S(1)}, bf16[1024,256]{1,0:T(8,128)(2,1)S(1)}, u32[]{:S(2)}, u32[]{:S(2)}) collective-permute-start(bf16[1024,256]{1,0:T(8,128)(2,1)S(1)} %all_gather.3.x0), channel_id=1, source_target_pairs={{0,1020},{4,8},{8,4},{12,16},{16,12},{20,24},{24,20},{28,32},{32,2... | collective-permute-start | bytes 1572872 | tf_op jit(solution)/shard_map/ppermute | solution.py:136
  45.6 37.5 %collective-permute-start.1 = (bf16[1024,256]{1,0:T(8,128)(2,1)S(1)}, bf16[1024,256]{1,0:T(8,128)(2,1)S(1)}, u32[]{:S(2)}, u32[]{:S(2)}) collective-permute-start(bf16[1024,256]{1,0:T(8,128)(2,1)S(1)} %all_gather.3.x0), channel_id=1, source_target_pairs={{0,8},{4,1020},{8,16},{12,4},{16,24},{20,12},{24,32},{28,20},{32,4... | collective-permute-start | bytes 1572872 | tf_op jit(solution)/shard_map/ppermute | solution.py:137
  59.4 23.6 %collective-permute-start.2 = (bf16[1024,256]{1,0:T(8,128)(2,1)S(1)}, bf16[1024,256]{1,0:T(8,128)(2,1)S(1)}, u32[]{:S(2)}, u32[]{:S(2)}) collective-permute-start(bf16[1024,256]{1,0:T(8,128)(2,1)S(1)} %all_gather.3.x0), channel_id=1, source_target_pairs={{0,4},{4,0},{1,5},{5,1},{2,6},{6,2},{3,7},{7,3},{8,12},{12,8},{9,1... | collective-permute-start | bytes 1572872 | tf_op jit(solution)/shard_map/ppermute | solution.py:138
  61.4 21.7 %collective-permute-start.3 = (bf16[1024,256]{1,0:T(8,128)(2,1)S(1)}, bf16[1024,256]{1,0:T(8,128)(2,1)S(1)}, u32[]{:S(2)}, u32[]{:S(2)}) collective-permute-start(bf16[1024,256]{1,0:T(8,128)(2,1)S(1)} %collective-permute-done.x1), channel_id=1, source_target_pairs={{0,4},{4,0},{1,5},{5,1},{2,6},{6,2},{3,7},{7,3},{8,12},{12,8},{9,1... | collective-permute-start | bytes 1572872 | tf_op jit(solution)/shard_map/ppermute | solution.py:139
  77.4 30.2 %collective-permute-start.6 = (bf16[1024,256]{1,0:T(8,128)(2,1)S(1)}, bf16[1024,256]{1,0:T(8,128)(2,1)S(1)}, u32[]{:S(2)}, u32[]{:S(2)}) collective-permute-start(bf16[1024,256]{1,0:T(8,128)(2,1)S(1)} %get-tuple-element.11), channel_id=1, source_target_pairs={{0,1016},{4,12},{8,0},{12,20},{16,8},{20,28},{24,16},{28,36},{32,2... | collective-permute-start | bytes 1572872 | tf_op jit(solution)/shard_map/ppermute | solution.py:167
  79.3 28.3 %collective-permute-start.5 = (bf16[1024,256]{1,0:T(8,128)(2,1)S(1)}, bf16[1024,256]{1,0:T(8,128)(2,1)S(1)}, u32[]{:S(2)}, u32[]{:S(2)}) collective-permute-start(bf16[1024,256]{1,0:T(8,128)(2,1)S(1)} %get-tuple-element.10), channel_id=1, source_target_pairs={{0,1020},{4,8},{8,4},{12,16},{16,12},{20,24},{24,20},{28,32},{32,2... | collective-permute-start | bytes 1572872 | tf_op jit(solution)/shard_map/ppermute | solution.py:166
  85.3 23.3 %all-to-all-start = ((bf16[64,8,128]{2,1,0:T(8,128)(2,1)}), bf16[64,8,128]{2,1,0:T(8,128)(2,1)S(1)}, u32[]{:S(2)}, u32[]{:S(2)}) async-start(bf16[64,8,128]{2,1,0:T(8,128)(2,1)} %bitcast.1), calls=%async_computation.1 | async-start | bytes 262144 | tf_op jit(solution)/shard_map/all_to_all | solution.py:188
  91.7 63.6 %reduce-scatter.2.cloned.1.call-start = ((), (), s32[]{:S(2)}) async-start(), calls=%async_computation.4 | async-start | bytes 655360 | tf_op jit(solution)/shard_map/reduce_scatter | solution.py:198
Sparse Core Ops, SparseCore 0:
  108.7 39.1 reduce-scatter.1

commit v2 on v1

v2 whole, which is shorter than its diff:
```python
import functools
import math

import jax
import jax.numpy as jnp
from jax import lax
from jax.experimental import pallas as pl
from jax.experimental.pallas import tpu as pltpu
from jax.sharding import Mesh, PartitionSpec as P

TILE = 128
ALL = ("zh", "x", "y", "c", "zl")
DOM = ("zh", "x", "y", "c")
PLANE = ("x", "y")
COLUMN = ("zh", "zl", "c")
SEND_BYTES = 64 << 20
FORWARD_BYTES = 64 << 20
VMEM_LIMIT = 24 * 1024 * 1024


def near_pairs(groups):
    pairs = []
    for d in range(groups):
        k, c = d // 2, d % 2
        pairs.append((d, (2 * (k - 1) + 1 if c == 0 else 2 * (k + 1)) % groups))
    return pairs


def far_pairs(groups, outward):
    pairs = []
    for d in range(groups):
        step = 2 if (d % 2 == 1) == outward else -2
        pairs.append((d, (d + step) % groups))
    return pairs


def tile_of(col, core, per_group):
    band = col // per_group
    band = jnp.where(core == 0, 4 - band, band)
    place = jnp.where(band >= 2, band - 2, 4 - band)
    return place * per_group + col % per_group


def turned_tile_of(col, core, member, members, per_group):
    tile = tile_of(col, core, per_group)
    share = per_group // members
    within = tile % per_group
    turn = (member - within // share + members) % members
    return tile - within + turn * share + within % share


def forward_kernel(place_ref, counts, cols, tiles, weight, mine, turn1, turn2, turn3, other, out, band, sems):
    turns = (mine, turn1, turn2, turn3)
    members = len(turns)
    rows = mine.shape[0] // 3
    group_rows = rows * members
    per_group = group_rows // TILE
    sources = []
    for index, turn in enumerate(turns):
        for place in range(3):
            sources.append((turn.at[pl.ds(place * rows, rows)], place * group_rows + index * rows, rows))
    sources.append((other, 3 * group_rows, 2 * group_rows))
    copies = []
    for index, (source, start, size) in enumerate(sources):
        copy = pltpu.make_async_copy(source, band.at[pl.ds(start, size)], sems.at[index])
        copy.start()
        copies.append(copy)
    for copy in copies:
        copy.wait()
    member = place_ref[1]
    width = mine.shape[1]
    core = place_ref[0]
    slots = tiles.shape[1]
    sums = []
    for t in range(tiles.shape[0]):
        count = counts[t]
        total = jnp.zeros((TILE, width), jnp.float32)
        for s in range(0, slots, 2):
            left, right = [], []
            for one in (s, s + 1):
                start = pl.multiple_of(turned_tile_of(cols[t, one], core, member, members, per_group) * TILE, TILE)
                value = tiles[t, one]
                left.append(jnp.where(one < count, value, jnp.zeros_like(value)))
                right.append(band[pl.ds(start, TILE), :])
            total = total + jnp.dot(
                jnp.concatenate(left, 1), jnp.concatenate(right, 0), preferred_element_type=jnp.float32
            )
        sums.append(total.astype(jnp.bfloat16))
    aggregated = jnp.concatenate(sums, 0)
    out[...] = jnp.dot(aggregated, weight[...], preferred_element_type=jnp.float32).astype(jnp.bfloat16)


def scatter_tiles(core, counts, cols, tiles, cotangent, total, least, most, per_group):
    for t in range(tiles.shape[0]):
        grads = cotangent[t * TILE : (t + 1) * TILE, :]

        def step(s, carry):
            place = tile_of(cols[t, s], core, per_group)

            @pl.when((place >= least) & (place < most))
            def _():
                start = pl.multiple_of((place - least) * TILE, TILE)
                total[pl.ds(start, TILE), :] += lax.dot_general(
                    tiles[t, s], grads, (((0,), (0,)), ((), ())), preferred_element_type=jnp.float32
                )

            return carry

        lax.fori_loop(0, counts[t], step, 0)


def send_kernel(place_ref, counts, cols, tiles, cotangent, out, total):
    per_group = out.shape[0] // TILE // 2
    total[...] = jnp.zeros_like(total)
    scatter_tiles(place_ref[0], counts, cols, tiles, cotangent, total, 3 * per_group, 5 * per_group, per_group)
    out[...] = total[...].astype(jnp.bfloat16)


def keep_kernel(place_ref, counts, cols, tiles, cotangent, received, features, out, passed, total):
    passed[...] = features[...]
    members, blocks, rows, _ = out.shape
    group_rows = members * rows
    per_group = group_rows // TILE
    total[0 : 2 * group_rows, :] = received[...].astype(jnp.float32)
    total[2 * group_rows : 3 * group_rows, :] = jnp.zeros_like(total[2 * group_rows : 3 * group_rows, :])
    scatter_tiles(place_ref[0], counts, cols, tiles, cotangent, total, 0, 3 * per_group, per_group)
    for m in range(members):
        for b in range(blocks):
            start = b * group_rows + m * rows
            out[m, b] = total[start : start + rows, :].astype(jnp.bfloat16)


def fold_kernel(parts, out):
    part = jnp.sum(parts[...].astype(jnp.float32), 0)
    for i in range(out.shape[0]):
        out[i] = part


def products_kernel(parts, features, near_x, far_x, own, near, far, local, mine):
    total = parts[0].astype(jnp.float32)
    for m in range(1, parts.shape[0]):
        total = total + parts[m].astype(jnp.float32)
    own[...] = total[0]
    rounded = total.astype(jnp.bfloat16)
    near[...] = rounded[1]
    far[...] = rounded[2]
    grad = jnp.zeros((features.shape[1], rounded.shape[2]), jnp.float32)
    for block, rows in enumerate((features, near_x, far_x)):
        grad = grad + lax.dot_general(
            rows[...], rounded[block], (((0,), (0,)), ((), ())), preferred_element_type=jnp.float32
        )
    grad = grad.astype(jnp.bfloat16)
    height = grad.shape[0]
    local[0:height, :] = grad[:, 0:TILE]
    local[height : 2 * height, :] = grad[:, TILE : 2 * TILE]
    size = features.shape[0]
    for index, rows in enumerate((features, near_x, far_x)):
        mine[index * size : (index + 1) * size, :] = rows[...]


def spread_kernel(scale, folded, own, near, far, weight, spread, feat):
    part = (jnp.sum(folded[...], 0) * scale).astype(jnp.bfloat16)
    for i in range(spread.shape[0]):
        spread[i] = part
    total = own[...] + near[...].astype(jnp.float32) + far[...].astype(jnp.float32)
    feat[...] = lax.dot_general(
        total.astype(jnp.bfloat16), weight[...], (((1,), (1,)), ((), ())), preferred_element_type=jnp.float32
    )


def pack_kernel(mine, turn1, turn2, turn3, after, out, sems):
    rows = mine.shape[0] // 3
    turns = (mine, turn1, turn2, turn3)
    copies = []
    for place in range(2):
        for index, turn in enumerate(turns):
            number = place * len(turns) + index
            copy = pltpu.make_async_copy(
                turn.at[pl.ds(place * rows, rows)], out.at[pl.ds(number * rows, rows)], sems.at[number]
            )
            copy.start()
            copies.append(copy)
    for copy in copies:
        copy.wait()


def last_kernel(parts, after, grad):
    count, depth, _ = parts.shape
    height = grad.shape[0]
    half = height // depth
    for side in range(count // half):
        grad[:, side * TILE : (side + 1) * TILE] = (
            parts[side * half : (side + 1) * half].astype(jnp.float32).reshape(height, TILE)
        )


def params():
    return pltpu.CompilerParams(vmem_limit_bytes=VMEM_LIMIT)


def per_device(features, tile_values, tile_cols, tile_counts, weight, cotangent):
    rows, width = features.shape
    slots = tile_cols.shape[1]
    groups = math.prod(lax.axis_size(axis) for axis in DOM)
    members = lax.axis_size("zl")
    group_rows = rows * members
    near = near_pairs(groups)
    swap = [(0, 1), (1, 0)]
    smem = pl.BlockSpec(memory_space=pltpu.SMEM)
    vmem = pl.BlockSpec(memory_space=pltpu.VMEM)
    anywhere = pl.BlockSpec(memory_space=pl.ANY)
    flops = 2 * 2 * slots * TILE * TILE * width

    place = jnp.stack([lax.axis_index("c"), lax.axis_index("zl")]).astype(jnp.int32)

    def turned(value):
        return [
            lax.ppermute(value, "zl", [(m, (m + turn) % members) for m in range(members)]) for turn in range(1, members)
        ]


    sent = pl.pallas_call(
        send_kernel,
        out_shape=jax.ShapeDtypeStruct((2 * group_rows, width), jnp.bfloat16),
        in_specs=[smem, smem, smem, vmem, vmem],
        out_specs=vmem,
        scratch_shapes=[pltpu.VMEM((2 * group_rows, width), jnp.float32)],
        compiler_params=params(),
        cost_estimate=pl.CostEstimate(flops=flops, bytes_accessed=SEND_BYTES, transcendentals=0),
        name="send",
    )(place, tile_counts, tile_cols, tile_values, cotangent)
    received = lax.ppermute(sent, "c", swap)
    kept, passed = pl.pallas_call(
        keep_kernel,
        out_shape=(
            jax.ShapeDtypeStruct((members, 3, rows, width), jnp.bfloat16),
            jax.ShapeDtypeStruct(features.shape, jnp.bfloat16),
        ),
        in_specs=[smem, smem, smem, vmem, vmem, vmem, vmem],
        out_specs=(vmem, vmem),
        scratch_shapes=[pltpu.VMEM((3 * group_rows, width), jnp.float32)],
        compiler_params=params(),
        cost_estimate=pl.CostEstimate(flops=flops, bytes_accessed=8 << 20, transcendentals=0),
        name="keep",
    )(place, tile_counts, tile_cols, tile_values, cotangent, received, features)
    kept = lax.all_to_all(kept, "zl", 0, 0)
    near_x = lax.ppermute(passed, DOM, near)
    far_x = lax.ppermute(passed, DOM, far_pairs(groups, False))

    own, near_sum, far_sum, local, mine = pl.pallas_call(
        products_kernel,
        out_shape=(
            jax.ShapeDtypeStruct((rows, width), jnp.float32),
            jax.ShapeDtypeStruct((rows, width), jnp.bfloat16),
            jax.ShapeDtypeStruct((rows, width), jnp.bfloat16),
            jax.ShapeDtypeStruct((2 * width, TILE), jnp.bfloat16),
            jax.ShapeDtypeStruct((3 * rows, width), jnp.bfloat16),
        ),
        in_specs=[vmem] * 4,
        out_specs=(vmem,) * 5,
        compiler_params=params(),
        cost_estimate=pl.CostEstimate(flops=flops, bytes_accessed=3 << 20, transcendentals=0),
        name="products",
    )(kept, features, near_x, far_x)

    plane = math.prod(lax.axis_size(axis) for axis in PLANE)
    column = math.prod(lax.axis_size(axis) for axis in COLUMN)
    parts = lax.all_to_all(local.reshape(plane, -1, TILE), PLANE, 0, 0)
    near_in = lax.ppermute(near_sum, DOM, near)
    far_in = lax.ppermute(far_sum, DOM, far_pairs(groups, True))
    turns = turned(mine)
    part = pl.pallas_call(
        fold_kernel,
        out_shape=jax.ShapeDtypeStruct((column,) + parts.shape[1:], jnp.float32),
        in_specs=[vmem],
        out_specs=vmem,
        compiler_params=params(),
        name="fold",
    )(parts)
    folded = lax.all_to_all(part, COLUMN, 0, 0)
    spread, feat_grad = pl.pallas_call(
        functools.partial(spread_kernel, 1 / math.sqrt(rows * groups * members)),
        out_shape=(
            jax.ShapeDtypeStruct(parts.shape, jnp.bfloat16),
            jax.ShapeDtypeStruct((rows, width), jnp.float32),
        ),
        in_specs=[vmem] * 5,
        out_specs=(vmem, vmem),
        compiler_params=params(),
        name="spread",
    )(folded, own, near_in, far_in, weight)
    parts = lax.all_to_all(spread, PLANE, 0, 0)
    packed = pl.pallas_call(
        pack_kernel,
        out_shape=jax.ShapeDtypeStruct((2 * group_rows, width), jnp.bfloat16),
        in_specs=[anywhere] * 5,
        out_specs=anywhere,
        scratch_shapes=[pltpu.SemaphoreType.DMA((8,))],
        compiler_params=params(),
        cost_estimate=pl.CostEstimate(flops=0, bytes_accessed=2 << 20, transcendentals=0),
        name="pack",
    )(mine, *turns, parts)
    other = lax.ppermute(packed, "c", swap)
    layer_out = pl.pallas_call(
        forward_kernel,
        out_shape=jax.ShapeDtypeStruct((rows, width), jnp.bfloat16),
        in_specs=[smem, smem, smem, vmem, vmem] + [anywhere] * 5,
        out_specs=vmem,
        scratch_shapes=[
            pltpu.VMEM((5 * group_rows, width), jnp.bfloat16),
            pltpu.SemaphoreType.DMA((13,)),
        ],
        compiler_params=params(),
        cost_estimate=pl.CostEstimate(flops=flops, bytes_accessed=FORWARD_BYTES, transcendentals=0),
        name="forward",
    )(place, tile_counts, tile_cols, tile_values, weight, mine, *turns, other)
    weight_grad = pl.pallas_call(
        last_kernel,
        out_shape=jax.ShapeDtypeStruct(weight.shape, jnp.float32),
        in_specs=[vmem, anywhere],
        out_specs=vmem,
        compiler_params=params(),
        name="last",
    )(parts, layer_out)
    return (layer_out, feat_grad, weight_grad)


def solution(mesh):
    split = Mesh(mesh.devices.reshape(2, 8, 8, 2, 4), ALL)
    rows = P(ALL)
    return jax.shard_map(
        per_device,
        mesh=split,
        in_specs=(rows, rows, rows, rows, P(), rows),
        out_specs=(rows, rows, P()),
        check_vma=False,
    )
```

time: 165 us -> 171 us (1.036)
  blocking collectives: 59.5 us -> 0 us
  waiting for transfers between devices: 15.9 us -> 67.1 us
  starting transfers between devices: 57.8 us -> 81.3 us
  between operations: 14.2 us -> 0.84 us
  Pallas kernels: 9.35 us -> 16.1 us
  matrix products: 1.83 us -> 0 us
  other arithmetic: 1.79 us -> 0.08 us
    all_to_all x0 -> x3, waiting for transfers between devices: none -> 57.9 us  [the longest x1 23.3 us: per_device(): kept = lax.all_to_all(kept, 'zl', 0, 0)]
    all_to_all x2 -> x0, blocking collectives: 45.8 us -> none  [the longest x1 27.1 us: per_device(): lax.all_to_all(jnp.broadcast_to(part[None], (column,) + part.shape), COLU...]
    all_to_all x0 -> x3, starting transfers between devices: none -> 25 us  [the longest x1 14.6 us: per_device(): folded = lax.all_to_all(part, COLUMN, 0, 0)]
    ppermute x1, waiting for transfers between devices: 15.9 us -> 0.01 us  [per_device(): far_in = lax.ppermute(far_sum, DOM, far_pairs(groups, True))]
    all_gather x1 -> x0, blocking collectives: 13.7 us -> none  [per_device(): x0 = lax.all_gather(features, 'zl', axis=0, tiled=True)]
    pallas_call x2 -> x7, Pallas kernels: 6.13 us -> 14.1 us  [the longest x1 4.73 us: per_device(): pl.pallas_call(keep_kernel, out_shape=(jax.ShapeDtypeStruct((members, 3,...]
    ppermute x4 -> x6, waiting for transfers between devices: 0.01 us -> 6.92 us  [the longest x1 4.64 us: per_device(): near_x = lax.ppermute(passed, DOM, near)]
    ppermute x4 -> x6, starting transfers between devices: 29.9 us -> 26.2 us  [the longest x1 12.2 us: per_device(): far_x = lax.ppermute(passed, DOM, far_pairs(groups, False))]
  transfers between devices with their start and end apart: 9 -> 13, of which waited for: 1 -> 6; matrix products, arithmetic and copies ran while one was open for 1% -> 0% of each run, Pallas kernels for 4% -> 1%
where the time goes in v2:
time: 171 us
  starting transfers between devices  81.3 us (48%)
  waiting for transfers between devices  67.1 us (39%)
  Pallas kernels  16.1 us (9%)
  local copies, waits for them, and re-layouts  5.13 us (3%)
    all_to_all x1, waiting for transfers between devices, per_device(): kept = lax.all_to_all(kept, 'zl', 0, 0)  23.3 us
    all_to_all x1, waiting for transfers between devices, per_device(): folded = lax.all_to_all(part, COLUMN, 0, 0)  23.2 us
    ppermute x1, starting transfers between devices, per_device(): received = lax.ppermute(sent, 'c', swap)  17.3 us
    all_to_all x1, starting transfers between devices, per_device(): folded = lax.all_to_all(part, COLUMN, 0, 0)  14.6 us
    ppermute x1, starting transfers between devices, per_device(): far_x = lax.ppermute(passed, DOM, far_pairs(groups, False))  12.2 us
    all_to_all x1, waiting for transfers between devices, per_device(): parts = lax.all_to_all(spread, PLANE, 0, 0)  11.5 us
    ppermute x3, starting transfers between devices, turned(): lax.ppermute(value, 'zl', [(m, (m + turn) % members) for m in range(membe...  8.09 us
    all_to_all x1, starting transfers between devices, per_device(): parts = lax.all_to_all(spread, PLANE, 0, 0)  6.8 us
  transfers between devices with their start and end apart: 13, of which 6 were waited for; matrix products, arithmetic and copies ran while one was open for 0% of the time, Pallas kernels for 1%

profile of v2, /device:TPU:1, one launch (start us, length us, event | category | flops | bytes accessed | tf_op | source)
XLA Modules:
  0.0 170.6 jit_solution(18076044513641461830)
XLA Ops:
  0.7 1.3 copy-done
  2.0 0.9 copy-done.2
  2.9 0.7 copy-done.6
  3.6 0.7 copy-done.8
  4.3 1.9 %send.1 = bf16[2048,256]{1,0:T(8,128)(2,1)S(1)} custom-call(s32[2]{0:T(128)S(1)} %pad_add_fusion.place_ref, s32[2]{0:T(128)S(1)} %copy-done.8, s32[2,20]{1,0:T(2,128)S(1)} %copy-done.6, bf16[2,20,128,128]{3,2,1,0:T(8,128)(2,1)S(1)} %copy-done, bf16[256,256]{1,0:T(8,128)(2,1)S(1)} %copy-done.2), custom_call_target="tpu_custom_call" | custom-call | flops 335544320 | bytes 67108864 | tf_op jit(solution)/shard_map/send/pallas_call | solution.py:222
  6.2 17.3 %collective-permute-start = (bf16[2048,256]{1,0:T(8,128)(2,1)S(1)}, bf16[2048,256]{1,0:T(8,128)(2,1)S(1)}, u32[]{:S(2)}, u32[]{:S(2)}) collective-permute-start(bf16[2048,256]{1,0:T(8,128)(2,1)S(1)} %send.1), channel_id=1, source_target_pairs={{0,4},{4,0},{1,5},{5,1},{2,6},{6,2},{3,7},{7,3},{8,12},{12,8},{9,1... | collective-permute-start | bytes 3145736 | tf_op jit(solution)/shard_map/ppermute | solution.py:232
  23.5 2.3 %collective-permute-done.received = bf16[2048,256]{1,0:T(8,128)(2,1)S(1)} collective-permute-done((bf16[2048,256]{1,0:T(8,128)(2,1)S(1)}, bf16[2048,256]{1,0:T(8,128)(2,1)S(1)}, u32[]{:S(2)}, u32[]{:S(2)}) %collective-permute-start) | collective-permute-done | bytes 1048608 | tf_op jit(solution)/shard_map/ppermute | solution.py:232
  25.8 4.7 %keep.1 = (bf16[4,3,256,256]{3,2,1,0:T(8,128)(2,1)}, bf16[256,256]{1,0:T(8,128)(2,1)S(1)}) custom-call(s32[2]{0:T(128)S(1)} %pad_add_fusion.place_ref, s32[2]{0:T(128)S(1)} %copy-done.8, s32[2,20]{1,0:T(2,128)S(1)} %copy-done.6, bf16[2,20,128,128]{3,2,1,0:T(8,128)(2,1)S(1)} %copy-done, bf16[256,256]{1,0:T(8,128)(2,1)S(1)} %copy-done.2, ...), custom_call_target="tpu_custom_call" | custom-call | flops 335544320 | bytes 8388608 | tf_op jit(solution)/shard_map/keep/pallas_call | solution.py:233
  30.5 3.6 %all-to-all-start = ((bf16[4,3,256,256]{3,2,1,0:T(8,128)(2,1)}), bf16[4,3,256,256]{3,2,1,0:T(8,128)(2,1)S(1)}, u32[]{:S(2)}, u32[]{:S(2)}) async-start(bf16[4,3,256,256]{3,2,1,0:T(8,128)(2,1)} %get-tuple-element.12), calls=%async_computation | async-start | bytes 3145728 | tf_op jit(solution)/shard_map/all_to_all | solution.py:246
  34.1 12.2 %collective-permute-start.2 = (bf16[256,256]{1,0:T(8,128)(2,1)S(1)}, bf16[256,256]{1,0:T(8,128)(2,1)S(1)}, u32[]{:S(2)}, u32[]{:S(2)}) collective-permute-start(bf16[256,256]{1,0:T(8,128)(2,1)S(1)} %get-tuple-element.13), channel_id=1, source_target_pairs={{0,8},{4,1020},{8,16},{12,4},{16,24},{20,12},{24,32},{28,20},{32,4... | collective-permute-start | bytes 393224 | tf_op jit(solution)/shard_map/ppermute | solution.py:248
  46.3 1.9 %collective-permute-start.1 = (bf16[256,256]{1,0:T(8,128)(2,1)S(1)}, bf16[256,256]{1,0:T(8,128)(2,1)S(1)}, u32[]{:S(2)}, u32[]{:S(2)}) collective-permute-start(bf16[256,256]{1,0:T(8,128)(2,1)S(1)} %get-tuple-element.13), channel_id=1, source_target_pairs={{0,1020},{4,8},{8,4},{12,16},{16,12},{20,24},{24,20},{28,32},{32,2... | collective-permute-start | bytes 393224 | tf_op jit(solution)/shard_map/ppermute | solution.py:247
  48.3 4.6 %collective-permute-done.1.near_x = bf16[256,256]{1,0:T(8,128)(2,1)S(1)} collective-permute-done((bf16[256,256]{1,0:T(8,128)(2,1)S(1)}, bf16[256,256]{1,0:T(8,128)(2,1)S(1)}, u32[]{:S(2)}, u32[]{:S(2)}) %collective-permute-start.1) | collective-permute-done | bytes 131104 | tf_op jit(solution)/shard_map/ppermute | solution.py:247
  52.9 23.3 %all-to-all-done.parts = bf16[4,3,256,256]{3,2,1,0:T(8,128)(2,1)S(1)} async-done(((bf16[4,3,256,256]{3,2,1,0:T(8,128)(2,1)}), bf16[4,3,256,256]{3,2,1,0:T(8,128)(2,1)S(1)}, u32[]{:S(2)}, u32[]{:S(2)}) %all-to-all-start) | async-done | bytes 1572896 | tf_op jit(solution)/shard_map/all_to_all | solution.py:246
  76.2 1.1 products.1
  77.9 4.6 %all-to-all-start.1 = ((bf16[64,8,128]{2,1,0:T(8,128)(2,1)}), bf16[64,8,128]{2,1,0:T(8,128)(2,1)S(1)}, u32[]{:S(2)}, u32[]{:S(2)}) async-start(bf16[64,8,128]{2,1,0:T(8,128)(2,1)} %bitcast.2), calls=%async_computation.1 | async-start | bytes 262144 | tf_op jit(solution)/shard_map/all_to_all | solution.py:268
  82.6 4.0 %collective-permute-start.5 = (bf16[768,256]{1,0:T(8,128)(2,1)S(1)}, bf16[768,256]{1,0:T(8,128)(2,1)S(1)}, u32[]{:S(2)}, u32[]{:S(2)}) collective-permute-start(bf16[768,256]{1,0:T(8,128)(2,1)S(1)} %get-tuple-element.14.mine), channel_id=1, source_target_pairs={{0,3},{1,0},{2,1},{3,2},{4,7},{5,4},{6,5},{7,6},{8,11},{9,8},{10,9... | collective-permute-start | bytes 1179656 | tf_op jit(solution)/shard_map/ppermute | solution.py:218
  86.5 1.9 %collective-permute-start.4 = (bf16[768,256]{1,0:T(8,128)(2,1)S(1)}, bf16[768,256]{1,0:T(8,128)(2,1)S(1)}, u32[]{:S(2)}, u32[]{:S(2)}) collective-permute-start(bf16[768,256]{1,0:T(8,128)(2,1)S(1)} %get-tuple-element.14.mine), channel_id=1, source_target_pairs={{0,2},{1,3},{2,0},{3,1},{4,6},{5,7},{6,4},{7,5},{8,10},{9,11},{10,... | collective-permute-start | bytes 1179656 | tf_op jit(solution)/shard_map/ppermute | solution.py:218
  88.5 2.2 %collective-permute-start.3 = (bf16[768,256]{1,0:T(8,128)(2,1)S(1)}, bf16[768,256]{1,0:T(8,128)(2,1)S(1)}, u32[]{:S(2)}, u32[]{:S(2)}) collective-permute-start(bf16[768,256]{1,0:T(8,128)(2,1)S(1)} %get-tuple-element.14.mine), channel_id=1, source_target_pairs={{0,1},{1,2},{2,3},{3,0},{4,5},{5,6},{6,7},{7,4},{8,9},{9,10},{10,1... | collective-permute-start | bytes 1179656 | tf_op jit(solution)/shard_map/ppermute | solution.py:218
  90.7 5.1 %collective-permute-start.6 = (bf16[256,256]{1,0:T(8,128)(2,1)}, bf16[256,256]{1,0:T(8,128)(2,1)S(1)}, u32[]{:S(2)}, u32[]{:S(2)}) collective-permute-start(bf16[256,256]{1,0:T(8,128)(2,1)} %copy-done.11), channel_id=1, source_target_pairs={{0,1020},{4,8},{8,4},{12,16},{16,12},{20,24},{24,20},{28,32},{32,2... | collective-permute-start | bytes 393224 | tf_op jit(solution)/shard_map/ppermute | solution.py:269
  95.8 3.1 %collective-permute-start.7 = (bf16[256,256]{1,0:T(8,128)(2,1)}, bf16[256,256]{1,0:T(8,128)(2,1)S(1)}, u32[]{:S(2)}, u32[]{:S(2)}) collective-permute-start(bf16[256,256]{1,0:T(8,128)(2,1)} %copy-done.10), channel_id=1, source_target_pairs={{0,1016},{4,12},{8,0},{12,20},{16,8},{20,28},{24,16},{28,36},{32,2... | collective-permute-start | bytes 393224 | tf_op jit(solution)/shard_map/ppermute | solution.py:270
  98.9 0.7 fold.1
  99.6 14.6 %all-to-all-start.2 = ((f32[16,8,128]{2,1,0:T(8,128)}), f32[16,8,128]{2,1,0:T(8,128)S(1)}, u32[]{:S(2)}, u32[]{:S(2)}) async-start(f32[16,8,128]{2,1,0:T(8,128)} %fold.1), calls=%async_computation.2 | async-start | bytes 131072 | tf_op jit(solution)/shard_map/all_to_all | solution.py:280
  114.3 23.2 %all-to-all-done.2.folded = f32[16,8,128]{2,1,0:T(8,128)S(1)} async-done(((f32[16,8,128]{2,1,0:T(8,128)}), f32[16,8,128]{2,1,0:T(8,128)S(1)}, u32[]{:S(2)}, u32[]{:S(2)}) %all-to-all-start.2) | async-done | bytes 65568 | tf_op jit(solution)/shard_map/all_to_all | solution.py:280
  137.4 0.9 spread.1
  138.4 6.8 %all-to-all-start.3 = ((bf16[64,8,128]{2,1,0:T(8,128)(2,1)}), bf16[64,8,128]{2,1,0:T(8,128)(2,1)S(1)}, u32[]{:S(2)}, u32[]{:S(2)}) async-start(bf16[64,8,128]{2,1,0:T(8,128)(2,1)} %get-tuple-element.19), calls=%async_computation.3 | async-start | bytes 262144 | tf_op jit(solution)/shard_map/all_to_all | solution.py:292
  145.2 11.5 %all-to-all-done.3.after.parts = bf16[64,8,128]{2,1,0:T(8,128)(2,1)S(1)} async-done(((bf16[64,8,128]{2,1,0:T(8,128)(2,1)}), bf16[64,8,128]{2,1,0:T(8,128)(2,1)S(1)}, u32[]{:S(2)}, u32[]{:S(2)}) %all-to-all-start.3) | async-done | bytes 131104 | tf_op jit(solution)/shard_map/all_to_all | solution.py:292
  156.7 1.4 pack.1
  158.1 4.0 %collective-permute-start.8 = (bf16[2048,256]{1,0:T(8,128)(2,1)S(1)}, bf16[2048,256]{1,0:T(8,128)(2,1)S(1)}, u32[]{:S(2)}, u32[]{:S(2)}) collective-permute-start(bf16[2048,256]{1,0:T(8,128)(2,1)S(1)} %pack.1), channel_id=1, source_target_pairs={{0,4},{4,0},{1,5},{5,1},{2,6},{6,2},{3,7},{7,3},{8,12},{12,8},{9,1... | collective-permute-start | bytes 3145736 | tf_op jit(solution)/shard_map/ppermute | solution.py:303
  162.1 2.3 %collective-permute-done.8.other = bf16[2048,256]{1,0:T(8,128)(2,1)S(1)} collective-permute-done((bf16[2048,256]{1,0:T(8,128)(2,1)S(1)}, bf16[2048,256]{1,0:T(8,128)(2,1)S(1)}, u32[]{:S(2)}, u32[]{:S(2)}) %collective-permute-start.8) | collective-permute-done | bytes 1048608 | tf_op jit(solution)/shard_map/ppermute | solution.py:303
  164.4 4.6 %forward.1.after = bf16[256,256]{1,0:T(8,128)(2,1)} custom-call(s32[2]{0:T(128)S(1)} %pad_add_fusion.place_ref, s32[2]{0:T(128)S(1)} %copy-done.9, s32[2,20]{1,0:T(2,128)S(1)} %copy-done.7, bf16[2,20,128,128]{3,2,1,0:T(8,128)(2,1)S(1)} %copy-done.1, bf16[256,256]{1,0:T(8,128)(2,1)S(1)} %copy-done.4, bf16[768,256]{1,0:T(8,128)(2,1)S(1)} %get-tuple-element.14.mine, ...), custom_call_target="tpu_custom_call" | custom-call | flops 335544320 | bytes 67108864 | tf_op jit(solution)/shard_map/forward/pallas_call | solution.py:304
  169.0 0.9 copy-done.5
  169.9 0.7 last.1
  (27 shorter events, 0.8 us)
Async XLA Ops:
  0.7 1.3 copy-start
  2.0 0.9 copy-start.2
  2.9 0.7 copy-start.6
  3.6 0.7 copy-start.8
  4.3 21.5 %copy-start.3 = (bf16[256,256]{1,0:T(8,128)(2,1)S(1)}, bf16[256,256]{1,0:T(8,128)(2,1)}, u32[]{:S(2)}) copy-start(bf16[256,256]{1,0:T(8,128)(2,1)} %features.3) | copy-start | bytes 393220
  6.2 19.6 %collective-permute-start = (bf16[2048,256]{1,0:T(8,128)(2,1)S(1)}, bf16[2048,256]{1,0:T(8,128)(2,1)S(1)}, u32[]{:S(2)}, u32[]{:S(2)}) collective-permute-start(bf16[2048,256]{1,0:T(8,128)(2,1)S(1)} %send.1), channel_id=1, source_target_pairs={{0,4},{4,0},{1,5},{5,1},{2,6},{6,2},{3,7},{7,3},{8,12},{12,8},{9,1... | collective-permute-start | bytes 3145736 | tf_op jit(solution)/shard_map/ppermute | solution.py:232
  30.5 45.6 %all-to-all-start = ((bf16[4,3,256,256]{3,2,1,0:T(8,128)(2,1)}), bf16[4,3,256,256]{3,2,1,0:T(8,128)(2,1)S(1)}, u32[]{:S(2)}, u32[]{:S(2)}) async-start(bf16[4,3,256,256]{3,2,1,0:T(8,128)(2,1)} %get-tuple-element.12), calls=%async_computation | async-start | bytes 3145728 | tf_op jit(solution)/shard_map/all_to_all | solution.py:246
  34.1 103.3 %copy-start.4 = (bf16[256,256]{1,0:T(8,128)(2,1)S(1)}, bf16[256,256]{1,0:T(8,128)(2,1)}, u32[]{:S(2)}) copy-start(bf16[256,256]{1,0:T(8,128)(2,1)} %weight.3) | copy-start | bytes 393220
  34.1 14.1 %collective-permute-start.2 = (bf16[256,256]{1,0:T(8,128)(2,1)S(1)}, bf16[256,256]{1,0:T(8,128)(2,1)S(1)}, u32[]{:S(2)}, u32[]{:S(2)}) collective-permute-start(bf16[256,256]{1,0:T(8,128)(2,1)S(1)} %get-tuple-element.13), channel_id=1, source_target_pairs={{0,8},{4,1020},{8,16},{12,4},{16,24},{20,12},{24,32},{28,20},{32,4... | collective-permute-start | bytes 393224 | tf_op jit(solution)/shard_map/ppermute | solution.py:248
  46.3 6.6 %collective-permute-start.1 = (bf16[256,256]{1,0:T(8,128)(2,1)S(1)}, bf16[256,256]{1,0:T(8,128)(2,1)S(1)}, u32[]{:S(2)}, u32[]{:S(2)}) collective-permute-start(bf16[256,256]{1,0:T(8,128)(2,1)S(1)} %get-tuple-element.13), channel_id=1, source_target_pairs={{0,1020},{4,8},{8,4},{12,16},{16,12},{20,24},{24,20},{28,32},{32,2... | collective-permute-start | bytes 393224 | tf_op jit(solution)/shard_map/ppermute | solution.py:247
  77.3 0.7 copy-start.10
  77.9 4.6 %copy-start.11 = (bf16[256,256]{1,0:T(8,128)(2,1)}, bf16[256,256]{1,0:T(8,128)(2,1)S(1)}, u32[]{:S(2)}) copy-start(bf16[256,256]{1,0:T(8,128)(2,1)S(1)} %get-tuple-element.17) | copy-start | bytes 393220
  77.9 21.0 %all-to-all-start.1 = ((bf16[64,8,128]{2,1,0:T(8,128)(2,1)}), bf16[64,8,128]{2,1,0:T(8,128)(2,1)S(1)}, u32[]{:S(2)}, u32[]{:S(2)}) async-start(bf16[64,8,128]{2,1,0:T(8,128)(2,1)} %bitcast.2), calls=%async_computation.1 | async-start | bytes 262144 | tf_op jit(solution)/shard_map/all_to_all | solution.py:268
  82.6 62.6 %collective-permute-start.5 = (bf16[768,256]{1,0:T(8,128)(2,1)S(1)}, bf16[768,256]{1,0:T(8,128)(2,1)S(1)}, u32[]{:S(2)}, u32[]{:S(2)}) collective-permute-start(bf16[768,256]{1,0:T(8,128)(2,1)S(1)} %get-tuple-element.14.mine), channel_id=1, source_target_pairs={{0,3},{1,0},{2,1},{3,2},{4,7},{5,4},{6,5},{7,6},{8,11},{9,8},{10,9... | collective-permute-start | bytes 1179656 | tf_op jit(solution)/shard_map/ppermute | solution.py:218
  86.5 58.7 %collective-permute-start.4 = (bf16[768,256]{1,0:T(8,128)(2,1)S(1)}, bf16[768,256]{1,0:T(8,128)(2,1)S(1)}, u32[]{:S(2)}, u32[]{:S(2)}) collective-permute-start(bf16[768,256]{1,0:T(8,128)(2,1)S(1)} %get-tuple-element.14.mine), channel_id=1, source_target_pairs={{0,2},{1,3},{2,0},{3,1},{4,6},{5,7},{6,4},{7,5},{8,10},{9,11},{10,... | collective-permute-start | bytes 1179656 | tf_op jit(solution)/shard_map/ppermute | solution.py:218
  88.5 56.7 %collective-permute-start.3 = (bf16[768,256]{1,0:T(8,128)(2,1)S(1)}, bf16[768,256]{1,0:T(8,128)(2,1)S(1)}, u32[]{:S(2)}, u32[]{:S(2)}) collective-permute-start(bf16[768,256]{1,0:T(8,128)(2,1)S(1)} %get-tuple-element.14.mine), channel_id=1, source_target_pairs={{0,1},{1,2},{2,3},{3,0},{4,5},{5,6},{6,7},{7,4},{8,9},{9,10},{10,1... | collective-permute-start | bytes 1179656 | tf_op jit(solution)/shard_map/ppermute | solution.py:218
  90.7 23.6 %collective-permute-start.6 = (bf16[256,256]{1,0:T(8,128)(2,1)}, bf16[256,256]{1,0:T(8,128)(2,1)S(1)}, u32[]{:S(2)}, u32[]{:S(2)}) collective-permute-start(bf16[256,256]{1,0:T(8,128)(2,1)} %copy-done.11), channel_id=1, source_target_pairs={{0,1020},{4,8},{8,4},{12,16},{16,12},{20,24},{24,20},{28,32},{32,2... | collective-permute-start | bytes 393224 | tf_op jit(solution)/shard_map/ppermute | solution.py:269
  95.8 18.4 %collective-permute-start.7 = (bf16[256,256]{1,0:T(8,128)(2,1)}, bf16[256,256]{1,0:T(8,128)(2,1)S(1)}, u32[]{:S(2)}, u32[]{:S(2)}) collective-permute-start(bf16[256,256]{1,0:T(8,128)(2,1)} %copy-done.10), channel_id=1, source_target_pairs={{0,1016},{4,12},{8,0},{12,20},{16,8},{20,28},{24,16},{28,36},{32,2... | collective-permute-start | bytes 393224 | tf_op jit(solution)/shard_map/ppermute | solution.py:270
  99.6 37.8 %all-to-all-start.2 = ((f32[16,8,128]{2,1,0:T(8,128)}), f32[16,8,128]{2,1,0:T(8,128)S(1)}, u32[]{:S(2)}, u32[]{:S(2)}) async-start(f32[16,8,128]{2,1,0:T(8,128)} %fold.1), calls=%async_computation.2 | async-start | bytes 131072 | tf_op jit(solution)/shard_map/all_to_all | solution.py:280
  138.4 26.0 %copy-start.1 = (bf16[2,20,128,128]{3,2,1,0:T(8,128)(2,1)S(1)}, bf16[2,20,128,128]{3,2,1,0:T(8,128)(2,1)}, u32[]{:S(2)}) copy-start(bf16[2,20,128,128]{3,2,1,0:T(8,128)(2,1)} %tiles.5) | copy-start | bytes 3932164
  138.4 26.0 %copy-start.7 = (s32[2,20]{1,0:T(2,128)S(1)}, s32[2,20]{1,0:T(2,128)}, u32[]{:S(2)}) copy-start(s32[2,20]{1,0:T(2,128)} %cols.5) | copy-start | bytes 484
  138.4 26.0 %copy-start.9 = (s32[2]{0:T(128)S(1)}, s32[2]{0:T(128)}, u32[]{:S(2)}) copy-start(s32[2]{0:T(128)} %counts.5) | copy-start | bytes 28
  138.4 18.3 %all-to-all-start.3 = ((bf16[64,8,128]{2,1,0:T(8,128)(2,1)}), bf16[64,8,128]{2,1,0:T(8,128)(2,1)S(1)}, u32[]{:S(2)}, u32[]{:S(2)}) async-start(bf16[64,8,128]{2,1,0:T(8,128)(2,1)} %get-tuple-element.19), calls=%async_computation.3 | async-start | bytes 262144 | tf_op jit(solution)/shard_map/all_to_all | solution.py:292
  158.1 6.3 %collective-permute-start.8 = (bf16[2048,256]{1,0:T(8,128)(2,1)S(1)}, bf16[2048,256]{1,0:T(8,128)(2,1)S(1)}, u32[]{:S(2)}, u32[]{:S(2)}) collective-permute-start(bf16[2048,256]{1,0:T(8,128)(2,1)S(1)} %pack.1), channel_id=1, source_target_pairs={{0,4},{4,0},{1,5},{5,1},{2,6},{6,2},{3,7},{7,3},{8,12},{12,8},{9,1... | collective-permute-start | bytes 3145736 | tf_op jit(solution)/shard_map/ppermute | solution.py:303
  168.9 0.9 copy-start.5

commit v3 on v1

--- a/solution.py
+++ b/solution.py
@@ -39,7 +39,7 @@
     return place * per_group + col % per_group
 
 
-def forward_kernel(core_ref, counts, cols, tiles, weight, cotangent, x0, x1, x2, x3, x4, out, local, band, sems):
+def forward_kernel(place_ref, counts, cols, tiles, weight, cotangent, x0, x1, x2, x3, x4, out, local, band, sems):
     sources = (x0, x1, x2, x3, x4)
     rows = x0.shape[0]
     per_group = rows // TILE
@@ -50,7 +50,7 @@
         copies.append(copy)
     for copy in copies:
         copy.wait()
-    core = core_ref[0]
+    core = place_ref[0]
     slots = tiles.shape[1]
     sums = []
     for t in range(tiles.shape[0]):
@@ -71,7 +71,7 @@
     out[...] = jnp.dot(aggregated, weight[...], preferred_element_type=jnp.float32).astype(jnp.bfloat16)
     grad = lax.dot_general(
         aggregated, cotangent[...], (((0,), (0,)), ((), ())), preferred_element_type=jnp.float32
-    ).astype(jnp.bfloat16)
+    )
     height = grad.shape[0]
     local[0:height, :] = grad[:, 0:TILE]
     local[height : 2 * height, :] = grad[:, TILE : 2 * TILE]
@@ -96,22 +96,65 @@
         lax.fori_loop(0, counts[t], step, 0)
 
 
-def send_kernel(core_ref, counts, cols, tiles, cotangent, out, total):
+def send_kernel(place_ref, counts, cols, tiles, cotangent, after, out, total):
     per_group = out.shape[0] // TILE // 2
     total[...] = jnp.zeros_like(total)
-    scatter_tiles(core_ref[0], counts, cols, tiles, cotangent, total, 3 * per_group, 5 * per_group, per_group)
+    scatter_tiles(place_ref[0], counts, cols, tiles, cotangent, total, 3 * per_group, 5 * per_group, per_group)
     out[...] = total[...].astype(jnp.bfloat16)
 
 
-def keep_kernel(core_ref, counts, cols, tiles, cotangent, received, own, near, far, total):
+def keep_kernel(place_ref, counts, cols, tiles, cotangent, received, after, own, near, far, total):
     rows = own.shape[0]
     per_group = rows // TILE
     total[0 : 2 * rows, :] = received[...].astype(jnp.float32)
     total[2 * rows : 3 * rows, :] = jnp.zeros_like(total[2 * rows : 3 * rows, :])
-    scatter_tiles(core_ref[0], counts, cols, tiles, cotangent, total, 0, 3 * per_group, per_group)
+    scatter_tiles(place_ref[0], counts, cols, tiles, cotangent, total, 0, 3 * per_group, per_group)
     own[...] = total[0:rows, :]
     near[...] = total[rows : 2 * rows, :].astype(jnp.bfloat16)
     far[...] = total[2 * rows : 3 * rows, :].astype(jnp.bfloat16)
+
+
+def fold_kernel(parts, out):
+    part = jnp.sum(parts[...].astype(jnp.float32), 0)
+    for i in range(out.shape[0]):
+        out[i] = part
+
+
+def spread_kernel(scale, folded, spread):
+    part = (jnp.sum(folded[...], 0) * scale).astype(jnp.bfloat16)
+    for i in range(spread.shape[0]):
+        spread[i] = part
+
+
+def meet_kernel(place_ref, own, near, far, mine, turn1, turn2, turn3):
+    rows = mine.shape[0]
+    turns = (turn1, turn2, turn3)
+    members = len(turns) + 1
+    for turn in range(members):
+        member = place_ref[1] + turn
+        member = jnp.where(member >= members, member - members, member)
+        part = pl.ds(pl.multiple_of(member * rows, rows), rows)
+        total = own[part, :] + near[part, :].astype(jnp.float32) + far[part, :].astype(jnp.float32)
+        if turn == 0:
+            mine[...] = total
+        else:
+            turns[turn - 1][...] = total.astype(jnp.bfloat16)
+
+
+def last_kernel(mine, turn1, turn2, turn3, weight, parts, feat, grad):
+    total = mine[...]
+    for turn in (turn1, turn2, turn3):
+        total = total + turn[...].astype(jnp.float32)
+    feat[...] = lax.dot_general(
+        total.astype(jnp.bfloat16), weight[...], (((1,), (1,)), ((), ())), preferred_element_type=jnp.float32
+    )
+    count, depth, _ = parts.shape
+    height = grad.shape[0]
+    half = height // depth
+    for side in range(count // half):
+        grad[:, side * TILE : (side + 1) * TILE] = (
+            parts[side * half : (side + 1) * half].astype(jnp.float32).reshape(height, TILE)
+        )
 
 
 def params():
@@ -124,7 +167,7 @@
     groups = math.prod(lax.axis_size(axis) for axis in DOM)
     members = lax.axis_size("zl")
     group_rows = rows * members
-    core = lax.axis_index("c").astype(jnp.int32).reshape(1)
+    core = jnp.stack([lax.axis_index("c"), lax.axis_index("zl")]).astype(jnp.int32)
     near = near_pairs(groups)
     swap = [(0, 1), (1, 0)]
     smem = pl.BlockSpec(memory_space=pltpu.SMEM)
@@ -141,14 +184,32 @@
     sent = pl.pallas_call(
         send_kernel,
         out_shape=jax.ShapeDtypeStruct((2 * group_rows, width), jnp.bfloat16),
-        in_specs=[smem, smem, smem, vmem, vmem],
+        in_specs=[smem, smem, smem, vmem, vmem, anywhere],
         out_specs=vmem,
         scratch_shapes=[pltpu.VMEM((2 * group_rows, width), jnp.float32)],
         compiler_params=params(),
         cost_estimate=pl.CostEstimate(flops=flops, bytes_accessed=4 << 20, transcendentals=0),
         name="send",
-    )(core, tile_counts, tile_cols, tile_values, cotangent)
+    )(core, tile_counts, tile_cols, tile_values, cotangent, x0)
     received = lax.ppermute(sent, "c", swap)
+
+    layer_out, local = pl.pallas_call(
+        forward_kernel,
+        out_shape=(
+            jax.ShapeDtypeStruct((rows, width), jnp.bfloat16),
+            jax.ShapeDtypeStruct((2 * width, TILE), jnp.float32),
+        ),
+        in_specs=[smem, smem, smem, vmem, vmem, vmem] + [anywhere] * 5,
+        out_specs=(vmem, vmem),
+        scratch_shapes=[
+            pltpu.VMEM((5 * group_rows, width), jnp.bfloat16),
+            pltpu.SemaphoreType.DMA((5,)),
+        ],
+        compiler_params=params(),
+        cost_estimate=pl.CostEstimate(flops=flops, bytes_accessed=6 << 20, transcendentals=0),
+        name="forward",
+    )(core, tile_counts, tile_cols, tile_values, weight, cotangent, x0, x1, x2, x3, x4)
+
     own, near_sum, far_sum = pl.pallas_call(
         keep_kernel,
         out_shape=(
@@ -156,47 +217,62 @@
             jax.ShapeDtypeStruct((group_rows, width), jnp.bfloat16),
             jax.ShapeDtypeStruct((group_rows, width), jnp.bfloat16),
         ),
-        in_specs=[smem, smem, smem, vmem, vmem, vmem],
+        in_specs=[smem, smem, smem, vmem, vmem, vmem, anywhere],
         out_specs=(vmem, vmem, vmem),
         scratch_shapes=[pltpu.VMEM((3 * group_rows, width), jnp.float32)],
         compiler_params=params(),
         cost_estimate=pl.CostEstimate(flops=flops, bytes_accessed=8 << 20, transcendentals=0),
         name="keep",
-    )(core, tile_counts, tile_cols, tile_values, cotangent, received)
+    )(core, tile_counts, tile_cols, tile_values, cotangent, received, local)
     near_in = lax.ppermute(near_sum, DOM, near)
     far_in = lax.ppermute(far_sum, DOM, far_pairs(groups, True))
-
-    layer_out, local = pl.pallas_call(
-        forward_kernel,
-        out_shape=(
-            jax.ShapeDtypeStruct((rows, width), jnp.bfloat16),
-            jax.ShapeDtypeStruct((2 * width, TILE), jnp.bfloat16),
-        ),
-        in_specs=[smem, smem, smem, vmem, vmem, vmem] + [anywhere] * 5,
-        out_specs=(vmem, vmem),
-        scratch_shapes=[
-            pltpu.VMEM((5 * group_rows, width), jnp.bfloat16),
-            pltpu.SemaphoreType.DMA((5,)),
-        ],
-        compiler_params=params(),
-        cost_estimate=pl.CostEstimate(flops=flops, bytes_accessed=6 << 20, transcendentals=0),
-        name="forward",
-    )(core, tile_counts, tile_cols, tile_values, weight, cotangent, x0, x1, x2, x3, x4)
 
     plane = math.prod(lax.axis_size(axis) for axis in PLANE)
     column = math.prod(lax.axis_size(axis) for axis in COLUMN)
     parts = lax.all_to_all(local.reshape(plane, -1, TILE), PLANE, 0, 0)
-    part = jnp.sum(parts.astype(jnp.float32), 0)
-    parts = lax.all_to_all(jnp.broadcast_to(part[None], (column,) + part.shape), COLUMN, 0, 0)
-    part = jnp.sum(parts, 0) / math.sqrt(rows * groups * members)
-    part = part.astype(jnp.bfloat16)
-    parts = lax.all_to_all(jnp.broadcast_to(part[None], (plane,) + part.shape), PLANE, 0, 0)
-    parts = parts.reshape(2, width, TILE).astype(jnp.float32)
-    weight_grad = jnp.concatenate([parts[0], parts[1]], 1)
-
-    total = (own + near_in.astype(jnp.float32) + far_in.astype(jnp.float32)).astype(jnp.bfloat16)
-    mine = lax.psum_scatter(total, "zl", scatter_dimension=0, tiled=True)
-    feat_grad = lax.dot_general(mine, weight, (((1,), (1,)), ((), ())), preferred_element_type=jnp.float32)
+    part = pl.pallas_call(
+        fold_kernel,
+        out_shape=jax.ShapeDtypeStruct((column,) + parts.shape[1:], jnp.float32),
+        in_specs=[vmem],
+        out_specs=vmem,
+        compiler_params=params(),
+        cost_estimate=pl.CostEstimate(flops=0, bytes_accessed=1 << 20, transcendentals=0),
+        name="fold",
+    )(parts)
+    folded = lax.all_to_all(part, COLUMN, 0, 0)
+    mine, *turns = pl.pallas_call(
+        meet_kernel,
+        out_shape=(jax.ShapeDtypeStruct((rows, width), jnp.float32),)
+        + (jax.ShapeDtypeStruct((rows, width), jnp.bfloat16),) * (members - 1),
+        in_specs=[smem] + [vmem] * 3,
+        out_specs=(vmem,) * members,
+        compiler_params=params(),
+        name="meet",
+    )(core, own, near_in, far_in)
+    turns = [
+        lax.ppermute(value, "zl", [(m, (m + turn + 1) % members) for m in range(members)])
+        for turn, value in enumerate(turns)
+    ]
+    spread = pl.pallas_call(
+        functools.partial(spread_kernel, 1 / math.sqrt(rows * groups * members)),
+        out_shape=jax.ShapeDtypeStruct(parts.shape, jnp.bfloat16),
+        in_specs=[vmem],
+        out_specs=vmem,
+        compiler_params=params(),
+        name="spread",
+    )(folded)
+    parts = lax.all_to_all(spread, PLANE, 0, 0)
+    feat_grad, weight_grad = pl.pallas_call(
+        last_kernel,
+        out_shape=(
+            jax.ShapeDtypeStruct((rows, width), jnp.float32),
+            jax.ShapeDtypeStruct(weight.shape, jnp.float32),
+        ),
+        in_specs=[vmem] * (members + 2),
+        out_specs=(vmem, vmem),
+        compiler_params=params(),
+        name="last",
+    )(mine, *turns, weight, parts)
     return (layer_out, feat_grad, weight_grad)
 
 

time: 165 us -> 153 us (0.927)
  starting transfers between devices: 57.8 us -> 76.6 us
  between operations: 14.2 us -> 0.85 us
  waiting for transfers between devices: 15.9 us -> 6.57 us
  blocking collectives: 59.5 us -> 53.6 us
  local copies, waits for them, and re-layouts: 3.61 us -> 5.79 us
  matrix products: 1.83 us -> 0 us
  other arithmetic: 1.79 us -> 0.08 us
    ppermute x1, waiting for transfers between devices: 15.9 us -> 0.01 us  [per_device(): far_in = lax.ppermute(far_sum, DOM, far_pairs(groups, True))]
    all_to_all x2 -> x1, blocking collectives: 45.8 us -> 35 us  [per_device(): folded = lax.all_to_all(part, COLUMN, 0, 0)]
    ppermute x1, starting transfers between devices: 13.9 us -> 3.53 us  [per_device(): x2 = lax.ppermute(x0, DOM, far_pairs(groups, False))]
    ppermute x0 -> x3, starting transfers between devices: none -> 10.1 us  [per_device(): lax.ppermute(value, 'zl', [(m, (m + turn + 1) % members) for m in range(m...]
    all_to_all x1, starting transfers between devices: 6.35 us -> 16.3 us  [per_device(): parts = lax.all_to_all(local.reshape(plane, -1, TILE), PLANE, 0, 0)]
    ppermute x1, starting transfers between devices: 12.1 us -> 2.41 us  [per_device(): x4 = lax.ppermute(x1, 'c', swap)]
    ppermute x1, starting transfers between devices: 3.71 us -> 9.67 us  [per_device(): near_in = lax.ppermute(near_sum, DOM, near)]
    ppermute x1, starting transfers between devices: 2.04 us -> 7.33 us  [per_device(): x1 = lax.ppermute(x0, DOM, near)]
  transfers between devices with their start and end apart: 9 -> 12, of which waited for: 1 -> 2; matrix products, arithmetic and copies ran while one was open for 1% -> 0% of each run, Pallas kernels for 4% -> 4%
where the time goes in v3:
time: 153 us; the launch traced here: 152 us
  starting transfers between devices  76.6 us (50%)
  blocking collectives  53.6 us (35%)
  Pallas kernels  8.84 us (6%)
  waiting for transfers between devices  6.57 us (4%)
  local copies, waits for them, and re-layouts  5.79 us (4%)
    all_to_all x1, blocking collectives, per_device(): folded = lax.all_to_all(part, COLUMN, 0, 0)  35 us
    all_gather x1, blocking collectives, per_device(): x0 = lax.all_gather(features, 'zl', axis=0, tiled=True)  18.6 us
    ppermute x1, starting transfers between devices, per_device(): received = lax.ppermute(sent, 'c', swap)  17.1 us
    all_to_all x1, starting transfers between devices, per_device(): parts = lax.all_to_all(local.reshape(plane, -1, TILE), PLANE, 0, 0)  16.3 us
    ppermute x3, starting transfers between devices, per_device(): lax.ppermute(value, 'zl', [(m, (m + turn + 1) % members) for m in range(m...  10.1 us
    ppermute x1, starting transfers between devices, per_device(): near_in = lax.ppermute(near_sum, DOM, near)  9.67 us
    ppermute x1, starting transfers between devices, per_device(): x1 = lax.ppermute(x0, DOM, near)  7.33 us
    unnamed x24, local copies, waits for them, and re-layouts  5.79 us
  transfers between devices with their start and end apart: 12, of which 2 were waited for; matrix products, arithmetic and copies ran while one was open for 0% of the time, Pallas kernels for 4%

profile of v3, /device:TPU:1, one launch (start us, length us, event | category | flops | bytes accessed | tf_op | source)
XLA Modules:
  0.0 152.4 jit_solution(11505237063116707683)
XLA Ops:
  0.6 18.6 %all_gather.3.x0.after = bf16[1024,256]{1,0:T(8,128)(2,1)S(1)} all-gather(bf16[256,256]{1,0:T(8,128)(2,1)} %param.6), channel_id=1, replica_groups=mesh['zh'=2,'x'=8,'y'=8,'c'=2,'zl'=4] {'zl'}, dimensions={0}, use_global_device_ids=true | all-gather | bytes 655360 | tf_op jit(solution)/shard_map/all_gather | solution.py:178
  19.2 7.3 %collective-permute-start = (bf16[1024,256]{1,0:T(8,128)(2,1)S(1)}, bf16[1024,256]{1,0:T(8,128)(2,1)S(1)}, u32[]{:S(2)}, u32[]{:S(2)}) collective-permute-start(bf16[1024,256]{1,0:T(8,128)(2,1)S(1)} %all_gather.3.x0.after), channel_id=1, source_target_pairs={{0,1020},{4,8},{8,4},{12,16},{16,12},{20,24},{24,20},{28,32},{32,2... | collective-permute-start | bytes 1572872 | tf_op jit(solution)/shard_map/ppermute | solution.py:179
  26.6 0.1 pad_add_fusion.place_ref
  26.7 1.3 copy-done
  28.0 0.9 copy-done.2
  28.9 0.7 copy-done.8
  29.6 0.7 copy-done.10
  30.2 2.0 %send.1 = bf16[2048,256]{1,0:T(8,128)(2,1)} custom-call(s32[2]{0:T(128)S(1)} %pad_add_fusion.place_ref, s32[2]{0:T(128)S(1)} %copy-done.10, s32[2,20]{1,0:T(2,128)S(1)} %copy-done.8, bf16[2,20,128,128]{3,2,1,0:T(8,128)(2,1)S(1)} %copy-done, bf16[256,256]{1,0:T(8,128)(2,1)S(1)} %copy-done.2, bf16[1024,256]{1,0:T(8,128)(2,1)S(1)} %all_gather.3.x0.after), custom_call_target="tpu_custom_call" | custom-call | flops 335544320 | bytes 4194304 | tf_op jit(solution)/shard_map/send/pallas_call | solution.py:184
  32.3 17.1 %collective-permute-start.4 = (bf16[2048,256]{1,0:T(8,128)(2,1)}, bf16[2048,256]{1,0:T(8,128)(2,1)S(1)}, u32[]{:S(2)}, u32[]{:S(2)}) collective-permute-start(bf16[2048,256]{1,0:T(8,128)(2,1)} %send.1), channel_id=1, source_target_pairs={{0,4},{4,0},{1,5},{5,1},{2,6},{6,2},{3,7},{7,3},{8,12},{12,8},{9,1... | collective-permute-start | bytes 3145736 | tf_op jit(solution)/shard_map/ppermute | solution.py:194
  49.4 3.5 %collective-permute-start.1 = (bf16[1024,256]{1,0:T(8,128)(2,1)S(1)}, bf16[1024,256]{1,0:T(8,128)(2,1)S(1)}, u32[]{:S(2)}, u32[]{:S(2)}) collective-permute-start(bf16[1024,256]{1,0:T(8,128)(2,1)S(1)} %all_gather.3.x0.after), channel_id=1, source_target_pairs={{0,8},{4,1020},{8,16},{12,4},{16,24},{20,12},{24,32},{28,20},{32,4... | collective-permute-start | bytes 1572872 | tf_op jit(solution)/shard_map/ppermute | solution.py:180
  52.9 1.9 %collective-permute-start.2 = (bf16[1024,256]{1,0:T(8,128)(2,1)S(1)}, bf16[1024,256]{1,0:T(8,128)(2,1)S(1)}, u32[]{:S(2)}, u32[]{:S(2)}) collective-permute-start(bf16[1024,256]{1,0:T(8,128)(2,1)S(1)} %all_gather.3.x0.after), channel_id=1, source_target_pairs={{0,4},{4,0},{1,5},{5,1},{2,6},{6,2},{3,7},{7,3},{8,12},{12,8},{9,1... | collective-permute-start | bytes 1572872 | tf_op jit(solution)/shard_map/ppermute | solution.py:181
  54.9 0.0 collective-permute-done.x1
  54.9 2.4 %collective-permute-start.3 = (bf16[1024,256]{1,0:T(8,128)(2,1)S(1)}, bf16[1024,256]{1,0:T(8,128)(2,1)S(1)}, u32[]{:S(2)}, u32[]{:S(2)}) collective-permute-start(bf16[1024,256]{1,0:T(8,128)(2,1)S(1)} %collective-permute-done.x1), channel_id=1, source_target_pairs={{0,4},{4,0},{1,5},{5,1},{2,6},{6,2},{3,7},{7,3},{8,12},{12,8},{9,1... | collective-permute-start | bytes 1572872 | tf_op jit(solution)/shard_map/ppermute | solution.py:182
  57.3 2.0 %collective-permute-done.1.x2 = bf16[1024,256]{1,0:T(8,128)(2,1)S(1)} collective-permute-done((bf16[1024,256]{1,0:T(8,128)(2,1)S(1)}, bf16[1024,256]{1,0:T(8,128)(2,1)S(1)}, u32[]{:S(2)}, u32[]{:S(2)}) %collective-permute-start.1) | collective-permute-done | bytes 524320 | tf_op jit(solution)/shard_map/ppermute | solution.py:180
  59.4 0.0 copy-start.1
  59.4 2.3 %forward.1 = (bf16[256,256]{1,0:T(8,128)(2,1)}, f32[512,128]{1,0:T(8,128)}) custom-call(s32[2]{0:T(128)S(1)} %pad_add_fusion.place_ref, s32[2]{0:T(128)S(1)} %copy-done.11, s32[2,20]{1,0:T(2,128)S(1)} %copy-done.8, bf16[2,20,128,128]{3,2,1,0:T(8,128)(2,1)S(1)} %copy-done, bf16[256,256]{1,0:T(8,128)(2,1)S(1)} %copy-done.6, bf16[256,256]{1,0:T(8,128)(2,1)S(1)} %copy-done.3, ...), custom_call_target="tpu_custom_call" | custom-call | flops 335544320 | bytes 6291456 | tf_op jit(solution)/shard_map/forward/pallas_call | solution.py:196
  61.7 16.3 %all-to-all-start = ((f32[64,8,128]{2,1,0:T(8,128)}), f32[64,8,128]{2,1,0:T(8,128)S(1)}, u32[]{:S(2)}, u32[]{:S(2)}) async-start(f32[64,8,128]{2,1,0:T(8,128)} %bitcast.2), calls=%async_computation | async-start | bytes 524288 | tf_op jit(solution)/shard_map/all_to_all | solution.py:232
  78.0 1.0 copy-done.4
  79.0 1.2 copy-done.5
  80.2 2.1 %keep.1 = (f32[1024,256]{1,0:T(8,128)S(1)}, bf16[1024,256]{1,0:T(8,128)(2,1)}, bf16[1024,256]{1,0:T(8,128)(2,1)S(1)}) custom-call(s32[2]{0:T(128)S(1)} %pad_add_fusion.place_ref, s32[2]{0:T(128)S(1)} %copy-done.11, s32[2,20]{1,0:T(2,128)S(1)} %copy-done.9, bf16[2,20,128,128]{3,2,1,0:T(8,128)(2,1)S(1)} %copy-done.1, bf16[256,256]{1,0:T(8,128)(2,1)S(1)} %copy-done.3, ...), custom_call_target="tpu_custom_call" | custom-call | flops 335544320 | bytes 8388608 | tf_op jit(solution)/shard_map/keep/pallas_call | solution.py:213
  82.3 9.7 %collective-permute-start.5 = (bf16[1024,256]{1,0:T(8,128)(2,1)}, bf16[1024,256]{1,0:T(8,128)(2,1)S(1)}, u32[]{:S(2)}, u32[]{:S(2)}) collective-permute-start(bf16[1024,256]{1,0:T(8,128)(2,1)} %get-tuple-element.17), channel_id=1, source_target_pairs={{0,1020},{4,8},{8,4},{12,16},{16,12},{20,24},{24,20},{28,32},{32,2... | collective-permute-start | bytes 1572872 | tf_op jit(solution)/shard_map/ppermute | solution.py:227
  92.0 3.6 %collective-permute-start.6 = (bf16[1024,256]{1,0:T(8,128)(2,1)S(1)}, bf16[1024,256]{1,0:T(8,128)(2,1)S(1)}, u32[]{:S(2)}, u32[]{:S(2)}) collective-permute-start(bf16[1024,256]{1,0:T(8,128)(2,1)S(1)} %get-tuple-element.18), channel_id=1, source_target_pairs={{0,1016},{4,12},{8,0},{12,20},{16,8},{20,28},{24,16},{28,36},{32,2... | collective-permute-start | bytes 1572872 | tf_op jit(solution)/shard_map/ppermute | solution.py:228
  95.7 0.1 fold.1
  95.7 35.0 %all_to_all.15.folded = f32[16,8,128]{2,1,0:T(8,128)S(1)} all-to-all(f32[16,8,128]{2,1,0:T(8,128)S(1)} %fold.1), channel_id=1, replica_groups=mesh['zh'=2,'x'=8,'y'=8,'c'=2,'zl'=4] {'zh','zl','c'}, dimensions={0} | all-to-all | bytes 131072 | tf_op jit(solution)/shard_map/all_to_all | solution.py:242
  130.8 0.7 spread.1
  131.4 4.6 %all-to-all-start.2 = ((bf16[64,8,128]{2,1,0:T(8,128)(2,1)}), bf16[64,8,128]{2,1,0:T(8,128)(2,1)S(1)}, u32[]{:S(2)}, u32[]{:S(2)}) async-start(bf16[64,8,128]{2,1,0:T(8,128)(2,1)} %spread.1), calls=%async_computation.2 | async-start | bytes 262144 | tf_op jit(solution)/shard_map/all_to_all | solution.py:264
  136.1 0.7 meet.1
  136.8 2.9 %collective-permute-start.7 = (bf16[256,256]{1,0:T(8,128)(2,1)S(1)}, bf16[256,256]{1,0:T(8,128)(2,1)S(1)}, u32[]{:S(2)}, u32[]{:S(2)}) collective-permute-start(bf16[256,256]{1,0:T(8,128)(2,1)S(1)} %get-tuple-element.20), channel_id=1, source_target_pairs={{0,1},{1,2},{2,3},{3,0},{4,5},{5,6},{6,7},{7,4},{8,9},{9,10},{10,1... | collective-permute-start | bytes 393224 | tf_op jit(solution)/shard_map/ppermute | solution.py:253
  139.7 3.0 %collective-permute-start.8 = (bf16[256,256]{1,0:T(8,128)(2,1)S(1)}, bf16[256,256]{1,0:T(8,128)(2,1)S(1)}, u32[]{:S(2)}, u32[]{:S(2)}) collective-permute-start(bf16[256,256]{1,0:T(8,128)(2,1)S(1)} %get-tuple-element.21), channel_id=1, source_target_pairs={{0,2},{1,3},{2,0},{3,1},{4,6},{5,7},{6,4},{7,5},{8,10},{9,11},{10,... | collective-permute-start | bytes 393224 | tf_op jit(solution)/shard_map/ppermute | solution.py:253
  142.6 4.3 %collective-permute-start.9 = (bf16[256,256]{1,0:T(8,128)(2,1)S(1)}, bf16[256,256]{1,0:T(8,128)(2,1)S(1)}, u32[]{:S(2)}, u32[]{:S(2)}) collective-permute-start(bf16[256,256]{1,0:T(8,128)(2,1)S(1)} %get-tuple-element.22), channel_id=1, source_target_pairs={{0,3},{1,0},{2,1},{3,2},{4,7},{5,4},{6,5},{7,6},{8,11},{9,8},{10,9... | collective-permute-start | bytes 393224 | tf_op jit(solution)/shard_map/ppermute | solution.py:253
  146.9 4.5 %collective-permute-done.8.turn2 = bf16[256,256]{1,0:T(8,128)(2,1)S(1)} collective-permute-done((bf16[256,256]{1,0:T(8,128)(2,1)S(1)}, bf16[256,256]{1,0:T(8,128)(2,1)S(1)}, u32[]{:S(2)}, u32[]{:S(2)}) %collective-permute-start.8) | collective-permute-done | bytes 131104 | tf_op jit(solution)/shard_map/ppermute | solution.py:253
  151.4 0.9 last.1
  (26 shorter events, 0.1 us)
Async XLA Ops:
  19.2 35.6 %collective-permute-start = (bf16[1024,256]{1,0:T(8,128)(2,1)S(1)}, bf16[1024,256]{1,0:T(8,128)(2,1)S(1)}, u32[]{:S(2)}, u32[]{:S(2)}) collective-permute-start(bf16[1024,256]{1,0:T(8,128)(2,1)S(1)} %all_gather.3.x0.after), channel_id=1, source_target_pairs={{0,1020},{4,8},{8,4},{12,16},{16,12},{20,24},{24,20},{28,32},{32,2... | collective-permute-start | bytes 1572872 | tf_op jit(solution)/shard_map/ppermute | solution.py:179
  26.7 1.3 copy-start
  28.0 0.9 copy-start.2
  28.9 0.7 copy-start.8
  29.6 0.7 copy-start.10
  30.2 29.1 %copy-start.3 = (bf16[256,256]{1,0:T(8,128)(2,1)S(1)}, bf16[256,256]{1,0:T(8,128)(2,1)}, u32[]{:S(2)}) copy-start(bf16[256,256]{1,0:T(8,128)(2,1)} %cotangent.5) | copy-start | bytes 393220
  30.2 29.1 %copy-start.6 = (bf16[256,256]{1,0:T(8,128)(2,1)S(1)}, bf16[256,256]{1,0:T(8,128)(2,1)}, u32[]{:S(2)}) copy-start(bf16[256,256]{1,0:T(8,128)(2,1)} %weight.3) | copy-start | bytes 393220
  30.2 29.1 %copy-start.11 = (s32[2]{0:T(128)S(1)}, s32[2]{0:T(128)}, u32[]{:S(2)}) copy-start(s32[2]{0:T(128)} %counts.5) | copy-start | bytes 28
  32.3 46.7 %copy-start.9 = (s32[2,20]{1,0:T(2,128)S(1)}, s32[2,20]{1,0:T(2,128)}, u32[]{:S(2)}) copy-start(s32[2,20]{1,0:T(2,128)} %cols.5) | copy-start | bytes 484
  32.3 45.7 %collective-permute-start.4 = (bf16[2048,256]{1,0:T(8,128)(2,1)}, bf16[2048,256]{1,0:T(8,128)(2,1)S(1)}, u32[]{:S(2)}, u32[]{:S(2)}) collective-permute-start(bf16[2048,256]{1,0:T(8,128)(2,1)} %send.1), channel_id=1, source_target_pairs={{0,4},{4,0},{1,5},{5,1},{2,6},{6,2},{3,7},{7,3},{8,12},{12,8},{9,1... | collective-permute-start | bytes 3145736 | tf_op jit(solution)/shard_map/ppermute | solution.py:194
  49.4 9.9 %collective-permute-start.1 = (bf16[1024,256]{1,0:T(8,128)(2,1)S(1)}, bf16[1024,256]{1,0:T(8,128)(2,1)S(1)}, u32[]{:S(2)}, u32[]{:S(2)}) collective-permute-start(bf16[1024,256]{1,0:T(8,128)(2,1)S(1)} %all_gather.3.x0.after), channel_id=1, source_target_pairs={{0,8},{4,1020},{8,16},{12,4},{16,24},{20,12},{24,32},{28,20},{32,4... | collective-permute-start | bytes 1572872 | tf_op jit(solution)/shard_map/ppermute | solution.py:180
  52.9 6.4 %collective-permute-start.2 = (bf16[1024,256]{1,0:T(8,128)(2,1)S(1)}, bf16[1024,256]{1,0:T(8,128)(2,1)S(1)}, u32[]{:S(2)}, u32[]{:S(2)}) collective-permute-start(bf16[1024,256]{1,0:T(8,128)(2,1)S(1)} %all_gather.3.x0.after), channel_id=1, source_target_pairs={{0,4},{4,0},{1,5},{5,1},{2,6},{6,2},{3,7},{7,3},{8,12},{12,8},{9,1... | collective-permute-start | bytes 1572872 | tf_op jit(solution)/shard_map/ppermute | solution.py:181
  54.9 4.5 %collective-permute-start.3 = (bf16[1024,256]{1,0:T(8,128)(2,1)S(1)}, bf16[1024,256]{1,0:T(8,128)(2,1)S(1)}, u32[]{:S(2)}, u32[]{:S(2)}) collective-permute-start(bf16[1024,256]{1,0:T(8,128)(2,1)S(1)} %collective-permute-done.x1), channel_id=1, source_target_pairs={{0,4},{4,0},{1,5},{5,1},{2,6},{6,2},{3,7},{7,3},{8,12},{12,8},{9,1... | collective-permute-start | bytes 1572872 | tf_op jit(solution)/shard_map/ppermute | solution.py:182
  59.4 19.6 %copy-start.1 = (bf16[2,20,128,128]{3,2,1,0:T(8,128)(2,1)S(1)}, bf16[2,20,128,128]{3,2,1,0:T(8,128)(2,1)}, u32[]{:S(2)}) copy-start(bf16[2,20,128,128]{3,2,1,0:T(8,128)(2,1)} %tiles.5) | copy-start | bytes 3932164
  61.7 34.0 %all-to-all-start = ((f32[64,8,128]{2,1,0:T(8,128)}), f32[64,8,128]{2,1,0:T(8,128)S(1)}, u32[]{:S(2)}, u32[]{:S(2)}) async-start(f32[64,8,128]{2,1,0:T(8,128)} %bitcast.2), calls=%async_computation | async-start | bytes 524288 | tf_op jit(solution)/shard_map/all_to_all | solution.py:232
  78.0 1.0 copy-start.4
  79.0 1.2 copy-start.5
  82.3 53.7 %collective-permute-start.5 = (bf16[1024,256]{1,0:T(8,128)(2,1)}, bf16[1024,256]{1,0:T(8,128)(2,1)S(1)}, u32[]{:S(2)}, u32[]{:S(2)}) collective-permute-start(bf16[1024,256]{1,0:T(8,128)(2,1)} %get-tuple-element.17), channel_id=1, source_target_pairs={{0,1020},{4,8},{8,4},{12,16},{16,12},{20,24},{24,20},{28,32},{32,2... | collective-permute-start | bytes 1572872 | tf_op jit(solution)/shard_map/ppermute | solution.py:227
  92.0 44.1 %collective-permute-start.6 = (bf16[1024,256]{1,0:T(8,128)(2,1)S(1)}, bf16[1024,256]{1,0:T(8,128)(2,1)S(1)}, u32[]{:S(2)}, u32[]{:S(2)}) collective-permute-start(bf16[1024,256]{1,0:T(8,128)(2,1)S(1)} %get-tuple-element.18), channel_id=1, source_target_pairs={{0,1016},{4,12},{8,0},{12,20},{16,8},{20,28},{24,16},{28,36},{32,2... | collective-permute-start | bytes 1572872 | tf_op jit(solution)/shard_map/ppermute | solution.py:228
  130.8 20.7 %copy-start.7 = (bf16[256,256]{1,0:T(8,128)(2,1)S(1)}, bf16[256,256]{1,0:T(8,128)(2,1)}, u32[]{:S(2)}) copy-start(bf16[256,256]{1,0:T(8,128)(2,1)} %weight.3) | copy-start | bytes 393220
  131.4 20.0 %all-to-all-start.2 = ((bf16[64,8,128]{2,1,0:T(8,128)(2,1)}), bf16[64,8,128]{2,1,0:T(8,128)(2,1)S(1)}, u32[]{:S(2)}, u32[]{:S(2)}) async-start(bf16[64,8,128]{2,1,0:T(8,128)(2,1)} %spread.1), calls=%async_computation.2 | async-start | bytes 262144 | tf_op jit(solution)/shard_map/all_to_all | solution.py:264
  136.8 10.1 %collective-permute-start.7 = (bf16[256,256]{1,0:T(8,128)(2,1)S(1)}, bf16[256,256]{1,0:T(8,128)(2,1)S(1)}, u32[]{:S(2)}, u32[]{:S(2)}) collective-permute-start(bf16[256,256]{1,0:T(8,128)(2,1)S(1)} %get-tuple-element.20), channel_id=1, source_target_pairs={{0,1},{1,2},{2,3},{3,0},{4,5},{5,6},{6,7},{7,4},{8,9},{9,10},{10,1... | collective-permute-start | bytes 393224 | tf_op jit(solution)/shard_map/ppermute | solution.py:253
  139.7 11.7 %collective-permute-start.8 = (bf16[256,256]{1,0:T(8,128)(2,1)S(1)}, bf16[256,256]{1,0:T(8,128)(2,1)S(1)}, u32[]{:S(2)}, u32[]{:S(2)}) collective-permute-start(bf16[256,256]{1,0:T(8,128)(2,1)S(1)} %get-tuple-element.21), channel_id=1, source_target_pairs={{0,2},{1,3},{2,0},{3,1},{4,6},{5,7},{6,4},{7,5},{8,10},{9,11},{10,... | collective-permute-start | bytes 393224 | tf_op jit(solution)/shard_map/ppermute | solution.py:253
  142.6 8.8 %collective-permute-start.9 = (bf16[256,256]{1,0:T(8,128)(2,1)S(1)}, bf16[256,256]{1,0:T(8,128)(2,1)S(1)}, u32[]{:S(2)}, u32[]{:S(2)}) collective-permute-start(bf16[256,256]{1,0:T(8,128)(2,1)S(1)} %get-tuple-element.22), channel_id=1, source_target_pairs={{0,3},{1,0},{2,1},{3,2},{4,7},{5,4},{6,5},{7,6},{8,11},{9,8},{10,9... | collective-permute-start | bytes 393224 | tf_op jit(solution)/shard_map/ppermute | solution.py:253

commit v4 on v3

--- a/solution.py
+++ b/solution.py
@@ -32,6 +32,18 @@
     return pairs
 
 
+def split_pairs(pairs):
+    part = len(pairs) // 2
+    inside = [(a, b) for a, b in pairs if a // part == b // part]
+    across = [(a, b) for a, b in pairs if a // part != b // part]
+    return inside, across
+
+
+def edge_devices(groups):
+    part = groups // 2
+    return [d for d in range(groups) if d % part in (0, part - 1)]
+
+
 def tile_of(col, core, per_group):
     band = col // per_group
     band = jnp.where(core == 0, 4 - band, band)
@@ -39,18 +51,27 @@
     return place * per_group + col % per_group
 
 
-def forward_kernel(place_ref, counts, cols, tiles, weight, cotangent, x0, x1, x2, x3, x4, out, local, band, sems):
-    sources = (x0, x1, x2, x3, x4)
+def turned_tile_of(col, core, member, members, per_group):
+    tile = tile_of(col, core, per_group)
+    share = per_group // members
+    within = tile % per_group
+    turn = (member - within // share + members) % members
+    return tile - within + turn * share + within % share
+
+
+def forward_kernel(
+    members, place_ref, counts, cols, tiles, weight, cotangent, x0, x1, x2, x3, x4, out, local, band, sems
+):
     rows = x0.shape[0]
     per_group = rows // TILE
     copies = []
-    for index, source in enumerate(sources):
+    for index, source in enumerate((x0, x1, x2, x3, x4)):
         copy = pltpu.make_async_copy(source, band.at[pl.ds(index * rows, rows)], sems.at[index])
         copy.start()
         copies.append(copy)
     for copy in copies:
         copy.wait()
-    core = place_ref[0]
+    core, member = place_ref[0], place_ref[1]
     slots = tiles.shape[1]
     sums = []
     for t in range(tiles.shape[0]):
@@ -59,7 +80,8 @@
         for s in range(0, slots, 2):
             left, right = [], []
             for one in (s, s + 1):
-                start = pl.multiple_of(tile_of(cols[t, one], core, per_group) * TILE, TILE)
+                tile = turned_tile_of(cols[t, one], core, member, members, per_group)
+                start = pl.multiple_of(tile * TILE, TILE)
                 value = tiles[t, one]
                 left.append(jnp.where(one < count, value, jnp.zeros_like(value)))
                 right.append(band[pl.ds(start, TILE), :])
@@ -103,7 +125,9 @@
     out[...] = total[...].astype(jnp.bfloat16)
 
 
-def keep_kernel(place_ref, counts, cols, tiles, cotangent, received, after, own, near, far, total):
+def keep_kernel(
+    place_ref, counts, cols, tiles, cotangent, received, after, own, near, far, chunk0, chunk1, chunk2, chunk3, total
+):
     rows = own.shape[0]
     per_group = rows // TILE
     total[0 : 2 * rows, :] = received[...].astype(jnp.float32)
@@ -112,6 +136,78 @@
     own[...] = total[0:rows, :]
     near[...] = total[rows : 2 * rows, :].astype(jnp.bfloat16)
     far[...] = total[2 * rows : 3 * rows, :].astype(jnp.bfloat16)
+    chunks = (chunk0, chunk1, chunk2, chunk3)
+    size = chunk0.shape[0] // 2
+
+    @pl.when(place_ref[2] == 1)
+    def _():
+        for turn, chunk in enumerate(chunks):
+            member = place_ref[1] + turn
+            member = jnp.where(member >= len(chunks), member - len(chunks), member)
+            for index in (1, 2):
+                start = pl.multiple_of(index * rows + member * size, size)
+                chunk[(index - 1) * size : index * size, :] = total[pl.ds(start, size), :].astype(jnp.bfloat16)
+
+    @pl.when(place_ref[2] == 0)
+    def _():
+        for chunk in chunks:
+            chunk[...] = jnp.zeros_like(chunk)
+
+
+def cross_kernel(chunk, turn1, turn2, turn3, near, far):
+    total = chunk[...].astype(jnp.float32)
+    for turn in (turn1, turn2, turn3):
+        total = total + turn[...].astype(jnp.float32)
+    total = total.astype(jnp.bfloat16)
+    rows = near.shape[0]
+    near[...] = total[0:rows, :]
+    far[...] = total[rows : 2 * rows, :]
+
+
+def pair_kernel(near, far, out):
+    rows = near.shape[0]
+    out[0:rows, :] = near[...]
+    out[rows : 2 * rows, :] = far[...]
+
+
+def pack_kernel(turn0, turn1, turn2, turn3, out, sems):
+    rows = turn0.shape[0]
+    copies = []
+    for index, turn in enumerate((turn0, turn1, turn2, turn3)):
+        copies.append(pltpu.make_async_copy(turn, out.at[pl.ds(index * rows, rows)], sems.at[index]))
+    for copy in copies:
+        copy.start()
+    for copy in copies:
+        copy.wait()
+
+
+def assemble_kernel(place_ref, near, far, turn0, turn1, turn2, turn3, near_out, far_out, sems):
+    rows = turn0.shape[0] // 2
+
+    @pl.when(place_ref[2] == 1)
+    def _():
+        copies = []
+        for index, turn in enumerate((turn0, turn1, turn2, turn3)):
+            for half, out in enumerate((near_out, far_out)):
+                source = turn.at[pl.ds(half * rows, rows)]
+                copies.append(
+                    pltpu.make_async_copy(source, out.at[pl.ds(index * rows, rows)], sems.at[2 * index + half])
+                )
+        for copy in copies:
+            copy.start()
+        for copy in copies:
+            copy.wait()
+
+    @pl.when(place_ref[2] == 0)
+    def _():
+        copies = [
+            pltpu.make_async_copy(near, near_out, sems.at[0]),
+            pltpu.make_async_copy(far, far_out, sems.at[1]),
+        ]
+        for copy in copies:
+            copy.start()
+        for copy in copies:
+            copy.wait()
 
 
 def fold_kernel(parts, out):
@@ -120,7 +216,7 @@
         out[i] = part
 
 
-def spread_kernel(scale, folded, spread):
+def spread_kernel(scale, folded, after, spread):
     part = (jnp.sum(folded[...], 0) * scale).astype(jnp.bfloat16)
     for i in range(spread.shape[0]):
         spread[i] = part
@@ -141,9 +237,9 @@
             turns[turn - 1][...] = total.astype(jnp.bfloat16)
 
 
-def last_kernel(mine, turn1, turn2, turn3, weight, parts, feat, grad):
+def last_kernel(mine, turn1, turn2, turn3, near, far, weight, parts, feat, grad):
     total = mine[...]
-    for turn in (turn1, turn2, turn3):
+    for turn in (turn1, turn2, turn3, near, far):
         total = total + turn[...].astype(jnp.float32)
     feat[...] = lax.dot_general(
         total.astype(jnp.bfloat16), weight[...], (((1,), (1,)), ((), ())), preferred_element_type=jnp.float32
@@ -167,17 +263,61 @@
     groups = math.prod(lax.axis_size(axis) for axis in DOM)
     members = lax.axis_size("zl")
     group_rows = rows * members
-    core = jnp.stack([lax.axis_index("c"), lax.axis_index("zl")]).astype(jnp.int32)
-    near = near_pairs(groups)
+    x_last, y_last = lax.axis_size("x") - 1, lax.axis_size("y") - 1
+    x_at, y_at, core_at = lax.axis_index("x"), lax.axis_index("y"), lax.axis_index("c")
+    low_edge = (x_at == 0) & (y_at == 0) & (core_at == 0)
+    high_edge = (x_at == x_last) & (y_at == y_last) & (core_at == 1)
+    core = jnp.stack([core_at, lax.axis_index("zl"), (low_edge | high_edge).astype(core_at.dtype)]).astype(jnp.int32)
+    near, near_across = split_pairs(near_pairs(groups))
+    far_inward, far_inward_across = split_pairs(far_pairs(groups, False))
+    far_outward, far_outward_across = split_pairs(far_pairs(groups, True))
+    edge = edge_devices(groups // 2)
+    edge = [2 * k + (0 if k % (groups // 4) == 0 else 1) for k in edge]
+
+    def edge_turned(value, turn):
+        pairs = [(d * members + m, d * members + (m + turn) % members) for d in edge for m in range(members)]
+        return lax.ppermute(value, ALL, pairs)
+
     swap = [(0, 1), (1, 0)]
     smem = pl.BlockSpec(memory_space=pltpu.SMEM)
     vmem = pl.BlockSpec(memory_space=pltpu.VMEM)
     anywhere = pl.BlockSpec(memory_space=pl.ANY)
     flops = 2 * 2 * slots * TILE * TILE * width
 
-    x0 = lax.all_gather(features, "zl", axis=0, tiled=True)
+    near_own = lax.ppermute(features, DOM, near_across)
+    far_own = lax.ppermute(features, DOM, far_inward_across)
+    turns = [
+        lax.ppermute(features, "zl", [(m, (m + turn) % members) for m in range(members)]) for turn in range(1, members)
+    ]
+    x0 = pl.pallas_call(
+        pack_kernel,
+        out_shape=jax.ShapeDtypeStruct((group_rows, width), jnp.bfloat16),
+        in_specs=[anywhere] * members,
+        out_specs=anywhere,
+        scratch_shapes=[pltpu.SemaphoreType.DMA((members,))],
+        compiler_params=params(),
+        name="pack",
+    )(features, *turns)
     x1 = lax.ppermute(x0, DOM, near)
-    x2 = lax.ppermute(x0, DOM, far_pairs(groups, False))
+    x2 = lax.ppermute(x0, DOM, far_inward)
+    edge_pair = pl.pallas_call(
+        pair_kernel,
+        out_shape=jax.ShapeDtypeStruct((2 * rows, width), jnp.bfloat16),
+        in_specs=[vmem, vmem],
+        out_specs=vmem,
+        compiler_params=params(),
+        name="pair",
+    )(near_own, far_own)
+    edge_turns = [edge_pair] + [edge_turned(edge_pair, turn) for turn in range(1, members)]
+    x1, x2 = pl.pallas_call(
+        assemble_kernel,
+        out_shape=(jax.ShapeDtypeStruct((group_rows, width), jnp.bfloat16),) * 2,
+        in_specs=[smem] + [anywhere] * (2 + members),
+        out_specs=(anywhere, anywhere),
+        scratch_shapes=[pltpu.SemaphoreType.DMA((2 * members,))],
+        compiler_params=params(),
+        name="assemble",
+    )(core, x1, x2, *edge_turns)
     x3 = lax.ppermute(x0, "c", swap)
     x4 = lax.ppermute(x1, "c", swap)
 
@@ -194,7 +334,7 @@
     received = lax.ppermute(sent, "c", swap)
 
     layer_out, local = pl.pallas_call(
-        forward_kernel,
+        functools.partial(forward_kernel, members),
         out_shape=(
             jax.ShapeDtypeStruct((rows, width), jnp.bfloat16),
             jax.ShapeDtypeStruct((2 * width, TILE), jnp.float32),
@@ -210,22 +350,34 @@
         name="forward",
     )(core, tile_counts, tile_cols, tile_values, weight, cotangent, x0, x1, x2, x3, x4)
 
-    own, near_sum, far_sum = pl.pallas_call(
+    own, near_sum, far_sum, *chunks = pl.pallas_call(
         keep_kernel,
         out_shape=(
             jax.ShapeDtypeStruct((group_rows, width), jnp.float32),
             jax.ShapeDtypeStruct((group_rows, width), jnp.bfloat16),
             jax.ShapeDtypeStruct((group_rows, width), jnp.bfloat16),
-        ),
+        )
+        + (jax.ShapeDtypeStruct((2 * rows, width), jnp.bfloat16),) * members,
         in_specs=[smem, smem, smem, vmem, vmem, vmem, anywhere],
-        out_specs=(vmem, vmem, vmem),
+        out_specs=(vmem,) * (3 + members),
         scratch_shapes=[pltpu.VMEM((3 * group_rows, width), jnp.float32)],
         compiler_params=params(),
         cost_estimate=pl.CostEstimate(flops=flops, bytes_accessed=8 << 20, transcendentals=0),
         name="keep",
     )(core, tile_counts, tile_cols, tile_values, cotangent, received, local)
     near_in = lax.ppermute(near_sum, DOM, near)
-    far_in = lax.ppermute(far_sum, DOM, far_pairs(groups, True))
+    far_in = lax.ppermute(far_sum, DOM, far_outward)
+    chunk_turns = [edge_turned(chunk, turn) for turn, chunk in enumerate(chunks) if turn > 0]
+    near_edge, far_edge = pl.pallas_call(
+        cross_kernel,
+        out_shape=(jax.ShapeDtypeStruct((rows, width), jnp.bfloat16),) * 2,
+        in_specs=[vmem] * members,
+        out_specs=(vmem, vmem),
+        compiler_params=params(),
+        name="cross",
+    )(chunks[0], *chunk_turns)
+    near_edge = lax.ppermute(near_edge, DOM, near_across)
+    far_edge = lax.ppermute(far_edge, DOM, far_outward_across)
 
     plane = math.prod(lax.axis_size(axis) for axis in PLANE)
     column = math.prod(lax.axis_size(axis) for axis in COLUMN)
@@ -256,11 +408,11 @@
     spread = pl.pallas_call(
         functools.partial(spread_kernel, 1 / math.sqrt(rows * groups * members)),
         out_shape=jax.ShapeDtypeStruct(parts.shape, jnp.bfloat16),
-        in_specs=[vmem],
+        in_specs=[vmem, anywhere],
         out_specs=vmem,
         compiler_params=params(),
         name="spread",
-    )(folded)
+    )(folded, mine)
     parts = lax.all_to_all(spread, PLANE, 0, 0)
     feat_grad, weight_grad = pl.pallas_call(
         last_kernel,
@@ -268,11 +420,11 @@
             jax.ShapeDtypeStruct((rows, width), jnp.float32),
             jax.ShapeDtypeStruct(weight.shape, jnp.float32),
         ),
-        in_specs=[vmem] * (members + 2),
+        in_specs=[vmem] * (members + 4),
         out_specs=(vmem, vmem),
         compiler_params=params(),
         name="last",
-    )(mine, *turns, weight, parts)
+    )(mine, *turns, near_edge, far_edge, weight, parts)
     return (layer_out, feat_grad, weight_grad)
 
 

time: 153 us -> 158 us (1.033)
  blocking collectives: 53.6 us -> 0 us
  starting transfers between devices: 76.6 us -> 114 us
  waiting for transfers between devices: 6.57 us -> 20.1 us
  Pallas kernels: 8.84 us -> 18.9 us
  local copies, waits for them, and re-layouts: 5.79 us -> 3.13 us
    ppermute x2 -> x15, starting transfers between devices: 7.16 us -> 47.6 us  [the longest x1 21.1 us: per_device(): far_own = lax.ppermute(features, DOM, far_inward_across)]
    all_to_all x1 -> x0, blocking collectives: 35 us -> none  [per_device(): folded = lax.all_to_all(part, COLUMN, 0, 0)]
    all_gather x1 -> x0, blocking collectives: 18.6 us -> none  [per_device(): x0 = lax.all_gather(features, 'zl', axis=0, tiled=True)]
    all_to_all x1, starting transfers between devices: 16.3 us -> 4.64 us  [per_device(): parts = lax.all_to_all(local.reshape(plane, -1, TILE), PLANE, 0, 0)]
    ppermute x1, starting transfers between devices: 1.92 us -> 11.9 us  [per_device(): x3 = lax.ppermute(x0, 'c', swap)]
    all_to_all x0 -> x1, starting transfers between devices: none -> 8.63 us  [per_device(): folded = lax.all_to_all(part, COLUMN, 0, 0)]
    ppermute x1, starting transfers between devices: 9.67 us -> 2.46 us  [per_device(): near_in = lax.ppermute(near_sum, DOM, near)]
    all_to_all x0 -> x1, waiting for transfers between devices: none -> 6.94 us  [per_device(): folded = lax.all_to_all(part, COLUMN, 0, 0)]
  transfers between devices with their start and end apart: 12 -> 26, of which waited for: 2 -> 4; matrix products, arithmetic and copies ran while one was open for 0% -> 0% of each run, Pallas kernels for 4% -> 9%
where the time goes in v4:
time: 158 us; the launch traced here: 157 us
  starting transfers between devices  114 us (72%)
  waiting for transfers between devices  20.1 us (13%)
  Pallas kernels  18.9 us (12%)
  local copies, waits for them, and re-layouts  3.13 us (2%)
    ppermute x1, starting transfers between devices, per_device(): far_own = lax.ppermute(features, DOM, far_inward_across)  21.1 us
    ppermute x3, starting transfers between devices, per_device(): lax.ppermute(features, 'zl', [(m, (m + turn) % members) for m in range(me...  15.4 us
    ppermute x1, starting transfers between devices, per_device(): received = lax.ppermute(sent, 'c', swap)  13.5 us
    ppermute x1, starting transfers between devices, per_device(): x3 = lax.ppermute(x0, 'c', swap)  11.9 us
    all_to_all x1, starting transfers between devices, per_device(): parts = lax.all_to_all(spread, PLANE, 0, 0)  10.6 us
    ppermute x3, starting transfers between devices, per_device(): lax.ppermute(value, 'zl', [(m, (m + turn + 1) % members) for m in range(m...  9 us
    all_to_all x1, starting transfers between devices, per_device(): folded = lax.all_to_all(part, COLUMN, 0, 0)  8.63 us
    ppermute x1, waiting for transfers between devices, per_device(): far_edge = lax.ppermute(far_edge, DOM, far_outward_across)  7.56 us
  transfers between devices with their start and end apart: 26, of which 4 were waited for; matrix products, arithmetic and copies ran while one was open for 0% of the time, Pallas kernels for 9%

profile of v4, /device:TPU:1, one launch (start us, length us, event | category | flops | bytes accessed | tf_op | source)
XLA Modules:
  0.0 156.8 jit_solution(13444889782611669804)
XLA Ops:
  0.7 5.9 %collective-permute-start = (bf16[256,256]{1,0:T(8,128)(2,1)}, bf16[256,256]{1,0:T(8,128)(2,1)S(1)}, u32[]{:S(2)}, u32[]{:S(2)}) collective-permute-start(bf16[256,256]{1,0:T(8,128)(2,1)} %turn0.1), channel_id=1, source_target_pairs={{0,1},{1,2},{2,3},{3,0},{4,5},{5,6},{6,7},{7,4},{8,9},{9,10},{10,1... | collective-permute-start | bytes 393224 | tf_op jit(solution)/shard_map/ppermute | solution.py:290
  6.5 7.6 %collective-permute-start.1 = (bf16[256,256]{1,0:T(8,128)(2,1)}, bf16[256,256]{1,0:T(8,128)(2,1)S(1)}, u32[]{:S(2)}, u32[]{:S(2)}) collective-permute-start(bf16[256,256]{1,0:T(8,128)(2,1)} %turn0.1), channel_id=1, source_target_pairs={{0,2},{1,3},{2,0},{3,1},{4,6},{5,7},{6,4},{7,5},{8,10},{9,11},{10,... | collective-permute-start | bytes 393224 | tf_op jit(solution)/shard_map/ppermute | solution.py:290
  14.2 1.9 %collective-permute-start.2 = (bf16[256,256]{1,0:T(8,128)(2,1)}, bf16[256,256]{1,0:T(8,128)(2,1)S(1)}, u32[]{:S(2)}, u32[]{:S(2)}) collective-permute-start(bf16[256,256]{1,0:T(8,128)(2,1)} %turn0.1), channel_id=1, source_target_pairs={{0,3},{1,0},{2,1},{3,2},{4,7},{5,4},{6,5},{7,6},{8,11},{9,8},{10,9... | collective-permute-start | bytes 393224 | tf_op jit(solution)/shard_map/ppermute | solution.py:290
  16.8 21.1 %collective-permute-start.6 = (bf16[256,256]{1,0:T(8,128)(2,1)}, bf16[256,256]{1,0:T(8,128)(2,1)S(1)}, u32[]{:S(2)}, u32[]{:S(2)}) collective-permute-start(bf16[256,256]{1,0:T(8,128)(2,1)} %turn0.1), channel_id=1, source_target_pairs={{4,1020},{504,512},{516,508},{1016,0},{5,1021},{505,513},{517,509}... | collective-permute-start | bytes 393224 | tf_op jit(solution)/shard_map/ppermute | solution.py:288
  37.9 0.9 copy-done.5
  39.5 1.9 %collective-permute-start.3 = (bf16[1024,256]{1,0:T(8,128)(2,1)S(1)}, bf16[1024,256]{1,0:T(8,128)(2,1)S(1)}, u32[]{:S(2)}, u32[]{:S(2)}) collective-permute-start(bf16[1024,256]{1,0:T(8,128)(2,1)S(1)} %pack.1.x0.after), channel_id=1, source_target_pairs={{4,8},{8,4},{12,16},{16,12},{20,24},{24,20},{28,32},{32,28},{36,40... | collective-permute-start | bytes 1572872 | tf_op jit(solution)/shard_map/ppermute | solution.py:301
  41.4 1.3 collective-permute-start.4
  43.6 4.1 %send.1 = bf16[2048,256]{1,0:T(8,128)(2,1)} custom-call(s32[3]{0:T(128)S(1)} %pad_add_fusion.place_ref, s32[2]{0:T(128)S(1)} %copy-done.7, s32[2,20]{1,0:T(2,128)S(1)} %copy-done.6, bf16[2,20,128,128]{3,2,1,0:T(8,128)(2,1)S(1)} %copy-done, bf16[256,256]{1,0:T(8,128)(2,1)S(1)} %copy-done.1, bf16[1024,256]{1,0:T(8,128)(2,1)S(1)} %pack.1.x0.after), custom_call_target="tpu_custom_call" | custom-call | flops 335544320 | bytes 4194304 | tf_op jit(solution)/shard_map/send/pallas_call | solution.py:324
  47.7 13.5 %collective-permute-start.12 = (bf16[2048,256]{1,0:T(8,128)(2,1)}, bf16[2048,256]{1,0:T(8,128)(2,1)S(1)}, u32[]{:S(2)}, u32[]{:S(2)}) collective-permute-start(bf16[2048,256]{1,0:T(8,128)(2,1)} %send.1), channel_id=1, source_target_pairs={{0,4},{4,0},{1,5},{5,1},{2,6},{6,2},{3,7},{7,3},{8,12},{12,8},{9,1... | collective-permute-start | bytes 3145736 | tf_op jit(solution)/shard_map/ppermute | solution.py:334
  62.6 11.9 %collective-permute-start.10 = (bf16[1024,256]{1,0:T(8,128)(2,1)S(1)}, bf16[1024,256]{1,0:T(8,128)(2,1)S(1)}, u32[]{:S(2)}, u32[]{:S(2)}) collective-permute-start(bf16[1024,256]{1,0:T(8,128)(2,1)S(1)} %pack.1.x0.after), channel_id=1, source_target_pairs={{0,4},{4,0},{1,5},{5,1},{2,6},{6,2},{3,7},{7,3},{8,12},{12,8},{9,1... | collective-permute-start | bytes 1572872 | tf_op jit(solution)/shard_map/ppermute | solution.py:321
  75.3 3.2 %collective-permute-start.11 = (bf16[1024,256]{1,0:T(8,128)(2,1)S(1)}, bf16[1024,256]{1,0:T(8,128)(2,1)S(1)}, u32[]{:S(2)}, u32[]{:S(2)}) collective-permute-start(bf16[1024,256]{1,0:T(8,128)(2,1)S(1)} %get-tuple-element.22.x1), channel_id=1, source_target_pairs={{0,4},{4,0},{1,5},{5,1},{2,6},{6,2},{3,7},{7,3},{8,12},{12,8},{9,1... | collective-permute-start | bytes 1572872 | tf_op jit(solution)/shard_map/ppermute | solution.py:322
  78.5 1.5 collective-permute-done.11.x4
  80.0 2.7 %forward.1 = (bf16[256,256]{1,0:T(8,128)(2,1)}, f32[512,128]{1,0:T(8,128)}) custom-call(s32[3]{0:T(128)S(1)} %pad_add_fusion.place_ref, s32[2]{0:T(128)S(1)} %copy-done.7, s32[2,20]{1,0:T(2,128)S(1)} %copy-done.6, bf16[2,20,128,128]{3,2,1,0:T(8,128)(2,1)S(1)} %copy-done, bf16[256,256]{1,0:T(8,128)(2,1)S(1)} %copy-done.4, bf16[256,256]{1,0:T(8,128)(2,1)S(1)} %copy-done.1, ...), custom_call_target="tpu_custom_call" | custom-call | flops 335544320 | bytes 6291456 | tf_op jit(solution)/shard_map/forward/pallas_call | solution.py:336
  82.7 4.6 %all-to-all-start = ((f32[64,8,128]{2,1,0:T(8,128)}), f32[64,8,128]{2,1,0:T(8,128)S(1)}, u32[]{:S(2)}, u32[]{:S(2)}) async-start(f32[64,8,128]{2,1,0:T(8,128)} %bitcast.3), calls=%async_computation | async-start | bytes 524288 | tf_op jit(solution)/shard_map/all_to_all | solution.py:384
  87.4 1.0 copy-done.2
  88.4 1.2 copy-done.3
  89.6 6.4 %keep.1 = (f32[1024,256]{1,0:T(8,128)S(1)}, bf16[1024,256]{1,0:T(8,128)(2,1)}, bf16[1024,256]{1,0:T(8,128)(2,1)}, bf16[512,256]{1,0:T(8,128)(2,1)S(1)}, bf16[512...) custom-call(s32[3]{0:T(128)S(1)} %pad_add_fusion.place_ref, s32[2]{0:T(128)S(1)} %copy-done.7, ...), custom_call_target="tpu_custom_call" | custom-call | flops 335544320 | bytes 8388608 | tf_op jit(solution)/shard_map/keep/pallas_call | solution.py:353
  96.0 2.5 %collective-permute-start.13 = (bf16[1024,256]{1,0:T(8,128)(2,1)}, bf16[1024,256]{1,0:T(8,128)(2,1)S(1)}, u32[]{:S(2)}, u32[]{:S(2)}) collective-permute-start(bf16[1024,256]{1,0:T(8,128)(2,1)} %get-tuple-element.27), channel_id=1, source_target_pairs={{4,8},{8,4},{12,16},{16,12},{20,24},{24,20},{28,32},{32,28},{36,40... | collective-permute-start | bytes 1572872 | tf_op jit(solution)/shard_map/ppermute | solution.py:368
  98.5 1.8 %collective-permute-start.14 = (bf16[1024,256]{1,0:T(8,128)(2,1)}, bf16[1024,256]{1,0:T(8,128)(2,1)S(1)}, u32[]{:S(2)}, u32[]{:S(2)}) collective-permute-start(bf16[1024,256]{1,0:T(8,128)(2,1)} %get-tuple-element.28), channel_id=1, source_target_pairs={{4,12},{8,0},{12,20},{16,8},{20,28},{24,16},{28,36},{32,24},{36,44... | collective-permute-start | bytes 1572872 | tf_op jit(solution)/shard_map/ppermute | solution.py:369
  101.0 1.4 collective-permute-start.19
  102.3 1.4 collective-permute-start.20
  104.4 8.6 %all-to-all-start.1 = ((f32[16,8,128]{2,1,0:T(8,128)}), f32[16,8,128]{2,1,0:T(8,128)S(1)}, u32[]{:S(2)}, u32[]{:S(2)}) async-start(f32[16,8,128]{2,1,0:T(8,128)} %fold.1), calls=%async_computation.1 | async-start | bytes 131072 | tf_op jit(solution)/shard_map/all_to_all | solution.py:394
  113.8 6.9 %all-to-all-done.1.folded = f32[16,8,128]{2,1,0:T(8,128)S(1)} async-done(((f32[16,8,128]{2,1,0:T(8,128)}), f32[16,8,128]{2,1,0:T(8,128)S(1)}, u32[]{:S(2)}, u32[]{:S(2)}) %all-to-all-start.1) | async-done | bytes 65568 | tf_op jit(solution)/shard_map/all_to_all | solution.py:394
  121.4 10.6 %all-to-all-start.2 = ((bf16[64,8,128]{2,1,0:T(8,128)(2,1)}), bf16[64,8,128]{2,1,0:T(8,128)(2,1)S(1)}, u32[]{:S(2)}, u32[]{:S(2)}) async-start(bf16[64,8,128]{2,1,0:T(8,128)(2,1)} %spread.1), calls=%async_computation.2 | async-start | bytes 262144 | tf_op jit(solution)/shard_map/all_to_all | solution.py:416
  132.0 1.2 cross.1
  133.9 1.3 collective-permute-start.22
  135.2 2.1 %collective-permute-start.15 = (bf16[256,256]{1,0:T(8,128)(2,1)S(1)}, bf16[256,256]{1,0:T(8,128)(2,1)S(1)}, u32[]{:S(2)}, u32[]{:S(2)}) collective-permute-start(bf16[256,256]{1,0:T(8,128)(2,1)S(1)} %get-tuple-element.30), channel_id=1, source_target_pairs={{0,1},{1,2},{2,3},{3,0},{4,5},{5,6},{6,7},{7,4},{8,9},{9,10},{10,1... | collective-permute-start | bytes 393224 | tf_op jit(solution)/shard_map/ppermute | solution.py:405
  137.3 2.3 %collective-permute-start.16 = (bf16[256,256]{1,0:T(8,128)(2,1)S(1)}, bf16[256,256]{1,0:T(8,128)(2,1)S(1)}, u32[]{:S(2)}, u32[]{:S(2)}) collective-permute-start(bf16[256,256]{1,0:T(8,128)(2,1)S(1)} %get-tuple-element.31), channel_id=1, source_target_pairs={{0,2},{1,3},{2,0},{3,1},{4,6},{5,7},{6,4},{7,5},{8,10},{9,11},{10,... | collective-permute-start | bytes 393224 | tf_op jit(solution)/shard_map/ppermute | solution.py:405
  139.7 4.6 %collective-permute-start.17 = (bf16[256,256]{1,0:T(8,128)(2,1)S(1)}, bf16[256,256]{1,0:T(8,128)(2,1)S(1)}, u32[]{:S(2)}, u32[]{:S(2)}) collective-permute-start(bf16[256,256]{1,0:T(8,128)(2,1)S(1)} %get-tuple-element.32), channel_id=1, source_target_pairs={{0,3},{1,0},{2,1},{3,2},{4,7},{5,4},{6,5},{7,6},{8,11},{9,8},{10,9... | collective-permute-start | bytes 393224 | tf_op jit(solution)/shard_map/ppermute | solution.py:405
  144.2 7.6 %collective-permute-done.22.far = bf16[256,256]{1,0:T(8,128)(2,1)S(1)} collective-permute-done((bf16[256,256]{1,0:T(8,128)(2,1)S(1)}, bf16[256,256]{1,0:T(8,128)(2,1)S(1)}, u32[]{:S(2)}, u32[]{:S(2)}) %collective-permute-start.22) | collective-permute-done | bytes 131104 | tf_op jit(solution)/shard_map/ppermute | solution.py:380
  151.8 4.1 %collective-permute-done.16.turn2 = bf16[256,256]{1,0:T(8,128)(2,1)S(1)} collective-permute-done((bf16[256,256]{1,0:T(8,128)(2,1)S(1)}, bf16[256,256]{1,0:T(8,128)(2,1)S(1)}, u32[]{:S(2)}, u32[]{:S(2)}) %collective-permute-start.16) | collective-permute-done | bytes 131104 | tf_op jit(solution)/shard_map/ppermute | solution.py:405
  155.9 0.9 last.1
  (48 shorter events, 7.7 us)
Async XLA Ops:
  0.6 42.9 %copy-start = (bf16[2,20,128,128]{3,2,1,0:T(8,128)(2,1)S(1)}, bf16[2,20,128,128]{3,2,1,0:T(8,128)(2,1)}, u32[]{:S(2)}) copy-start(bf16[2,20,128,128]{3,2,1,0:T(8,128)(2,1)} %tiles.5) | copy-start | bytes 3932164
  0.6 42.9 %copy-start.1 = (bf16[256,256]{1,0:T(8,128)(2,1)S(1)}, bf16[256,256]{1,0:T(8,128)(2,1)}, u32[]{:S(2)}) copy-start(bf16[256,256]{1,0:T(8,128)(2,1)} %cotangent.5) | copy-start | bytes 393220
  0.7 37.2 %collective-permute-start = (bf16[256,256]{1,0:T(8,128)(2,1)}, bf16[256,256]{1,0:T(8,128)(2,1)S(1)}, u32[]{:S(2)}, u32[]{:S(2)}) collective-permute-start(bf16[256,256]{1,0:T(8,128)(2,1)} %turn0.1), channel_id=1, source_target_pairs={{0,1},{1,2},{2,3},{3,0},{4,5},{5,6},{6,7},{7,4},{8,9},{9,10},{10,1... | collective-permute-start | bytes 393224 | tf_op jit(solution)/shard_map/ppermute | solution.py:290
  6.5 31.3 %collective-permute-start.1 = (bf16[256,256]{1,0:T(8,128)(2,1)}, bf16[256,256]{1,0:T(8,128)(2,1)S(1)}, u32[]{:S(2)}, u32[]{:S(2)}) collective-permute-start(bf16[256,256]{1,0:T(8,128)(2,1)} %turn0.1), channel_id=1, source_target_pairs={{0,2},{1,3},{2,0},{3,1},{4,6},{5,7},{6,4},{7,5},{8,10},{9,11},{10,... | collective-permute-start | bytes 393224 | tf_op jit(solution)/shard_map/ppermute | solution.py:290
  14.2 23.7 %collective-permute-start.2 = (bf16[256,256]{1,0:T(8,128)(2,1)}, bf16[256,256]{1,0:T(8,128)(2,1)S(1)}, u32[]{:S(2)}, u32[]{:S(2)}) collective-permute-start(bf16[256,256]{1,0:T(8,128)(2,1)} %turn0.1), channel_id=1, source_target_pairs={{0,3},{1,0},{2,1},{3,2},{4,7},{5,4},{6,5},{7,6},{8,11},{9,8},{10,9... | collective-permute-start | bytes 393224 | tf_op jit(solution)/shard_map/ppermute | solution.py:290
  16.1 26.6 %collective-permute-start.5 = (bf16[256,256]{1,0:T(8,128)(2,1)}, bf16[256,256]{1,0:T(8,128)(2,1)S(1)}, u32[]{:S(2)}, u32[]{:S(2)}) collective-permute-start(bf16[256,256]{1,0:T(8,128)(2,1)} %turn0.1), channel_id=1, source_target_pairs={{0,1020},{508,512},{512,508},{1020,0},{1,1021},{509,513},{513,509}... | collective-permute-start | bytes 393224 | tf_op jit(solution)/shard_map/ppermute | solution.py:287
  16.8 26.0 %collective-permute-start.6 = (bf16[256,256]{1,0:T(8,128)(2,1)}, bf16[256,256]{1,0:T(8,128)(2,1)S(1)}, u32[]{:S(2)}, u32[]{:S(2)}) collective-permute-start(bf16[256,256]{1,0:T(8,128)(2,1)} %turn0.1), channel_id=1, source_target_pairs={{4,1020},{504,512},{516,508},{1016,0},{5,1021},{505,513},{517,509}... | collective-permute-start | bytes 393224 | tf_op jit(solution)/shard_map/ppermute | solution.py:288
  38.8 4.8 %copy-start.6 = (s32[2,20]{1,0:T(2,128)S(1)}, s32[2,20]{1,0:T(2,128)}, u32[]{:S(2)}) copy-start(s32[2,20]{1,0:T(2,128)} %cols.5) | copy-start | bytes 484
  38.8 4.8 %copy-start.7 = (s32[2]{0:T(128)S(1)}, s32[2]{0:T(128)}, u32[]{:S(2)}) copy-start(s32[2]{0:T(128)} %counts.5) | copy-start | bytes 28
  39.5 35.0 %collective-permute-start.3 = (bf16[1024,256]{1,0:T(8,128)(2,1)S(1)}, bf16[1024,256]{1,0:T(8,128)(2,1)S(1)}, u32[]{:S(2)}, u32[]{:S(2)}) collective-permute-start(bf16[1024,256]{1,0:T(8,128)(2,1)S(1)} %pack.1.x0.after), channel_id=1, source_target_pairs={{4,8},{8,4},{12,16},{16,12},{20,24},{24,20},{28,32},{32,28},{36,40... | collective-permute-start | bytes 1572872 | tf_op jit(solution)/shard_map/ppermute | solution.py:301
  41.4 33.1 %collective-permute-start.4 = (bf16[1024,256]{1,0:T(8,128)(2,1)S(1)}, bf16[1024,256]{1,0:T(8,128)(2,1)S(1)}, u32[]{:S(2)}, u32[]{:S(2)}) collective-permute-start(bf16[1024,256]{1,0:T(8,128)(2,1)S(1)} %pack.1.x0.after), channel_id=1, source_target_pairs={{0,8},{8,16},{12,4},{16,24},{20,12},{24,32},{28,20},{32,40},{36,28... | collective-permute-start | bytes 1572872 | tf_op jit(solution)/shard_map/ppermute | solution.py:302
  42.8 19.1 %collective-permute-start.7 = (bf16[512,256]{1,0:T(8,128)(2,1)S(1)}, bf16[512,256]{1,0:T(8,128)(2,1)S(1)}, u32[]{:S(2)}, u32[]{:S(2)}) collective-permute-start(bf16[512,256]{1,0:T(8,128)(2,1)S(1)} %pair.1.turn0), channel_id=1, source_target_pairs={{0,1},{1,2},{2,3},{3,0},{508,509},{509,510},{510,511},{511,508},{5... | collective-permute-start | bytes 786440 | tf_op jit(solution)/shard_map/ppermute | solution.py:279
  47.7 32.3 %copy-start.4 = (bf16[256,256]{1,0:T(8,128)(2,1)S(1)}, bf16[256,256]{1,0:T(8,128)(2,1)}, u32[]{:S(2)}) copy-start(bf16[256,256]{1,0:T(8,128)(2,1)} %weight.3) | copy-start | bytes 393220
  47.7 39.7 %collective-permute-start.12 = (bf16[2048,256]{1,0:T(8,128)(2,1)}, bf16[2048,256]{1,0:T(8,128)(2,1)S(1)}, u32[]{:S(2)}, u32[]{:S(2)}) collective-permute-start(bf16[2048,256]{1,0:T(8,128)(2,1)} %send.1), channel_id=1, source_target_pairs={{0,4},{4,0},{1,5},{5,1},{2,6},{6,2},{3,7},{7,3},{8,12},{12,8},{9,1... | collective-permute-start | bytes 3145736 | tf_op jit(solution)/shard_map/ppermute | solution.py:334
  61.2 1.4 collective-permute-start.8
  61.9 12.6 %collective-permute-start.9 = (bf16[512,256]{1,0:T(8,128)(2,1)S(1)}, bf16[512,256]{1,0:T(8,128)(2,1)S(1)}, u32[]{:S(2)}, u32[]{:S(2)}) collective-permute-start(bf16[512,256]{1,0:T(8,128)(2,1)S(1)} %pair.1.turn0), channel_id=1, source_target_pairs={{0,3},{1,0},{2,1},{3,2},{508,511},{509,508},{510,509},{511,510},{5... | collective-permute-start | bytes 786440 | tf_op jit(solution)/shard_map/ppermute | solution.py:279
  62.6 15.9 %collective-permute-start.10 = (bf16[1024,256]{1,0:T(8,128)(2,1)S(1)}, bf16[1024,256]{1,0:T(8,128)(2,1)S(1)}, u32[]{:S(2)}, u32[]{:S(2)}) collective-permute-start(bf16[1024,256]{1,0:T(8,128)(2,1)S(1)} %pack.1.x0.after), channel_id=1, source_target_pairs={{0,4},{4,0},{1,5},{5,1},{2,6},{6,2},{3,7},{7,3},{8,12},{12,8},{9,1... | collective-permute-start | bytes 1572872 | tf_op jit(solution)/shard_map/ppermute | solution.py:321
  75.3 4.7 %collective-permute-start.11 = (bf16[1024,256]{1,0:T(8,128)(2,1)S(1)}, bf16[1024,256]{1,0:T(8,128)(2,1)S(1)}, u32[]{:S(2)}, u32[]{:S(2)}) collective-permute-start(bf16[1024,256]{1,0:T(8,128)(2,1)S(1)} %get-tuple-element.22.x1), channel_id=1, source_target_pairs={{0,4},{4,0},{1,5},{5,1},{2,6},{6,2},{3,7},{7,3},{8,12},{12,8},{9,1... | collective-permute-start | bytes 1572872 | tf_op jit(solution)/shard_map/ppermute | solution.py:322
  82.7 21.0 %all-to-all-start = ((f32[64,8,128]{2,1,0:T(8,128)}), f32[64,8,128]{2,1,0:T(8,128)S(1)}, u32[]{:S(2)}, u32[]{:S(2)}) async-start(f32[64,8,128]{2,1,0:T(8,128)} %bitcast.3), calls=%async_computation | async-start | bytes 524288 | tf_op jit(solution)/shard_map/all_to_all | solution.py:384
  88.4 1.2 copy-start.3
  96.0 17.0 %collective-permute-start.13 = (bf16[1024,256]{1,0:T(8,128)(2,1)}, bf16[1024,256]{1,0:T(8,128)(2,1)S(1)}, u32[]{:S(2)}, u32[]{:S(2)}) collective-permute-start(bf16[1024,256]{1,0:T(8,128)(2,1)} %get-tuple-element.27), channel_id=1, source_target_pairs={{4,8},{8,4},{12,16},{16,12},{20,24},{24,20},{28,32},{32,28},{36,40... | collective-permute-start | bytes 1572872 | tf_op jit(solution)/shard_map/ppermute | solution.py:368
  98.5 14.6 %collective-permute-start.14 = (bf16[1024,256]{1,0:T(8,128)(2,1)}, bf16[1024,256]{1,0:T(8,128)(2,1)S(1)}, u32[]{:S(2)}, u32[]{:S(2)}) collective-permute-start(bf16[1024,256]{1,0:T(8,128)(2,1)} %get-tuple-element.28), channel_id=1, source_target_pairs={{4,12},{8,0},{12,20},{16,8},{20,28},{24,16},{28,36},{32,24},{36,44... | collective-permute-start | bytes 1572872 | tf_op jit(solution)/shard_map/ppermute | solution.py:369
  100.3 31.7 %collective-permute-start.18 = (bf16[512,256]{1,0:T(8,128)(2,1)}, bf16[512,256]{1,0:T(8,128)(2,1)S(1)}, u32[]{:S(2)}, u32[]{:S(2)}) collective-permute-start(bf16[512,256]{1,0:T(8,128)(2,1)} %get-tuple-element.34), channel_id=1, source_target_pairs={{0,1},{1,2},{2,3},{3,0},{508,509},{509,510},{510,511},{511,508},{5... | collective-permute-start | bytes 786440 | tf_op jit(solution)/shard_map/ppermute | solution.py:279
  101.0 31.1 %collective-permute-start.19 = (bf16[512,256]{1,0:T(8,128)(2,1)}, bf16[512,256]{1,0:T(8,128)(2,1)}, u32[]{:S(2)}, u32[]{:S(2)}) collective-permute-start(bf16[512,256]{1,0:T(8,128)(2,1)} %get-tuple-element.35), channel_id=1, source_target_pairs={{0,2},{1,3},{2,0},{3,1},{508,510},{509,511},{510,508},{511,509},{5... | collective-permute-start | bytes 786440 | tf_op jit(solution)/shard_map/ppermute | solution.py:279
  102.3 29.7 %collective-permute-start.20 = (bf16[512,256]{1,0:T(8,128)(2,1)}, bf16[512,256]{1,0:T(8,128)(2,1)}, u32[]{:S(2)}, u32[]{:S(2)}) collective-permute-start(bf16[512,256]{1,0:T(8,128)(2,1)} %get-tuple-element.36), channel_id=1, source_target_pairs={{0,3},{1,0},{2,1},{3,2},{508,511},{509,508},{510,509},{511,510},{5... | collective-permute-start | bytes 786440 | tf_op jit(solution)/shard_map/ppermute | solution.py:279
  104.4 16.3 %all-to-all-start.1 = ((f32[16,8,128]{2,1,0:T(8,128)}), f32[16,8,128]{2,1,0:T(8,128)S(1)}, u32[]{:S(2)}, u32[]{:S(2)}) async-start(f32[16,8,128]{2,1,0:T(8,128)} %fold.1), calls=%async_computation.1 | async-start | bytes 131072 | tf_op jit(solution)/shard_map/all_to_all | solution.py:394
  121.4 34.5 %all-to-all-start.2 = ((bf16[64,8,128]{2,1,0:T(8,128)(2,1)}), bf16[64,8,128]{2,1,0:T(8,128)(2,1)S(1)}, u32[]{:S(2)}, u32[]{:S(2)}) async-start(bf16[64,8,128]{2,1,0:T(8,128)(2,1)} %spread.1), calls=%async_computation.2 | async-start | bytes 262144 | tf_op jit(solution)/shard_map/all_to_all | solution.py:416
  133.2 11.0 %collective-permute-start.21 = (bf16[256,256]{1,0:T(8,128)(2,1)S(1)}, bf16[256,256]{1,0:T(8,128)(2,1)S(1)}, u32[]{:S(2)}, u32[]{:S(2)}) collective-permute-start(bf16[256,256]{1,0:T(8,128)(2,1)S(1)} %get-tuple-element.37), channel_id=1, source_target_pairs={{0,1020},{508,512},{512,508},{1020,0},{1,1021},{509,513},{513,509}... | collective-permute-start | bytes 393224 | tf_op jit(solution)/shard_map/ppermute | solution.py:379
  133.9 17.9 %collective-permute-start.22 = (bf16[256,256]{1,0:T(8,128)(2,1)S(1)}, bf16[256,256]{1,0:T(8,128)(2,1)S(1)}, u32[]{:S(2)}, u32[]{:S(2)}) collective-permute-start(bf16[256,256]{1,0:T(8,128)(2,1)S(1)} %get-tuple-element.38), channel_id=1, source_target_pairs={{0,1016},{508,516},{512,504},{1020,4},{1,1017},{509,517},{513,505}... | collective-permute-start | bytes 393224 | tf_op jit(solution)/shard_map/ppermute | solution.py:380
  135.2 16.6 %collective-permute-start.15 = (bf16[256,256]{1,0:T(8,128)(2,1)S(1)}, bf16[256,256]{1,0:T(8,128)(2,1)S(1)}, u32[]{:S(2)}, u32[]{:S(2)}) collective-permute-start(bf16[256,256]{1,0:T(8,128)(2,1)S(1)} %get-tuple-element.30), channel_id=1, source_target_pairs={{0,1},{1,2},{2,3},{3,0},{4,5},{5,6},{6,7},{7,4},{8,9},{9,10},{10,1... | collective-permute-start | bytes 393224 | tf_op jit(solution)/shard_map/ppermute | solution.py:405
  137.3 18.6 %collective-permute-start.16 = (bf16[256,256]{1,0:T(8,128)(2,1)S(1)}, bf16[256,256]{1,0:T(8,128)(2,1)S(1)}, u32[]{:S(2)}, u32[]{:S(2)}) collective-permute-start(bf16[256,256]{1,0:T(8,128)(2,1)S(1)} %get-tuple-element.31), channel_id=1, source_target_pairs={{0,2},{1,3},{2,0},{3,1},{4,6},{5,7},{6,4},{7,5},{8,10},{9,11},{10,... | collective-permute-start | bytes 393224 | tf_op jit(solution)/shard_map/ppermute | solution.py:405
  139.7 16.2 %collective-permute-start.17 = (bf16[256,256]{1,0:T(8,128)(2,1)S(1)}, bf16[256,256]{1,0:T(8,128)(2,1)S(1)}, u32[]{:S(2)}, u32[]{:S(2)}) collective-permute-start(bf16[256,256]{1,0:T(8,128)(2,1)S(1)} %get-tuple-element.32), channel_id=1, source_target_pairs={{0,3},{1,0},{2,1},{3,2},{4,7},{5,4},{6,5},{7,6},{8,11},{9,8},{10,9... | collective-permute-start | bytes 393224 | tf_op jit(solution)/shard_map/ppermute | solution.py:405
  (2 other events, 1.9 us)

commit v5 on v3

--- a/solution.py
+++ b/solution.py
@@ -30,6 +30,18 @@
         step = 2 if (d % 2 == 1) == outward else -2
         pairs.append((d, (d + step) % groups))
     return pairs
+
+
+def split_pairs(pairs):
+    part = len(pairs) // 2
+    inside = [(a, b) for a, b in pairs if a // part == b // part]
+    across = [(a, b) for a, b in pairs if a // part != b // part]
+    return inside, across
+
+
+def edge_devices(groups):
+    part = groups // 2
+    return [d for d in range(groups) if d % part in (0, part - 1)]
 
 
 def tile_of(col, core, per_group):
@@ -103,7 +115,9 @@
     out[...] = total[...].astype(jnp.bfloat16)
 
 
-def keep_kernel(place_ref, counts, cols, tiles, cotangent, received, after, own, near, far, total):
+def keep_kernel(
+    place_ref, counts, cols, tiles, cotangent, received, after, own, near, far, chunk0, chunk1, chunk2, chunk3, total
+):
     rows = own.shape[0]
     per_group = rows // TILE
     total[0 : 2 * rows, :] = received[...].astype(jnp.float32)
@@ -112,6 +126,32 @@
     own[...] = total[0:rows, :]
     near[...] = total[rows : 2 * rows, :].astype(jnp.bfloat16)
     far[...] = total[2 * rows : 3 * rows, :].astype(jnp.bfloat16)
+    chunks = (chunk0, chunk1, chunk2, chunk3)
+    size = chunk0.shape[0] // 2
+
+    @pl.when(place_ref[2] == 1)
+    def _():
+        for turn, chunk in enumerate(chunks):
+            member = place_ref[1] + turn
+            member = jnp.where(member >= len(chunks), member - len(chunks), member)
+            for index in (1, 2):
+                start = pl.multiple_of(index * rows + member * size, size)
+                chunk[(index - 1) * size : index * size, :] = total[pl.ds(start, size), :].astype(jnp.bfloat16)
+
+    @pl.when(place_ref[2] == 0)
+    def _():
+        for chunk in chunks:
+            chunk[...] = jnp.zeros_like(chunk)
+
+
+def cross_kernel(chunk, turn1, turn2, turn3, after, near, far):
+    total = chunk[...].astype(jnp.float32)
+    for turn in (turn1, turn2, turn3):
+        total = total + turn[...].astype(jnp.float32)
+    total = total.astype(jnp.bfloat16)
+    rows = near.shape[0]
+    near[...] = total[0:rows, :]
+    far[...] = total[rows : 2 * rows, :]
 
 
 def fold_kernel(parts, out):
@@ -120,7 +160,8 @@
         out[i] = part
 
 
-def spread_kernel(scale, folded, spread):
+def spread_kernel(scale, folded, *refs):
+    spread = refs[-1]
     part = (jnp.sum(folded[...], 0) * scale).astype(jnp.bfloat16)
     for i in range(spread.shape[0]):
         spread[i] = part
@@ -141,9 +182,9 @@
             turns[turn - 1][...] = total.astype(jnp.bfloat16)
 
 
-def last_kernel(mine, turn1, turn2, turn3, weight, parts, feat, grad):
+def last_kernel(mine, turn1, turn2, turn3, near, far, weight, parts, feat, grad):
     total = mine[...]
-    for turn in (turn1, turn2, turn3):
+    for turn in (turn1, turn2, turn3, near, far):
         total = total + turn[...].astype(jnp.float32)
     feat[...] = lax.dot_general(
         total.astype(jnp.bfloat16), weight[...], (((1,), (1,)), ((), ())), preferred_element_type=jnp.float32
@@ -167,8 +208,21 @@
     groups = math.prod(lax.axis_size(axis) for axis in DOM)
     members = lax.axis_size("zl")
     group_rows = rows * members
-    core = jnp.stack([lax.axis_index("c"), lax.axis_index("zl")]).astype(jnp.int32)
-    near = near_pairs(groups)
+    x_last, y_last = lax.axis_size("x") - 1, lax.axis_size("y") - 1
+    x_at, y_at, core_at = lax.axis_index("x"), lax.axis_index("y"), lax.axis_index("c")
+    low_edge = (x_at == 0) & (y_at == 0) & (core_at == 0)
+    high_edge = (x_at == x_last) & (y_at == y_last) & (core_at == 1)
+    core = jnp.stack([core_at, lax.axis_index("zl"), (low_edge | high_edge).astype(core_at.dtype)]).astype(jnp.int32)
+    near, near_across = split_pairs(near_pairs(groups))
+    far_inward = far_pairs(groups, False)
+    far_outward, far_outward_across = split_pairs(far_pairs(groups, True))
+    edge = edge_devices(groups // 2)
+    edge = [2 * k + (0 if k % (groups // 4) == 0 else 1) for k in edge]
+
+    def edge_turned(value, turn):
+        pairs = [(d * members + m, d * members + (m + turn) % members) for d in edge for m in range(members)]
+        return lax.ppermute(value, ALL, pairs)
+
     swap = [(0, 1), (1, 0)]
     smem = pl.BlockSpec(memory_space=pltpu.SMEM)
     vmem = pl.BlockSpec(memory_space=pltpu.VMEM)
@@ -176,8 +230,8 @@
     flops = 2 * 2 * slots * TILE * TILE * width
 
     x0 = lax.all_gather(features, "zl", axis=0, tiled=True)
-    x1 = lax.ppermute(x0, DOM, near)
-    x2 = lax.ppermute(x0, DOM, far_pairs(groups, False))
+    x1 = lax.ppermute(x0, DOM, near + near_across)
+    x2 = lax.ppermute(x0, DOM, far_inward)
     x3 = lax.ppermute(x0, "c", swap)
     x4 = lax.ppermute(x1, "c", swap)
 
@@ -210,22 +264,24 @@
         name="forward",
     )(core, tile_counts, tile_cols, tile_values, weight, cotangent, x0, x1, x2, x3, x4)
 
-    own, near_sum, far_sum = pl.pallas_call(
+    own, near_sum, far_sum, *chunks = pl.pallas_call(
         keep_kernel,
         out_shape=(
             jax.ShapeDtypeStruct((group_rows, width), jnp.float32),
             jax.ShapeDtypeStruct((group_rows, width), jnp.bfloat16),
             jax.ShapeDtypeStruct((group_rows, width), jnp.bfloat16),
-        ),
+        )
+        + (jax.ShapeDtypeStruct((2 * rows, width), jnp.bfloat16),) * members,
         in_specs=[smem, smem, smem, vmem, vmem, vmem, anywhere],
-        out_specs=(vmem, vmem, vmem),
+        out_specs=(vmem,) * (3 + members),
         scratch_shapes=[pltpu.VMEM((3 * group_rows, width), jnp.float32)],
         compiler_params=params(),
         cost_estimate=pl.CostEstimate(flops=flops, bytes_accessed=8 << 20, transcendentals=0),
         name="keep",
-    )(core, tile_counts, tile_cols, tile_values, cotangent, received, local)
+    )(core, tile_counts, tile_cols, tile_values, cotangent, received, x1)
     near_in = lax.ppermute(near_sum, DOM, near)
-    far_in = lax.ppermute(far_sum, DOM, far_pairs(groups, True))
+    far_in = lax.ppermute(far_sum, DOM, far_outward)
+    chunk_turns = [edge_turned(chunk, turn) for turn, chunk in enumerate(chunks) if turn > 0]
 
     plane = math.prod(lax.axis_size(axis) for axis in PLANE)
     column = math.prod(lax.axis_size(axis) for axis in COLUMN)
@@ -240,6 +296,16 @@
         name="fold",
     )(parts)
     folded = lax.all_to_all(part, COLUMN, 0, 0)
+    near_edge, far_edge = pl.pallas_call(
+        cross_kernel,
+        out_shape=(jax.ShapeDtypeStruct((rows, width), jnp.bfloat16),) * 2,
+        in_specs=[vmem] * members + [anywhere],
+        out_specs=(vmem, vmem),
+        compiler_params=params(),
+        name="cross",
+    )(chunks[0], *chunk_turns, part)
+    near_edge = lax.ppermute(near_edge, DOM, near_across)
+    far_edge = lax.ppermute(far_edge, DOM, far_outward_across)
     mine, *turns = pl.pallas_call(
         meet_kernel,
         out_shape=(jax.ShapeDtypeStruct((rows, width), jnp.float32),)
@@ -256,11 +322,11 @@
     spread = pl.pallas_call(
         functools.partial(spread_kernel, 1 / math.sqrt(rows * groups * members)),
         out_shape=jax.ShapeDtypeStruct(parts.shape, jnp.bfloat16),
-        in_specs=[vmem],
+        in_specs=[vmem] + [anywhere] * 3,
         out_specs=vmem,
         compiler_params=params(),
         name="spread",
-    )(folded)
+    )(folded, *turns)
     parts = lax.all_to_all(spread, PLANE, 0, 0)
     feat_grad, weight_grad = pl.pallas_call(
         last_kernel,
@@ -268,11 +334,11 @@
             jax.ShapeDtypeStruct((rows, width), jnp.float32),
             jax.ShapeDtypeStruct(weight.shape, jnp.float32),
         ),
-        in_specs=[vmem] * (members + 2),
+        in_specs=[vmem] * (members + 4),
         out_specs=(vmem, vmem),
         compiler_params=params(),
         name="last",
-    )(mine, *turns, weight, parts)
+    )(mine, *turns, near_edge, far_edge, weight, parts)
     return (layer_out, feat_grad, weight_grad)
 
 

time: 153 us -> 158 us (1.033)
  waiting for transfers between devices: 6.57 us -> 20.2 us
  blocking collectives: 53.6 us -> 45.8 us
  Pallas kernels: 8.84 us -> 12.9 us
  starting transfers between devices: 76.6 us -> 73.4 us
  local copies, waits for them, and re-layouts: 5.79 us -> 3.57 us
    ppermute x3 -> x8, waiting for transfers between devices: 2.04 us -> 20.1 us  [the longest x1 16.7 us: per_device(): far_edge = lax.ppermute(far_edge, DOM, far_outward_across)]
    all_to_all x1, starting transfers between devices: 16.3 us -> 5.37 us  [per_device(): parts = lax.all_to_all(local.reshape(plane, -1, TILE), PLANE, 0, 0)]
    ppermute x1, starting transfers between devices: 1.92 us -> 11.1 us  [per_device(): x3 = lax.ppermute(x0, 'c', swap)]
    all_to_all x1, blocking collectives: 35 us -> 27.2 us  [per_device(): folded = lax.all_to_all(part, COLUMN, 0, 0)]
    ppermute x1, starting transfers between devices: 9.67 us -> 1.91 us  [per_device(): near_in = lax.ppermute(near_sum, DOM, near)]
    ppermute x1, starting transfers between devices: 2.41 us -> 10 us  [per_device(): x4 = lax.ppermute(x1, 'c', swap)]
    ppermute x1, starting transfers between devices: 17.1 us -> 12.4 us  [per_device(): received = lax.ppermute(sent, 'c', swap)]
    all_to_all x1, starting transfers between devices: 4.62 us -> 9.13 us  [per_device(): parts = lax.all_to_all(spread, PLANE, 0, 0)]
  transfers between devices with their start and end apart: 12 -> 17, of which waited for: 2 -> 2; matrix products, arithmetic and copies ran while one was open for 0% -> 0% of each run, Pallas kernels for 4% -> 5%
where the time goes in v5:
time: 158 us; the launch traced here: 157 us
  starting transfers between devices  73.4 us (46%)
  blocking collectives  45.8 us (29%)
  waiting for transfers between devices  20.2 us (13%)
  Pallas kernels  12.9 us (8%)
  local copies, waits for them, and re-layouts  3.57 us (2%)
    all_to_all x1, blocking collectives, per_device(): folded = lax.all_to_all(part, COLUMN, 0, 0)  27.2 us
    all_gather x1, blocking collectives, per_device(): x0 = lax.all_gather(features, 'zl', axis=0, tiled=True)  18.6 us
    ppermute x1, waiting for transfers between devices, per_device(): far_edge = lax.ppermute(far_edge, DOM, far_outward_across)  16.7 us
    ppermute x3, starting transfers between devices, per_device(): lax.ppermute(value, 'zl', [(m, (m + turn + 1) % members) for m in range(m...  13.4 us
    ppermute x1, starting transfers between devices, per_device(): received = lax.ppermute(sent, 'c', swap)  12.4 us
    ppermute x1, starting transfers between devices, per_device(): x3 = lax.ppermute(x0, 'c', swap)  11.1 us
    ppermute x1, starting transfers between devices, per_device(): x4 = lax.ppermute(x1, 'c', swap)  10 us
    all_to_all x1, starting transfers between devices, per_device(): parts = lax.all_to_all(spread, PLANE, 0, 0)  9.13 us
  transfers between devices with their start and end apart: 17, of which 2 were waited for; matrix products, arithmetic and copies ran while one was open for 0% of the time, Pallas kernels for 5%

profile of v5, /device:TPU:1, one launch (start us, length us, event | category | flops | bytes accessed | tf_op | source)
XLA Modules:
  0.0 156.8 jit_solution(4169181894705853923)
XLA Ops:
  0.7 18.6 %all_gather.3.x0.after = bf16[1024,256]{1,0:T(8,128)(2,1)S(1)} all-gather(bf16[256,256]{1,0:T(8,128)(2,1)} %param.6), channel_id=1, replica_groups=mesh['zh'=2,'x'=8,'y'=8,'c'=2,'zl'=4] {'zl'}, dimensions={0}, use_global_device_ids=true | all-gather | bytes 655360 | tf_op jit(solution)/shard_map/all_gather | solution.py:232
  19.3 1.3 copy-done
  20.7 0.9 copy-done.1
  21.6 0.7 copy-done.4
  22.2 0.7 copy-done.5
  22.9 3.9 %send.1 = bf16[2048,256]{1,0:T(8,128)(2,1)S(1)} custom-call(s32[3]{0:T(128)S(1)} %pad_add_fusion.place_ref, s32[2]{0:T(128)S(1)} %copy-done.5, s32[2,20]{1,0:T(2,128)S(1)} %copy-done.4, bf16[2,20,128,128]{3,2,1,0:T(8,128)(2,1)S(1)} %copy-done, bf16[256,256]{1,0:T(8,128)(2,1)S(1)} %copy-done.1, bf16[1024,256]{1,0:T(8,128)(2,1)S(1)} %all_gather.3.x0.after), custom_call_target="tpu_custom_call" | custom-call | flops 335544320 | bytes 4194304 | tf_op jit(solution)/shard_map/send/pallas_call | solution.py:238
  26.8 12.4 %collective-permute-start.4 = (bf16[2048,256]{1,0:T(8,128)(2,1)S(1)}, bf16[2048,256]{1,0:T(8,128)(2,1)S(1)}, u32[]{:S(2)}, u32[]{:S(2)}) collective-permute-start(bf16[2048,256]{1,0:T(8,128)(2,1)S(1)} %send.1), channel_id=1, source_target_pairs={{0,4},{4,0},{1,5},{5,1},{2,6},{6,2},{3,7},{7,3},{8,12},{12,8},{9,1... | collective-permute-start | bytes 3145736 | tf_op jit(solution)/shard_map/ppermute | solution.py:248
  39.2 1.9 %collective-permute-start = (bf16[1024,256]{1,0:T(8,128)(2,1)S(1)}, bf16[1024,256]{1,0:T(8,128)(2,1)S(1)}, u32[]{:S(2)}, u32[]{:S(2)}) collective-permute-start(bf16[1024,256]{1,0:T(8,128)(2,1)S(1)} %all_gather.3.x0.after), channel_id=1, source_target_pairs={{4,8},{8,4},{12,16},{16,12},{20,24},{24,20},{28,32},{32,28},{36,40... | collective-permute-start | bytes 1572872 | tf_op jit(solution)/shard_map/ppermute | solution.py:233
  41.2 11.1 %collective-permute-start.2 = (bf16[1024,256]{1,0:T(8,128)(2,1)S(1)}, bf16[1024,256]{1,0:T(8,128)(2,1)S(1)}, u32[]{:S(2)}, u32[]{:S(2)}) collective-permute-start(bf16[1024,256]{1,0:T(8,128)(2,1)S(1)} %all_gather.3.x0.after), channel_id=1, source_target_pairs={{0,4},{4,0},{1,5},{5,1},{2,6},{6,2},{3,7},{7,3},{8,12},{12,8},{9,1... | collective-permute-start | bytes 1572872 | tf_op jit(solution)/shard_map/ppermute | solution.py:235
  52.3 2.8 %collective-permute-start.1 = (bf16[1024,256]{1,0:T(8,128)(2,1)S(1)}, bf16[1024,256]{1,0:T(8,128)(2,1)S(1)}, u32[]{:S(2)}, u32[]{:S(2)}) collective-permute-start(bf16[1024,256]{1,0:T(8,128)(2,1)S(1)} %all_gather.3.x0.after), channel_id=1, source_target_pairs={{0,8},{4,1020},{8,16},{12,4},{16,24},{20,12},{24,32},{28,20},{32,4... | collective-permute-start | bytes 1572872 | tf_op jit(solution)/shard_map/ppermute | solution.py:234
  55.1 10.0 %collective-permute-start.3 = (bf16[1024,256]{1,0:T(8,128)(2,1)S(1)}, bf16[1024,256]{1,0:T(8,128)(2,1)S(1)}, u32[]{:S(2)}, u32[]{:S(2)}) collective-permute-start(bf16[1024,256]{1,0:T(8,128)(2,1)S(1)} %collective-permute-done.x1.after), channel_id=1, source_target_pairs={{0,4},{4,0},{1,5},{5,1},{2,6},{6,2},{3,7},{7,3},{8,12},{12,8},{9,1... | collective-permute-start | bytes 1572872 | tf_op jit(solution)/shard_map/ppermute | solution.py:236
  65.1 4.2 %keep.1 = (f32[1024,256]{1,0:T(8,128)S(1)}, bf16[1024,256]{1,0:T(8,128)(2,1)}, bf16[1024,256]{1,0:T(8,128)(2,1)S(1)}, bf16[512,256]{1,0:T(8,128)(2,1)S(1)}, bf16...) custom-call(s32[3]{0:T(128)S(1)} %pad_add_fusion.place_ref, s32[2]{0:T(128)S(1)} %copy-done.5, ...), custom_call_target="tpu_custom_call" | custom-call | flops 335544320 | bytes 8388608 | tf_op jit(solution)/shard_map/keep/pallas_call | solution.py:267
  69.3 1.9 %collective-permute-start.5 = (bf16[1024,256]{1,0:T(8,128)(2,1)}, bf16[1024,256]{1,0:T(8,128)(2,1)S(1)}, u32[]{:S(2)}, u32[]{:S(2)}) collective-permute-start(bf16[1024,256]{1,0:T(8,128)(2,1)} %get-tuple-element.22), channel_id=1, source_target_pairs={{4,8},{8,4},{12,16},{16,12},{20,24},{24,20},{28,32},{32,28},{36,40... | collective-permute-start | bytes 1572872 | tf_op jit(solution)/shard_map/ppermute | solution.py:282
  71.2 1.3 collective-permute-start.6
  72.6 2.3 %forward.1 = (bf16[256,256]{1,0:T(8,128)(2,1)}, f32[512,128]{1,0:T(8,128)}) custom-call(s32[3]{0:T(128)S(1)} %pad_add_fusion.place_ref, s32[2]{0:T(128)S(1)} %copy-done.5, s32[2,20]{1,0:T(2,128)S(1)} %copy-done.4, bf16[2,20,128,128]{3,2,1,0:T(8,128)(2,1)S(1)} %copy-done, bf16[256,256]{1,0:T(8,128)(2,1)S(1)} %copy-done.3, bf16[256,256]{1,0:T(8,128)(2,1)S(1)} %copy-done.2, ...), custom_call_target="tpu_custom_call" | custom-call | flops 335544320 | bytes 6291456 | tf_op jit(solution)/shard_map/forward/pallas_call | solution.py:250
  74.9 5.4 %all-to-all-start = ((f32[64,8,128]{2,1,0:T(8,128)}), f32[64,8,128]{2,1,0:T(8,128)S(1)}, u32[]{:S(2)}, u32[]{:S(2)}) async-start(f32[64,8,128]{2,1,0:T(8,128)} %bitcast.3), calls=%async_computation | async-start | bytes 524288 | tf_op jit(solution)/shard_map/all_to_all | solution.py:288
  80.3 3.4 %collective-permute-done.6.far = bf16[1024,256]{1,0:T(8,128)(2,1)S(1)} collective-permute-done((bf16[1024,256]{1,0:T(8,128)(2,1)S(1)}, bf16[1024,256]{1,0:T(8,128)(2,1)S(1)}, u32[]{:S(2)}, u32[]{:S(2)}) %collective-permute-start.6) | collective-permute-done | bytes 524320 | tf_op jit(solution)/shard_map/ppermute | solution.py:283
  83.8 0.7 meet.1
  84.5 1.9 %collective-permute-start.7 = (bf16[256,256]{1,0:T(8,128)(2,1)S(1)}, bf16[256,256]{1,0:T(8,128)(2,1)S(1)}, u32[]{:S(2)}, u32[]{:S(2)}) collective-permute-start(bf16[256,256]{1,0:T(8,128)(2,1)S(1)} %get-tuple-element.25), channel_id=1, source_target_pairs={{0,1},{1,2},{2,3},{3,0},{4,5},{5,6},{6,7},{7,4},{8,9},{9,10},{10,1... | collective-permute-start | bytes 393224 | tf_op jit(solution)/shard_map/ppermute | solution.py:319
  86.4 0.7 collective-permute-start.10
  87.1 0.7 collective-permute-start.11
  87.8 0.7 collective-permute-start.12
  88.5 9.6 %collective-permute-start.8 = (bf16[256,256]{1,0:T(8,128)(2,1)S(1)}, bf16[256,256]{1,0:T(8,128)(2,1)S(1)}, u32[]{:S(2)}, u32[]{:S(2)}) collective-permute-start(bf16[256,256]{1,0:T(8,128)(2,1)S(1)} %get-tuple-element.26), channel_id=1, source_target_pairs={{0,2},{1,3},{2,0},{3,1},{4,6},{5,7},{6,4},{7,5},{8,10},{9,11},{10,... | collective-permute-start | bytes 393224 | tf_op jit(solution)/shard_map/ppermute | solution.py:319
  98.0 1.9 %collective-permute-start.9 = (bf16[256,256]{1,0:T(8,128)(2,1)S(1)}, bf16[256,256]{1,0:T(8,128)(2,1)S(1)}, u32[]{:S(2)}, u32[]{:S(2)}) collective-permute-start(bf16[256,256]{1,0:T(8,128)(2,1)S(1)} %get-tuple-element.27), channel_id=1, source_target_pairs={{0,3},{1,0},{2,1},{3,2},{4,7},{5,4},{6,5},{7,6},{8,11},{9,8},{10,9... | collective-permute-start | bytes 393224 | tf_op jit(solution)/shard_map/ppermute | solution.py:319
  100.1 27.2 %all_to_all.15.folded = f32[16,8,128]{2,1,0:T(8,128)S(1)} all-to-all(f32[16,8,128]{2,1,0:T(8,128)S(1)} %fold.1.after), channel_id=1, replica_groups=mesh['zh'=2,'x'=8,'y'=8,'c'=2,'zl'=4] {'zh','zl','c'}, dimensions={0} | all-to-all | bytes 131072 | tf_op jit(solution)/shard_map/all_to_all | solution.py:298
  127.2 0.7 spread.1
  127.9 9.1 %all-to-all-start.2 = ((bf16[64,8,128]{2,1,0:T(8,128)(2,1)}), bf16[64,8,128]{2,1,0:T(8,128)(2,1)S(1)}, u32[]{:S(2)}, u32[]{:S(2)}) async-start(bf16[64,8,128]{2,1,0:T(8,128)(2,1)} %spread.1), calls=%async_computation.2 | async-start | bytes 262144 | tf_op jit(solution)/shard_map/all_to_all | solution.py:330
  137.1 0.1 cross.1
  137.2 0.7 collective-permute-start.13
  137.9 1.3 collective-permute-start.14
  139.2 16.7 %collective-permute-done.14.far = bf16[256,256]{1,0:T(8,128)(2,1)S(1)} collective-permute-done((bf16[256,256]{1,0:T(8,128)(2,1)S(1)}, bf16[256,256]{1,0:T(8,128)(2,1)S(1)}, u32[]{:S(2)}, u32[]{:S(2)}) %collective-permute-start.14) | collective-permute-done | bytes 131104 | tf_op jit(solution)/shard_map/ppermute | solution.py:308
  155.9 0.9 last.1
  (29 shorter events, 0.2 us)
Async XLA Ops:
  19.3 1.3 copy-start
  20.7 0.9 copy-start.1
  21.6 0.7 copy-start.4
  22.2 0.7 copy-start.5
  26.8 45.8 %copy-start.2 = (bf16[256,256]{1,0:T(8,128)(2,1)S(1)}, bf16[256,256]{1,0:T(8,128)(2,1)}, u32[]{:S(2)}) copy-start(bf16[256,256]{1,0:T(8,128)(2,1)} %cotangent.5) | copy-start | bytes 393220
  26.8 45.8 %copy-start.3 = (bf16[256,256]{1,0:T(8,128)(2,1)S(1)}, bf16[256,256]{1,0:T(8,128)(2,1)}, u32[]{:S(2)}) copy-start(bf16[256,256]{1,0:T(8,128)(2,1)} %weight.3) | copy-start | bytes 393220
  26.8 38.3 %collective-permute-start.4 = (bf16[2048,256]{1,0:T(8,128)(2,1)S(1)}, bf16[2048,256]{1,0:T(8,128)(2,1)S(1)}, u32[]{:S(2)}, u32[]{:S(2)}) collective-permute-start(bf16[2048,256]{1,0:T(8,128)(2,1)S(1)} %send.1), channel_id=1, source_target_pairs={{0,4},{4,0},{1,5},{5,1},{2,6},{6,2},{3,7},{7,3},{8,12},{12,8},{9,1... | collective-permute-start | bytes 3145736 | tf_op jit(solution)/shard_map/ppermute | solution.py:248
  39.2 15.8 %collective-permute-start = (bf16[1024,256]{1,0:T(8,128)(2,1)S(1)}, bf16[1024,256]{1,0:T(8,128)(2,1)S(1)}, u32[]{:S(2)}, u32[]{:S(2)}) collective-permute-start(bf16[1024,256]{1,0:T(8,128)(2,1)S(1)} %all_gather.3.x0.after), channel_id=1, source_target_pairs={{4,8},{8,4},{12,16},{16,12},{20,24},{24,20},{28,32},{32,28},{36,40... | collective-permute-start | bytes 1572872 | tf_op jit(solution)/shard_map/ppermute | solution.py:233
  41.2 31.4 %collective-permute-start.2 = (bf16[1024,256]{1,0:T(8,128)(2,1)S(1)}, bf16[1024,256]{1,0:T(8,128)(2,1)S(1)}, u32[]{:S(2)}, u32[]{:S(2)}) collective-permute-start(bf16[1024,256]{1,0:T(8,128)(2,1)S(1)} %all_gather.3.x0.after), channel_id=1, source_target_pairs={{0,4},{4,0},{1,5},{5,1},{2,6},{6,2},{3,7},{7,3},{8,12},{12,8},{9,1... | collective-permute-start | bytes 1572872 | tf_op jit(solution)/shard_map/ppermute | solution.py:235
  52.3 20.3 %collective-permute-start.1 = (bf16[1024,256]{1,0:T(8,128)(2,1)S(1)}, bf16[1024,256]{1,0:T(8,128)(2,1)S(1)}, u32[]{:S(2)}, u32[]{:S(2)}) collective-permute-start(bf16[1024,256]{1,0:T(8,128)(2,1)S(1)} %all_gather.3.x0.after), channel_id=1, source_target_pairs={{0,8},{4,1020},{8,16},{12,4},{16,24},{20,12},{24,32},{28,20},{32,4... | collective-permute-start | bytes 1572872 | tf_op jit(solution)/shard_map/ppermute | solution.py:234
  55.1 17.5 %collective-permute-start.3 = (bf16[1024,256]{1,0:T(8,128)(2,1)S(1)}, bf16[1024,256]{1,0:T(8,128)(2,1)S(1)}, u32[]{:S(2)}, u32[]{:S(2)}) collective-permute-start(bf16[1024,256]{1,0:T(8,128)(2,1)S(1)} %collective-permute-done.x1.after), channel_id=1, source_target_pairs={{0,4},{4,0},{1,5},{5,1},{2,6},{6,2},{3,7},{7,3},{8,12},{12,8},{9,1... | collective-permute-start | bytes 1572872 | tf_op jit(solution)/shard_map/ppermute | solution.py:236
  69.3 14.4 %copy-start.6 = (bf16[512,256]{1,0:T(8,128)(2,1)}, bf16[512,256]{1,0:T(8,128)(2,1)S(1)}, u32[]{:S(2)}) copy-start(bf16[512,256]{1,0:T(8,128)(2,1)S(1)} %get-tuple-element.29) | copy-start | bytes 786436
  69.3 11.0 %collective-permute-start.5 = (bf16[1024,256]{1,0:T(8,128)(2,1)}, bf16[1024,256]{1,0:T(8,128)(2,1)S(1)}, u32[]{:S(2)}, u32[]{:S(2)}) collective-permute-start(bf16[1024,256]{1,0:T(8,128)(2,1)} %get-tuple-element.22), channel_id=1, source_target_pairs={{4,8},{8,4},{12,16},{16,12},{20,24},{24,20},{28,32},{32,28},{36,40... | collective-permute-start | bytes 1572872 | tf_op jit(solution)/shard_map/ppermute | solution.py:282
  71.2 12.5 %collective-permute-start.6 = (bf16[1024,256]{1,0:T(8,128)(2,1)S(1)}, bf16[1024,256]{1,0:T(8,128)(2,1)S(1)}, u32[]{:S(2)}, u32[]{:S(2)}) collective-permute-start(bf16[1024,256]{1,0:T(8,128)(2,1)S(1)} %get-tuple-element.23), channel_id=1, source_target_pairs={{4,12},{8,0},{12,20},{16,8},{20,28},{24,16},{28,36},{32,24},{36,44... | collective-permute-start | bytes 1572872 | tf_op jit(solution)/shard_map/ppermute | solution.py:283
  74.9 25.0 %all-to-all-start = ((f32[64,8,128]{2,1,0:T(8,128)}), f32[64,8,128]{2,1,0:T(8,128)S(1)}, u32[]{:S(2)}, u32[]{:S(2)}) async-start(f32[64,8,128]{2,1,0:T(8,128)} %bitcast.3), calls=%async_computation | async-start | bytes 524288 | tf_op jit(solution)/shard_map/all_to_all | solution.py:288
  83.8 2.6 %copy-start.7 = (bf16[512,256]{1,0:T(8,128)(2,1)S(1)}, bf16[512,256]{1,0:T(8,128)(2,1)}, u32[]{:S(2)}) copy-start(bf16[512,256]{1,0:T(8,128)(2,1)} %copy-done.6) | copy-start | bytes 786436
  84.5 13.6 %collective-permute-start.7 = (bf16[256,256]{1,0:T(8,128)(2,1)S(1)}, bf16[256,256]{1,0:T(8,128)(2,1)S(1)}, u32[]{:S(2)}, u32[]{:S(2)}) collective-permute-start(bf16[256,256]{1,0:T(8,128)(2,1)S(1)} %get-tuple-element.25), channel_id=1, source_target_pairs={{0,1},{1,2},{2,3},{3,0},{4,5},{5,6},{6,7},{7,4},{8,9},{9,10},{10,1... | collective-permute-start | bytes 393224 | tf_op jit(solution)/shard_map/ppermute | solution.py:319
  86.4 50.6 %collective-permute-start.10 = (bf16[512,256]{1,0:T(8,128)(2,1)S(1)}, bf16[512,256]{1,0:T(8,128)(2,1)S(1)}, u32[]{:S(2)}, u32[]{:S(2)}) collective-permute-start(bf16[512,256]{1,0:T(8,128)(2,1)S(1)} %copy-done.7), channel_id=1, source_target_pairs={{0,1},{1,2},{2,3},{3,0},{508,509},{509,510},{510,511},{511,508},{5... | collective-permute-start | bytes 786440 | tf_op jit(solution)/shard_map/ppermute | solution.py:224
  87.1 50.0 %collective-permute-start.11 = (bf16[512,256]{1,0:T(8,128)(2,1)}, bf16[512,256]{1,0:T(8,128)(2,1)S(1)}, u32[]{:S(2)}, u32[]{:S(2)}) collective-permute-start(bf16[512,256]{1,0:T(8,128)(2,1)} %get-tuple-element.30), channel_id=1, source_target_pairs={{0,2},{1,3},{2,0},{3,1},{508,510},{509,511},{510,508},{511,509},{5... | collective-permute-start | bytes 786440 | tf_op jit(solution)/shard_map/ppermute | solution.py:224
  87.8 49.3 %collective-permute-start.12 = (bf16[512,256]{1,0:T(8,128)(2,1)}, bf16[512,256]{1,0:T(8,128)(2,1)S(1)}, u32[]{:S(2)}, u32[]{:S(2)}) collective-permute-start(bf16[512,256]{1,0:T(8,128)(2,1)} %get-tuple-element.31), channel_id=1, source_target_pairs={{0,3},{1,0},{2,1},{3,2},{508,511},{509,508},{510,509},{511,510},{5... | collective-permute-start | bytes 786440 | tf_op jit(solution)/shard_map/ppermute | solution.py:224
  88.5 38.8 %collective-permute-start.8 = (bf16[256,256]{1,0:T(8,128)(2,1)S(1)}, bf16[256,256]{1,0:T(8,128)(2,1)S(1)}, u32[]{:S(2)}, u32[]{:S(2)}) collective-permute-start(bf16[256,256]{1,0:T(8,128)(2,1)S(1)} %get-tuple-element.26), channel_id=1, source_target_pairs={{0,2},{1,3},{2,0},{3,1},{4,6},{5,7},{6,4},{7,5},{8,10},{9,11},{10,... | collective-permute-start | bytes 393224 | tf_op jit(solution)/shard_map/ppermute | solution.py:319
  98.0 29.2 %collective-permute-start.9 = (bf16[256,256]{1,0:T(8,128)(2,1)S(1)}, bf16[256,256]{1,0:T(8,128)(2,1)S(1)}, u32[]{:S(2)}, u32[]{:S(2)}) collective-permute-start(bf16[256,256]{1,0:T(8,128)(2,1)S(1)} %get-tuple-element.27), channel_id=1, source_target_pairs={{0,3},{1,0},{2,1},{3,2},{4,7},{5,4},{6,5},{7,6},{8,11},{9,8},{10,9... | collective-permute-start | bytes 393224 | tf_op jit(solution)/shard_map/ppermute | solution.py:319
  127.9 28.0 %all-to-all-start.2 = ((bf16[64,8,128]{2,1,0:T(8,128)(2,1)}), bf16[64,8,128]{2,1,0:T(8,128)(2,1)S(1)}, u32[]{:S(2)}, u32[]{:S(2)}) async-start(bf16[64,8,128]{2,1,0:T(8,128)(2,1)} %spread.1), calls=%async_computation.2 | async-start | bytes 262144 | tf_op jit(solution)/shard_map/all_to_all | solution.py:330
  137.2 2.0 %collective-permute-start.13 = (bf16[256,256]{1,0:T(8,128)(2,1)S(1)}, bf16[256,256]{1,0:T(8,128)(2,1)S(1)}, u32[]{:S(2)}, u32[]{:S(2)}) collective-permute-start(bf16[256,256]{1,0:T(8,128)(2,1)S(1)} %get-tuple-element.33), channel_id=1, source_target_pairs={{0,1020},{508,512},{512,508},{1020,0},{1,1021},{509,513},{513,509}... | collective-permute-start | bytes 393224 | tf_op jit(solution)/shard_map/ppermute | solution.py:307
  137.9 18.0 %collective-permute-start.14 = (bf16[256,256]{1,0:T(8,128)(2,1)S(1)}, bf16[256,256]{1,0:T(8,128)(2,1)S(1)}, u32[]{:S(2)}, u32[]{:S(2)}) collective-permute-start(bf16[256,256]{1,0:T(8,128)(2,1)S(1)} %get-tuple-element.34), channel_id=1, source_target_pairs={{0,1016},{508,516},{512,504},{1020,4},{1,1017},{509,517},{513,505}... | collective-permute-start | bytes 393224 | tf_op jit(solution)/shard_map/ppermute | solution.py:308

commit v6 on v3

--- a/solution.py
+++ b/solution.py
@@ -16,15 +16,7 @@
 VMEM_LIMIT = 24 * 1024 * 1024
 
 
-def near_pairs(groups):
-    pairs = []
-    for d in range(groups):
-        k, c = d // 2, d % 2
-        pairs.append((d, (2 * (k - 1) + 1 if c == 0 else 2 * (k + 1)) % groups))
-    return pairs
-
-
-def far_pairs(groups, outward):
+def near_pairs(groups, outward):
     pairs = []
     for d in range(groups):
         step = 2 if (d % 2 == 1) == outward else -2
@@ -32,20 +24,24 @@
     return pairs
 
 
+def far_pairs(groups):
+    return [(d, (d + (3 if d % 2 == 0 else -3)) % groups) for d in range(groups)]
+
+
 def tile_of(col, core, per_group):
     band = col // per_group
-    band = jnp.where(core == 0, 4 - band, band)
-    place = jnp.where(band >= 2, band - 2, 4 - band)
+    band = jnp.where(core == 0, band, 4 - band)
+    place = jnp.where(band >= 3, jnp.where(band == 3, 3, 1), jnp.where(band == 2, 0, 5 - band))
     return place * per_group + col % per_group
 
 
-def forward_kernel(place_ref, counts, cols, tiles, weight, cotangent, x0, x1, x2, x3, x4, out, local, band, sems):
-    sources = (x0, x1, x2, x3, x4)
+def forward_kernel(place_ref, counts, cols, tiles, weight, cotangent, x0, x1, x3, x4, x5, out, local, band, sems):
+    sources = ((0, x0), (1, x1), (3, x3), (4, x4), (5, x5))
     rows = x0.shape[0]
     per_group = rows // TILE
     copies = []
-    for index, source in enumerate(sources):
-        copy = pltpu.make_async_copy(source, band.at[pl.ds(index * rows, rows)], sems.at[index])
+    for index, (place, source) in enumerate(sources):
+        copy = pltpu.make_async_copy(source, band.at[pl.ds(place * rows, rows)], sems.at[index])
         copy.start()
         copies.append(copy)
     for copy in copies:
@@ -97,21 +93,20 @@
 
 
 def send_kernel(place_ref, counts, cols, tiles, cotangent, after, out, total):
-    per_group = out.shape[0] // TILE // 2
+    per_group = out.shape[0] // TILE // 3
     total[...] = jnp.zeros_like(total)
-    scatter_tiles(place_ref[0], counts, cols, tiles, cotangent, total, 3 * per_group, 5 * per_group, per_group)
+    scatter_tiles(place_ref[0], counts, cols, tiles, cotangent, total, 3 * per_group, 6 * per_group, per_group)
     out[...] = total[...].astype(jnp.bfloat16)
 
 
 def keep_kernel(place_ref, counts, cols, tiles, cotangent, received, after, own, near, far, total):
     rows = own.shape[0]
     per_group = rows // TILE
-    total[0 : 2 * rows, :] = received[...].astype(jnp.float32)
-    total[2 * rows : 3 * rows, :] = jnp.zeros_like(total[2 * rows : 3 * rows, :])
-    scatter_tiles(place_ref[0], counts, cols, tiles, cotangent, total, 0, 3 * per_group, per_group)
+    total[...] = received[0 : 2 * rows, :].astype(jnp.float32)
+    scatter_tiles(place_ref[0], counts, cols, tiles, cotangent, total, 0, 2 * per_group, per_group)
     own[...] = total[0:rows, :]
     near[...] = total[rows : 2 * rows, :].astype(jnp.bfloat16)
-    far[...] = total[2 * rows : 3 * rows, :].astype(jnp.bfloat16)
+    far[...] = received[2 * rows : 3 * rows, :]
 
 
 def fold_kernel(parts, out):
@@ -168,7 +163,6 @@
     members = lax.axis_size("zl")
     group_rows = rows * members
     core = jnp.stack([lax.axis_index("c"), lax.axis_index("zl")]).astype(jnp.int32)
-    near = near_pairs(groups)
     swap = [(0, 1), (1, 0)]
     smem = pl.BlockSpec(memory_space=pltpu.SMEM)
     vmem = pl.BlockSpec(memory_space=pltpu.VMEM)
@@ -176,22 +170,11 @@
     flops = 2 * 2 * slots * TILE * TILE * width
 
     x0 = lax.all_gather(features, "zl", axis=0, tiled=True)
-    x1 = lax.ppermute(x0, DOM, near)
-    x2 = lax.ppermute(x0, DOM, far_pairs(groups, False))
+    x1 = lax.ppermute(x0, DOM, near_pairs(groups, True))
+    x2 = lax.ppermute(x0, DOM, far_pairs(groups))
     x3 = lax.ppermute(x0, "c", swap)
     x4 = lax.ppermute(x1, "c", swap)
-
-    sent = pl.pallas_call(
-        send_kernel,
-        out_shape=jax.ShapeDtypeStruct((2 * group_rows, width), jnp.bfloat16),
-        in_specs=[smem, smem, smem, vmem, vmem, anywhere],
-        out_specs=vmem,
-        scratch_shapes=[pltpu.VMEM((2 * group_rows, width), jnp.float32)],
-        compiler_params=params(),
-        cost_estimate=pl.CostEstimate(flops=flops, bytes_accessed=4 << 20, transcendentals=0),
-        name="send",
-    )(core, tile_counts, tile_cols, tile_values, cotangent, x0)
-    received = lax.ppermute(sent, "c", swap)
+    x5 = lax.ppermute(x2, "c", swap)
 
     layer_out, local = pl.pallas_call(
         forward_kernel,
@@ -202,13 +185,25 @@
         in_specs=[smem, smem, smem, vmem, vmem, vmem] + [anywhere] * 5,
         out_specs=(vmem, vmem),
         scratch_shapes=[
-            pltpu.VMEM((5 * group_rows, width), jnp.bfloat16),
+            pltpu.VMEM((6 * group_rows, width), jnp.bfloat16),
             pltpu.SemaphoreType.DMA((5,)),
         ],
         compiler_params=params(),
         cost_estimate=pl.CostEstimate(flops=flops, bytes_accessed=6 << 20, transcendentals=0),
         name="forward",
-    )(core, tile_counts, tile_cols, tile_values, weight, cotangent, x0, x1, x2, x3, x4)
+    )(core, tile_counts, tile_cols, tile_values, weight, cotangent, x0, x1, x3, x4, x5)
+
+    sent = pl.pallas_call(
+        send_kernel,
+        out_shape=jax.ShapeDtypeStruct((3 * group_rows, width), jnp.bfloat16),
+        in_specs=[smem, smem, smem, vmem, vmem, anywhere],
+        out_specs=vmem,
+        scratch_shapes=[pltpu.VMEM((3 * group_rows, width), jnp.float32)],
+        compiler_params=params(),
+        cost_estimate=pl.CostEstimate(flops=flops, bytes_accessed=4 << 20, transcendentals=0),
+        name="send",
+    )(core, tile_counts, tile_cols, tile_values, cotangent, local)
+    received = lax.ppermute(sent, "c", swap)
 
     own, near_sum, far_sum = pl.pallas_call(
         keep_kernel,
@@ -219,13 +214,13 @@
         ),
         in_specs=[smem, smem, smem, vmem, vmem, vmem, anywhere],
         out_specs=(vmem, vmem, vmem),
-        scratch_shapes=[pltpu.VMEM((3 * group_rows, width), jnp.float32)],
+        scratch_shapes=[pltpu.VMEM((2 * group_rows, width), jnp.float32)],
         compiler_params=params(),
         cost_estimate=pl.CostEstimate(flops=flops, bytes_accessed=8 << 20, transcendentals=0),
         name="keep",
     )(core, tile_counts, tile_cols, tile_values, cotangent, received, local)
-    near_in = lax.ppermute(near_sum, DOM, near)
-    far_in = lax.ppermute(far_sum, DOM, far_pairs(groups, True))
+    near_in = lax.ppermute(near_sum, DOM, near_pairs(groups, False))
+    far_in = lax.ppermute(far_sum, DOM, far_pairs(groups))
 
     plane = math.prod(lax.axis_size(axis) for axis in PLANE)
     column = math.prod(lax.axis_size(axis) for axis in COLUMN)

time: 153 us -> 170 us (1.11)
  waiting for transfers between devices: 6.57 us -> 18.6 us
  Pallas kernels: 8.84 us -> 14.3 us
    ppermute x4 -> x5, starting transfers between devices: 24.2 us -> 44.5 us  [the longest x1 19.4 us: per_device(): x2 = lax.ppermute(x0, DOM, far_pairs(groups))]
    ppermute x1, starting transfers between devices: 17.1 us -> 1.91 us  [per_device(): received = lax.ppermute(sent, 'c', swap)]
    ppermute x4 -> x5, waiting for transfers between devices: 2.04 us -> 12.8 us  [the longest x1 5.74 us: per_device(): x1 = lax.ppermute(x0, DOM, near_pairs(groups, True))]
    all_to_all x1, starting transfers between devices: 16.3 us -> 6.42 us  [per_device(): parts = lax.all_to_all(local.reshape(plane, -1, TILE), PLANE, 0, 0)]
    pallas_call x1, Pallas kernels: 2.05 us -> 4.97 us  [per_device(): pl.pallas_call(send_kernel, out_shape=jax.ShapeDtypeStruct((3 * group_row...]
    ppermute x1, starting transfers between devices: 2.41 us -> 5.23 us  [per_device(): x4 = lax.ppermute(x1, 'c', swap)]
    pallas_call x1, Pallas kernels: 2.11 us -> 4.59 us  [per_device(): pl.pallas_call(keep_kernel, out_shape=(jax.ShapeDtypeStruct((group_rows,...]
    all_to_all x1, starting transfers between devices: 4.62 us -> 6.99 us  [per_device(): parts = lax.all_to_all(spread, PLANE, 0, 0)]
  transfers between devices with their start and end apart: 12 -> 13, of which waited for: 2 -> 5; matrix products, arithmetic and copies ran while one was open for 0% -> 0% of each run, Pallas kernels for 4% -> 4%
where the time goes in v6:
time: 170 us; the launch traced here: 169 us
  starting transfers between devices  75.9 us (45%)
  blocking collectives  52.5 us (31%)
  waiting for transfers between devices  18.6 us (11%)
  Pallas kernels  14.3 us (8%)
  local copies, waits for them, and re-layouts  6.69 us (4%)
    all_to_all x1, blocking collectives, per_device(): folded = lax.all_to_all(part, COLUMN, 0, 0)  33.9 us
    ppermute x1, starting transfers between devices, per_device(): x2 = lax.ppermute(x0, DOM, far_pairs(groups))  19.4 us
    all_gather x1, blocking collectives, per_device(): x0 = lax.all_gather(features, 'zl', axis=0, tiled=True)  18.6 us
    ppermute x1, starting transfers between devices, per_device(): near_in = lax.ppermute(near_sum, DOM, near_pairs(groups, False))  14.8 us
    ppermute x3, starting transfers between devices, per_device(): lax.ppermute(value, 'zl', [(m, (m + turn + 1) % members) for m in range(m...  9 us
    all_to_all x1, starting transfers between devices, per_device(): parts = lax.all_to_all(spread, PLANE, 0, 0)  6.99 us
    unnamed x24, local copies, waits for them, and re-layouts  6.69 us
    all_to_all x1, starting transfers between devices, per_device(): parts = lax.all_to_all(local.reshape(plane, -1, TILE), PLANE, 0, 0)  6.42 us
  transfers between devices with their start and end apart: 13, of which 5 were waited for; matrix products, arithmetic and copies ran while one was open for 0% of the time, Pallas kernels for 4%

profile of v6, /device:TPU:1, one launch (start us, length us, event | category | flops | bytes accessed | tf_op | source)
XLA Modules:
  0.0 168.9 jit_solution(5999149453616853105)
XLA Ops:
  0.6 18.6 %all_gather.3.x0 = bf16[1024,256]{1,0:T(8,128)(2,1)S(1)} all-gather(bf16[256,256]{1,0:T(8,128)(2,1)} %param.6), channel_id=1, replica_groups=mesh['zh'=2,'x'=8,'y'=8,'c'=2,'zl'=4] {'zl'}, dimensions={0}, use_global_device_ids=true | all-gather | bytes 655360 | tf_op jit(solution)/shard_map/all_gather | solution.py:172
  19.2 5.3 %collective-permute-start = (bf16[1024,256]{1,0:T(8,128)(2,1)S(1)}, bf16[1024,256]{1,0:T(8,128)(2,1)S(1)}, u32[]{:S(2)}, u32[]{:S(2)}) collective-permute-start(bf16[1024,256]{1,0:T(8,128)(2,1)S(1)} %all_gather.3.x0), channel_id=1, source_target_pairs={{0,1016},{4,12},{8,0},{12,20},{16,8},{20,28},{24,16},{28,36},{32,2... | collective-permute-start | bytes 1572872 | tf_op jit(solution)/shard_map/ppermute | solution.py:173
  24.6 19.4 %collective-permute-start.3 = (bf16[1024,256]{1,0:T(8,128)(2,1)S(1)}, bf16[1024,256]{1,0:T(8,128)(2,1)S(1)}, u32[]{:S(2)}, u32[]{:S(2)}) collective-permute-start(bf16[1024,256]{1,0:T(8,128)(2,1)S(1)} %all_gather.3.x0), channel_id=1, source_target_pairs={{0,12},{4,1016},{8,20},{12,0},{16,28},{20,8},{24,36},{28,16},{32,4... | collective-permute-start | bytes 1572872 | tf_op jit(solution)/shard_map/ppermute | solution.py:174
  44.0 1.9 %collective-permute-start.1 = (bf16[1024,256]{1,0:T(8,128)(2,1)S(1)}, bf16[1024,256]{1,0:T(8,128)(2,1)S(1)}, u32[]{:S(2)}, u32[]{:S(2)}) collective-permute-start(bf16[1024,256]{1,0:T(8,128)(2,1)S(1)} %all_gather.3.x0), channel_id=1, source_target_pairs={{0,4},{4,0},{1,5},{5,1},{2,6},{6,2},{3,7},{7,3},{8,12},{12,8},{9,1... | collective-permute-start | bytes 1572872 | tf_op jit(solution)/shard_map/ppermute | solution.py:175
  45.9 5.7 %collective-permute-done.x1 = bf16[1024,256]{1,0:T(8,128)(2,1)S(1)} collective-permute-done((bf16[1024,256]{1,0:T(8,128)(2,1)S(1)}, bf16[1024,256]{1,0:T(8,128)(2,1)S(1)}, u32[]{:S(2)}, u32[]{:S(2)}) %collective-permute-start) | collective-permute-done | bytes 524320 | tf_op jit(solution)/shard_map/ppermute | solution.py:173
  51.7 5.2 %collective-permute-start.2 = (bf16[1024,256]{1,0:T(8,128)(2,1)S(1)}, bf16[1024,256]{1,0:T(8,128)(2,1)S(1)}, u32[]{:S(2)}, u32[]{:S(2)}) collective-permute-start(bf16[1024,256]{1,0:T(8,128)(2,1)S(1)} %collective-permute-done.x1), channel_id=1, source_target_pairs={{0,4},{4,0},{1,5},{5,1},{2,6},{6,2},{3,7},{7,3},{8,12},{12,8},{9,1... | collective-permute-start | bytes 1572872 | tf_op jit(solution)/shard_map/ppermute | solution.py:176
  56.9 5.3 %collective-permute-done.3 = bf16[1024,256]{1,0:T(8,128)(2,1)S(1)} collective-permute-done((bf16[1024,256]{1,0:T(8,128)(2,1)S(1)}, bf16[1024,256]{1,0:T(8,128)(2,1)S(1)}, u32[]{:S(2)}, u32[]{:S(2)}) %collective-permute-start.3) | collective-permute-done | bytes 524320 | tf_op jit(solution)/shard_map/ppermute | solution.py:174
  62.2 1.9 %collective-permute-start.4 = (bf16[1024,256]{1,0:T(8,128)(2,1)S(1)}, bf16[1024,256]{1,0:T(8,128)(2,1)S(1)}, u32[]{:S(2)}, u32[]{:S(2)}) collective-permute-start(bf16[1024,256]{1,0:T(8,128)(2,1)S(1)} %collective-permute-done.3), channel_id=1, source_target_pairs={{0,4},{4,0},{1,5},{5,1},{2,6},{6,2},{3,7},{7,3},{8,12},{12,8},{9,1... | collective-permute-start | bytes 1572872 | tf_op jit(solution)/shard_map/ppermute | solution.py:177
  64.2 1.8 %collective-permute-done.4.x5 = bf16[1024,256]{1,0:T(8,128)(2,1)S(1)} collective-permute-done((bf16[1024,256]{1,0:T(8,128)(2,1)S(1)}, bf16[1024,256]{1,0:T(8,128)(2,1)S(1)}, u32[]{:S(2)}, u32[]{:S(2)}) %collective-permute-start.4) | collective-permute-done | bytes 524320 | tf_op jit(solution)/shard_map/ppermute | solution.py:177
  66.0 1.3 copy-done
  67.3 0.9 copy-done.2
  68.2 0.9 copy-done.6
  69.1 0.7 copy-done.8
  69.8 0.7 copy-done.10
  70.5 2.3 %forward.1 = (bf16[256,256]{1,0:T(8,128)(2,1)}, f32[512,128]{1,0:T(8,128)}) custom-call(s32[2]{0:T(128)S(1)} %pad_add_fusion.place_ref, s32[2]{0:T(128)S(1)} %copy-done.10, s32[2,20]{1,0:T(2,128)S(1)} %copy-done.8, bf16[2,20,128,128]{3,2,1,0:T(8,128)(2,1)S(1)} %copy-done, bf16[256,256]{1,0:T(8,128)(2,1)S(1)} %copy-done.6, bf16[256,256]{1,0:T(8,128)(2,1)S(1)} %copy-done.2, ...), custom_call_target="tpu_custom_call" | custom-call | flops 335544320 | bytes 6291456 | tf_op jit(solution)/shard_map/forward/pallas_call | solution.py:179
  72.8 5.0 %send.1 = bf16[3072,256]{1,0:T(8,128)(2,1)} custom-call(s32[2]{0:T(128)S(1)} %pad_add_fusion.place_ref, s32[2]{0:T(128)S(1)} %copy-done.10, s32[2,20]{1,0:T(2,128)S(1)} %copy-done.8, bf16[2,20,128,128]{3,2,1,0:T(8,128)(2,1)S(1)} %copy-done, bf16[256,256]{1,0:T(8,128)(2,1)S(1)} %copy-done.3, f32[512,128]{1,0:T(8,128)} %get-tuple-element.15.after), custom_call_target="tpu_custom_call" | custom-call | flops 335544320 | bytes 4194304 | tf_op jit(solution)/shard_map/send/pallas_call | solution.py:196
  77.8 1.9 %collective-permute-start.5 = (bf16[3072,256]{1,0:T(8,128)(2,1)}, bf16[3072,256]{1,0:T(8,128)(2,1)S(1)}, u32[]{:S(2)}, u32[]{:S(2)}) collective-permute-start(bf16[3072,256]{1,0:T(8,128)(2,1)} %send.1), channel_id=1, source_target_pairs={{0,4},{4,0},{1,5},{5,1},{2,6},{6,2},{3,7},{7,3},{8,12},{12,8},{9,1... | collective-permute-start | bytes 4718600 | tf_op jit(solution)/shard_map/ppermute | solution.py:206
  79.7 6.4 %all-to-all-start = ((f32[64,8,128]{2,1,0:T(8,128)}), f32[64,8,128]{2,1,0:T(8,128)S(1)}, u32[]{:S(2)}, u32[]{:S(2)}) async-start(f32[64,8,128]{2,1,0:T(8,128)} %bitcast.2), calls=%async_computation | async-start | bytes 524288 | tf_op jit(solution)/shard_map/all_to_all | solution.py:227
  86.2 4.6 %keep.1 = (f32[1024,256]{1,0:T(8,128)S(1)}, bf16[1024,256]{1,0:T(8,128)(2,1)}, bf16[1024,256]{1,0:T(8,128)(2,1)}) custom-call(s32[2]{0:T(128)S(1)} %pad_add_fusion.place_ref, s32[2]{0:T(128)S(1)} %copy-done.11, s32[2,20]{1,0:T(2,128)S(1)} %copy-done.9, bf16[2,20,128,128]{3,2,1,0:T(8,128)(2,1)S(1)} %copy-done.1, bf16[256,256]{1,0:T(8,128)(2,1)S(1)} %copy-done.3, ...), custom_call_target="tpu_custom_call" | custom-call | flops 335544320 | bytes 8388608 | tf_op jit(solution)/shard_map/keep/pallas_call | solution.py:208
  90.8 1.0 copy-done.4
  91.8 14.8 %collective-permute-start.6 = (bf16[1024,256]{1,0:T(8,128)(2,1)}, bf16[1024,256]{1,0:T(8,128)(2,1)S(1)}, u32[]{:S(2)}, u32[]{:S(2)}) collective-permute-start(bf16[1024,256]{1,0:T(8,128)(2,1)} %get-tuple-element.17), channel_id=1, source_target_pairs={{0,8},{4,1020},{8,16},{12,4},{16,24},{20,12},{24,32},{28,20},{32,4... | collective-permute-start | bytes 1572872 | tf_op jit(solution)/shard_map/ppermute | solution.py:222
  106.5 3.0 %collective-permute-start.7 = (bf16[1024,256]{1,0:T(8,128)(2,1)}, bf16[1024,256]{1,0:T(8,128)(2,1)S(1)}, u32[]{:S(2)}, u32[]{:S(2)}) collective-permute-start(bf16[1024,256]{1,0:T(8,128)(2,1)} %get-tuple-element.18), channel_id=1, source_target_pairs={{0,12},{4,1016},{8,20},{12,0},{16,28},{20,8},{24,36},{28,16},{32,4... | collective-permute-start | bytes 1572872 | tf_op jit(solution)/shard_map/ppermute | solution.py:223
  109.7 33.9 %all_to_all.15.folded = f32[16,8,128]{2,1,0:T(8,128)S(1)} all-to-all(f32[16,8,128]{2,1,0:T(8,128)S(1)} %fold.1), channel_id=1, replica_groups=mesh['zh'=2,'x'=8,'y'=8,'c'=2,'zl'=4] {'zh','zl','c'}, dimensions={0} | all-to-all | bytes 131072 | tf_op jit(solution)/shard_map/all_to_all | solution.py:237
  143.6 0.7 spread.1
  144.2 7.0 %all-to-all-start.2 = ((bf16[64,8,128]{2,1,0:T(8,128)(2,1)}), bf16[64,8,128]{2,1,0:T(8,128)(2,1)S(1)}, u32[]{:S(2)}, u32[]{:S(2)}) async-start(bf16[64,8,128]{2,1,0:T(8,128)(2,1)} %spread.1), calls=%async_computation.2 | async-start | bytes 262144 | tf_op jit(solution)/shard_map/all_to_all | solution.py:259
  151.3 1.2 copy-done.5
  152.5 0.7 meet.1
  153.2 1.9 %collective-permute-start.8 = (bf16[256,256]{1,0:T(8,128)(2,1)S(1)}, bf16[256,256]{1,0:T(8,128)(2,1)S(1)}, u32[]{:S(2)}, u32[]{:S(2)}) collective-permute-start(bf16[256,256]{1,0:T(8,128)(2,1)S(1)} %get-tuple-element.20), channel_id=1, source_target_pairs={{0,1},{1,2},{2,3},{3,0},{4,5},{5,6},{6,7},{7,4},{8,9},{9,10},{10,1... | collective-permute-start | bytes 393224 | tf_op jit(solution)/shard_map/ppermute | solution.py:248
  155.1 1.9 %collective-permute-start.9 = (bf16[256,256]{1,0:T(8,128)(2,1)S(1)}, bf16[256,256]{1,0:T(8,128)(2,1)S(1)}, u32[]{:S(2)}, u32[]{:S(2)}) collective-permute-start(bf16[256,256]{1,0:T(8,128)(2,1)S(1)} %get-tuple-element.21), channel_id=1, source_target_pairs={{0,2},{1,3},{2,0},{3,1},{4,6},{5,7},{6,4},{7,5},{8,10},{9,11},{10,... | collective-permute-start | bytes 393224 | tf_op jit(solution)/shard_map/ppermute | solution.py:248
  157.1 5.2 %collective-permute-start.10 = (bf16[256,256]{1,0:T(8,128)(2,1)S(1)}, bf16[256,256]{1,0:T(8,128)(2,1)S(1)}, u32[]{:S(2)}, u32[]{:S(2)}) collective-permute-start(bf16[256,256]{1,0:T(8,128)(2,1)S(1)} %get-tuple-element.22), channel_id=1, source_target_pairs={{0,3},{1,0},{2,1},{3,2},{4,7},{5,4},{6,5},{7,6},{8,11},{9,8},{10,9... | collective-permute-start | bytes 393224 | tf_op jit(solution)/shard_map/ppermute | solution.py:248
  162.7 5.2 %collective-permute-done.9.turn2 = bf16[256,256]{1,0:T(8,128)(2,1)S(1)} collective-permute-done((bf16[256,256]{1,0:T(8,128)(2,1)S(1)}, bf16[256,256]{1,0:T(8,128)(2,1)S(1)}, u32[]{:S(2)}, u32[]{:S(2)}) %collective-permute-start.9) | collective-permute-done | bytes 131104 | tf_op jit(solution)/shard_map/ppermute | solution.py:248
  168.0 0.9 last.1
  (28 shorter events, 0.7 us)
Async XLA Ops:
  19.2 32.4 %collective-permute-start = (bf16[1024,256]{1,0:T(8,128)(2,1)S(1)}, bf16[1024,256]{1,0:T(8,128)(2,1)S(1)}, u32[]{:S(2)}, u32[]{:S(2)}) collective-permute-start(bf16[1024,256]{1,0:T(8,128)(2,1)S(1)} %all_gather.3.x0), channel_id=1, source_target_pairs={{0,1016},{4,12},{8,0},{12,20},{16,8},{20,28},{24,16},{28,36},{32,2... | collective-permute-start | bytes 1572872 | tf_op jit(solution)/shard_map/ppermute | solution.py:173
  24.6 37.6 %collective-permute-start.3 = (bf16[1024,256]{1,0:T(8,128)(2,1)S(1)}, bf16[1024,256]{1,0:T(8,128)(2,1)S(1)}, u32[]{:S(2)}, u32[]{:S(2)}) collective-permute-start(bf16[1024,256]{1,0:T(8,128)(2,1)S(1)} %all_gather.3.x0), channel_id=1, source_target_pairs={{0,12},{4,1016},{8,20},{12,0},{16,28},{20,8},{24,36},{28,16},{32,4... | collective-permute-start | bytes 1572872 | tf_op jit(solution)/shard_map/ppermute | solution.py:174
  44.0 20.2 %collective-permute-start.1 = (bf16[1024,256]{1,0:T(8,128)(2,1)S(1)}, bf16[1024,256]{1,0:T(8,128)(2,1)S(1)}, u32[]{:S(2)}, u32[]{:S(2)}) collective-permute-start(bf16[1024,256]{1,0:T(8,128)(2,1)S(1)} %all_gather.3.x0), channel_id=1, source_target_pairs={{0,4},{4,0},{1,5},{5,1},{2,6},{6,2},{3,7},{7,3},{8,12},{12,8},{9,1... | collective-permute-start | bytes 1572872 | tf_op jit(solution)/shard_map/ppermute | solution.py:175
  51.7 12.5 %collective-permute-start.2 = (bf16[1024,256]{1,0:T(8,128)(2,1)S(1)}, bf16[1024,256]{1,0:T(8,128)(2,1)S(1)}, u32[]{:S(2)}, u32[]{:S(2)}) collective-permute-start(bf16[1024,256]{1,0:T(8,128)(2,1)S(1)} %collective-permute-done.x1), channel_id=1, source_target_pairs={{0,4},{4,0},{1,5},{5,1},{2,6},{6,2},{3,7},{7,3},{8,12},{12,8},{9,1... | collective-permute-start | bytes 1572872 | tf_op jit(solution)/shard_map/ppermute | solution.py:176
  62.2 3.8 %collective-permute-start.4 = (bf16[1024,256]{1,0:T(8,128)(2,1)S(1)}, bf16[1024,256]{1,0:T(8,128)(2,1)S(1)}, u32[]{:S(2)}, u32[]{:S(2)}) collective-permute-start(bf16[1024,256]{1,0:T(8,128)(2,1)S(1)} %collective-permute-done.3), channel_id=1, source_target_pairs={{0,4},{4,0},{1,5},{5,1},{2,6},{6,2},{3,7},{7,3},{8,12},{12,8},{9,1... | collective-permute-start | bytes 1572872 | tf_op jit(solution)/shard_map/ppermute | solution.py:177
  66.0 1.3 copy-start
  67.3 0.9 copy-start.2
  68.2 0.9 copy-start.6
  69.1 0.7 copy-start.8
  69.8 0.7 copy-start.10
  70.5 2.3 %copy-start.3 = (bf16[256,256]{1,0:T(8,128)(2,1)S(1)}, bf16[256,256]{1,0:T(8,128)(2,1)}, u32[]{:S(2)}) copy-start(bf16[256,256]{1,0:T(8,128)(2,1)} %cotangent.5) | copy-start | bytes 393220
  72.8 13.4 %copy-start.1 = (bf16[2,20,128,128]{3,2,1,0:T(8,128)(2,1)S(1)}, bf16[2,20,128,128]{3,2,1,0:T(8,128)(2,1)}, u32[]{:S(2)}) copy-start(bf16[2,20,128,128]{3,2,1,0:T(8,128)(2,1)} %tiles.5) | copy-start | bytes 3932164
  72.8 13.4 %copy-start.9 = (s32[2,20]{1,0:T(2,128)S(1)}, s32[2,20]{1,0:T(2,128)}, u32[]{:S(2)}) copy-start(s32[2,20]{1,0:T(2,128)} %cols.5) | copy-start | bytes 484
  72.8 13.4 %copy-start.11 = (s32[2]{0:T(128)S(1)}, s32[2]{0:T(128)}, u32[]{:S(2)}) copy-start(s32[2]{0:T(128)} %counts.5) | copy-start | bytes 28
  77.8 8.3 %collective-permute-start.5 = (bf16[3072,256]{1,0:T(8,128)(2,1)}, bf16[3072,256]{1,0:T(8,128)(2,1)S(1)}, u32[]{:S(2)}, u32[]{:S(2)}) collective-permute-start(bf16[3072,256]{1,0:T(8,128)(2,1)} %send.1), channel_id=1, source_target_pairs={{0,4},{4,0},{1,5},{5,1},{2,6},{6,2},{3,7},{7,3},{8,12},{12,8},{9,1... | collective-permute-start | bytes 4718600 | tf_op jit(solution)/shard_map/ppermute | solution.py:206
  79.7 29.9 %all-to-all-start = ((f32[64,8,128]{2,1,0:T(8,128)}), f32[64,8,128]{2,1,0:T(8,128)S(1)}, u32[]{:S(2)}, u32[]{:S(2)}) async-start(f32[64,8,128]{2,1,0:T(8,128)} %bitcast.2), calls=%async_computation | async-start | bytes 524288 | tf_op jit(solution)/shard_map/all_to_all | solution.py:227
  90.8 1.0 copy-start.4
  91.8 76.2 %copy-start.7 = (bf16[256,256]{1,0:T(8,128)(2,1)S(1)}, bf16[256,256]{1,0:T(8,128)(2,1)}, u32[]{:S(2)}) copy-start(bf16[256,256]{1,0:T(8,128)(2,1)} %weight.3) | copy-start | bytes 393220
  91.8 59.5 %collective-permute-start.6 = (bf16[1024,256]{1,0:T(8,128)(2,1)}, bf16[1024,256]{1,0:T(8,128)(2,1)S(1)}, u32[]{:S(2)}, u32[]{:S(2)}) collective-permute-start(bf16[1024,256]{1,0:T(8,128)(2,1)} %get-tuple-element.17), channel_id=1, source_target_pairs={{0,8},{4,1020},{8,16},{12,4},{16,24},{20,12},{24,32},{28,20},{32,4... | collective-permute-start | bytes 1572872 | tf_op jit(solution)/shard_map/ppermute | solution.py:222
  106.5 44.7 %collective-permute-start.7 = (bf16[1024,256]{1,0:T(8,128)(2,1)}, bf16[1024,256]{1,0:T(8,128)(2,1)S(1)}, u32[]{:S(2)}, u32[]{:S(2)}) collective-permute-start(bf16[1024,256]{1,0:T(8,128)(2,1)} %get-tuple-element.18), channel_id=1, source_target_pairs={{0,12},{4,1016},{8,20},{12,0},{16,28},{20,8},{24,36},{28,16},{32,4... | collective-permute-start | bytes 1572872 | tf_op jit(solution)/shard_map/ppermute | solution.py:223
  144.2 18.5 %all-to-all-start.2 = ((bf16[64,8,128]{2,1,0:T(8,128)(2,1)}), bf16[64,8,128]{2,1,0:T(8,128)(2,1)S(1)}, u32[]{:S(2)}, u32[]{:S(2)}) async-start(bf16[64,8,128]{2,1,0:T(8,128)(2,1)} %spread.1), calls=%async_computation.2 | async-start | bytes 262144 | tf_op jit(solution)/shard_map/all_to_all | solution.py:259
  151.3 1.2 copy-start.5
  153.2 9.5 %collective-permute-start.8 = (bf16[256,256]{1,0:T(8,128)(2,1)S(1)}, bf16[256,256]{1,0:T(8,128)(2,1)S(1)}, u32[]{:S(2)}, u32[]{:S(2)}) collective-permute-start(bf16[256,256]{1,0:T(8,128)(2,1)S(1)} %get-tuple-element.20), channel_id=1, source_target_pairs={{0,1},{1,2},{2,3},{3,0},{4,5},{5,6},{6,7},{7,4},{8,9},{9,10},{10,1... | collective-permute-start | bytes 393224 | tf_op jit(solution)/shard_map/ppermute | solution.py:248
  155.1 12.8 %collective-permute-start.9 = (bf16[256,256]{1,0:T(8,128)(2,1)S(1)}, bf16[256,256]{1,0:T(8,128)(2,1)S(1)}, u32[]{:S(2)}, u32[]{:S(2)}) collective-permute-start(bf16[256,256]{1,0:T(8,128)(2,1)S(1)} %get-tuple-element.21), channel_id=1, source_target_pairs={{0,2},{1,3},{2,0},{3,1},{4,6},{5,7},{6,4},{7,5},{8,10},{9,11},{10,... | collective-permute-start | bytes 393224 | tf_op jit(solution)/shard_map/ppermute | solution.py:248
  157.1 10.9 %collective-permute-start.10 = (bf16[256,256]{1,0:T(8,128)(2,1)S(1)}, bf16[256,256]{1,0:T(8,128)(2,1)S(1)}, u32[]{:S(2)}, u32[]{:S(2)}) collective-permute-start(bf16[256,256]{1,0:T(8,128)(2,1)S(1)} %get-tuple-element.22), channel_id=1, source_target_pairs={{0,3},{1,0},{2,1},{3,2},{4,7},{5,4},{6,5},{7,6},{8,11},{9,8},{10,9... | collective-permute-start | bytes 393224 | tf_op jit(solution)/shard_map/ppermute | solution.py:248

commit v7 on v3

--- a/solution.py
+++ b/solution.py
@@ -120,7 +120,8 @@
         out[i] = part
 
 
-def spread_kernel(scale, folded, spread):
+def spread_kernel(scale, folded, *refs):
+    spread = refs[-1]
     part = (jnp.sum(folded[...], 0) * scale).astype(jnp.bfloat16)
     for i in range(spread.shape[0]):
         spread[i] = part
@@ -256,11 +257,11 @@
     spread = pl.pallas_call(
         functools.partial(spread_kernel, 1 / math.sqrt(rows * groups * members)),
         out_shape=jax.ShapeDtypeStruct(parts.shape, jnp.bfloat16),
-        in_specs=[vmem],
+        in_specs=[vmem] + [anywhere],
         out_specs=vmem,
         compiler_params=params(),
         name="spread",
-    )(folded)
+    )(folded, mine)
     parts = lax.all_to_all(spread, PLANE, 0, 0)
     feat_grad, weight_grad = pl.pallas_call(
         last_kernel,

time: 153 us -> 152 us (level)
  blocking collectives: 53.6 us -> 18.6 us
  waiting for transfers between devices: 6.57 us -> 32.2 us
  Pallas kernels: 8.84 us -> 13.9 us
  starting transfers between devices: 76.6 us -> 80.6 us
    all_to_all x1 -> x0, blocking collectives: 35 us -> none  [per_device(): folded = lax.all_to_all(part, COLUMN, 0, 0)]
    ppermute x1, waiting for transfers between devices: 0.01 us -> 23.7 us  [per_device(): far_in = lax.ppermute(far_sum, DOM, far_pairs(groups, True))]
    all_to_all x0 -> x1, starting transfers between devices: none -> 10.3 us  [per_device(): folded = lax.all_to_all(part, COLUMN, 0, 0)]
    ppermute x1, starting transfers between devices: 9.67 us -> 5.96 us  [per_device(): near_in = lax.ppermute(near_sum, DOM, near)]
    ppermute x1, starting transfers between devices: 17.1 us -> 13.7 us  [per_device(): received = lax.ppermute(sent, 'c', swap)]
    all_to_all x1, starting transfers between devices: 16.3 us -> 13.4 us  [per_device(): parts = lax.all_to_all(local.reshape(plane, -1, TILE), PLANE, 0, 0)]
    pallas_call x1, Pallas kernels: 2.05 us -> 4.34 us  [per_device(): pl.pallas_call(send_kernel, out_shape=jax.ShapeDtypeStruct((2 * group_row...]
    pallas_call x1, Pallas kernels: 2.11 us -> 4.21 us  [per_device(): pl.pallas_call(keep_kernel, out_shape=(jax.ShapeDtypeStruct((group_rows,...]
  transfers between devices with their start and end apart: 12 -> 13, of which waited for: 2 -> 5; matrix products, arithmetic and copies ran while one was open for 0% -> 0% of each run, Pallas kernels for 4% -> 5%
where the time goes in v7:
time: 152 us
  starting transfers between devices  80.6 us (53%)
  waiting for transfers between devices  32.2 us (21%)
  blocking collectives  18.6 us (12%)
  Pallas kernels  13.9 us (9%)
  local copies, waits for them, and re-layouts  5.78 us (4%)
    ppermute x1, waiting for transfers between devices, per_device(): far_in = lax.ppermute(far_sum, DOM, far_pairs(groups, True))  23.7 us
    all_gather x1, blocking collectives, per_device(): x0 = lax.all_gather(features, 'zl', axis=0, tiled=True)  18.6 us
    ppermute x1, starting transfers between devices, per_device(): received = lax.ppermute(sent, 'c', swap)  13.7 us
    all_to_all x1, starting transfers between devices, per_device(): parts = lax.all_to_all(local.reshape(plane, -1, TILE), PLANE, 0, 0)  13.4 us
    ppermute x3, starting transfers between devices, per_device(): lax.ppermute(value, 'zl', [(m, (m + turn + 1) % members) for m in range(m...  11.1 us
    all_to_all x1, starting transfers between devices, per_device(): folded = lax.all_to_all(part, COLUMN, 0, 0)  10.3 us
    ppermute x1, starting transfers between devices, per_device(): x1 = lax.ppermute(x0, DOM, near)  7.33 us
    ppermute x1, starting transfers between devices, per_device(): near_in = lax.ppermute(near_sum, DOM, near)  5.96 us
  transfers between devices with their start and end apart: 13, of which 5 were waited for; matrix products, arithmetic and copies ran while one was open for 0% of the time, Pallas kernels for 5%

profile of v7, /device:TPU:1, one launch (start us, length us, event | category | flops | bytes accessed | tf_op | source)
XLA Modules:
  0.0 151.9 jit_solution(694787361544620085)
XLA Ops:
  0.6 18.6 %all_gather.3.x0.after = bf16[1024,256]{1,0:T(8,128)(2,1)S(1)} all-gather(bf16[256,256]{1,0:T(8,128)(2,1)} %param.6), channel_id=1, replica_groups=mesh['zh'=2,'x'=8,'y'=8,'c'=2,'zl'=4] {'zl'}, dimensions={0}, use_global_device_ids=true | all-gather | bytes 655360 | tf_op jit(solution)/shard_map/all_gather | solution.py:179
  19.2 7.3 %collective-permute-start = (bf16[1024,256]{1,0:T(8,128)(2,1)S(1)}, bf16[1024,256]{1,0:T(8,128)(2,1)S(1)}, u32[]{:S(2)}, u32[]{:S(2)}) collective-permute-start(bf16[1024,256]{1,0:T(8,128)(2,1)S(1)} %all_gather.3.x0.after), channel_id=1, source_target_pairs={{0,1020},{4,8},{8,4},{12,16},{16,12},{20,24},{24,20},{28,32},{32,2... | collective-permute-start | bytes 1572872 | tf_op jit(solution)/shard_map/ppermute | solution.py:180
  26.7 1.3 copy-done
  28.0 0.9 copy-done.2
  28.9 0.7 copy-done.8
  29.6 0.7 copy-done.10
  30.2 4.3 %send.1 = bf16[2048,256]{1,0:T(8,128)(2,1)} custom-call(s32[2]{0:T(128)S(1)} %pad_add_fusion.place_ref, s32[2]{0:T(128)S(1)} %copy-done.10, s32[2,20]{1,0:T(2,128)S(1)} %copy-done.8, bf16[2,20,128,128]{3,2,1,0:T(8,128)(2,1)S(1)} %copy-done, bf16[256,256]{1,0:T(8,128)(2,1)S(1)} %copy-done.2, bf16[1024,256]{1,0:T(8,128)(2,1)S(1)} %all_gather.3.x0.after), custom_call_target="tpu_custom_call" | custom-call | flops 335544320 | bytes 4194304 | tf_op jit(solution)/shard_map/send/pallas_call | solution.py:185
  34.6 13.7 %collective-permute-start.4 = (bf16[2048,256]{1,0:T(8,128)(2,1)}, bf16[2048,256]{1,0:T(8,128)(2,1)S(1)}, u32[]{:S(2)}, u32[]{:S(2)}) collective-permute-start(bf16[2048,256]{1,0:T(8,128)(2,1)} %send.1), channel_id=1, source_target_pairs={{0,4},{4,0},{1,5},{5,1},{2,6},{6,2},{3,7},{7,3},{8,12},{12,8},{9,1... | collective-permute-start | bytes 3145736 | tf_op jit(solution)/shard_map/ppermute | solution.py:195
  48.3 5.6 %collective-permute-start.1 = (bf16[1024,256]{1,0:T(8,128)(2,1)S(1)}, bf16[1024,256]{1,0:T(8,128)(2,1)S(1)}, u32[]{:S(2)}, u32[]{:S(2)}) collective-permute-start(bf16[1024,256]{1,0:T(8,128)(2,1)S(1)} %all_gather.3.x0.after), channel_id=1, source_target_pairs={{0,8},{4,1020},{8,16},{12,4},{16,24},{20,12},{24,32},{28,20},{32,4... | collective-permute-start | bytes 1572872 | tf_op jit(solution)/shard_map/ppermute | solution.py:181
  53.9 1.9 %collective-permute-start.2 = (bf16[1024,256]{1,0:T(8,128)(2,1)S(1)}, bf16[1024,256]{1,0:T(8,128)(2,1)S(1)}, u32[]{:S(2)}, u32[]{:S(2)}) collective-permute-start(bf16[1024,256]{1,0:T(8,128)(2,1)S(1)} %all_gather.3.x0.after), channel_id=1, source_target_pairs={{0,4},{4,0},{1,5},{5,1},{2,6},{6,2},{3,7},{7,3},{8,12},{12,8},{9,1... | collective-permute-start | bytes 1572872 | tf_op jit(solution)/shard_map/ppermute | solution.py:182
  55.8 2.4 %collective-permute-start.3 = (bf16[1024,256]{1,0:T(8,128)(2,1)S(1)}, bf16[1024,256]{1,0:T(8,128)(2,1)S(1)}, u32[]{:S(2)}, u32[]{:S(2)}) collective-permute-start(bf16[1024,256]{1,0:T(8,128)(2,1)S(1)} %collective-permute-done.x1), channel_id=1, source_target_pairs={{0,4},{4,0},{1,5},{5,1},{2,6},{6,2},{3,7},{7,3},{8,12},{12,8},{9,1... | collective-permute-start | bytes 1572872 | tf_op jit(solution)/shard_map/ppermute | solution.py:183
  58.2 2.6 %collective-permute-done.1.x2 = bf16[1024,256]{1,0:T(8,128)(2,1)S(1)} collective-permute-done((bf16[1024,256]{1,0:T(8,128)(2,1)S(1)}, bf16[1024,256]{1,0:T(8,128)(2,1)S(1)}, u32[]{:S(2)}, u32[]{:S(2)}) %collective-permute-start.1) | collective-permute-done | bytes 524320 | tf_op jit(solution)/shard_map/ppermute | solution.py:181
  60.8 2.3 %forward.1 = (bf16[256,256]{1,0:T(8,128)(2,1)}, f32[512,128]{1,0:T(8,128)}) custom-call(s32[2]{0:T(128)S(1)} %pad_add_fusion.place_ref, s32[2]{0:T(128)S(1)} %copy-done.11, s32[2,20]{1,0:T(2,128)S(1)} %copy-done.8, bf16[2,20,128,128]{3,2,1,0:T(8,128)(2,1)S(1)} %copy-done, bf16[256,256]{1,0:T(8,128)(2,1)S(1)} %copy-done.6, bf16[256,256]{1,0:T(8,128)(2,1)S(1)} %copy-done.3, ...), custom_call_target="tpu_custom_call" | custom-call | flops 335544320 | bytes 6291456 | tf_op jit(solution)/shard_map/forward/pallas_call | solution.py:197
  63.1 13.4 %all-to-all-start = ((f32[64,8,128]{2,1,0:T(8,128)}), f32[64,8,128]{2,1,0:T(8,128)S(1)}, u32[]{:S(2)}, u32[]{:S(2)}) async-start(f32[64,8,128]{2,1,0:T(8,128)} %bitcast.2), calls=%async_computation | async-start | bytes 524288 | tf_op jit(solution)/shard_map/all_to_all | solution.py:233
  76.6 1.0 copy-done.4
  77.6 1.2 copy-done.5
  78.8 4.2 %keep.1 = (f32[1024,256]{1,0:T(8,128)S(1)}, bf16[1024,256]{1,0:T(8,128)(2,1)}, bf16[1024,256]{1,0:T(8,128)(2,1)S(1)}) custom-call(s32[2]{0:T(128)S(1)} %pad_add_fusion.place_ref, s32[2]{0:T(128)S(1)} %copy-done.11, s32[2,20]{1,0:T(2,128)S(1)} %copy-done.9, bf16[2,20,128,128]{3,2,1,0:T(8,128)(2,1)S(1)} %copy-done.1, bf16[256,256]{1,0:T(8,128)(2,1)S(1)} %copy-done.3, ...), custom_call_target="tpu_custom_call" | custom-call | flops 335544320 | bytes 8388608 | tf_op jit(solution)/shard_map/keep/pallas_call | solution.py:214
  83.0 6.0 %collective-permute-start.5 = (bf16[1024,256]{1,0:T(8,128)(2,1)}, bf16[1024,256]{1,0:T(8,128)(2,1)S(1)}, u32[]{:S(2)}, u32[]{:S(2)}) collective-permute-start(bf16[1024,256]{1,0:T(8,128)(2,1)} %get-tuple-element.17), channel_id=1, source_target_pairs={{0,1020},{4,8},{8,4},{12,16},{16,12},{20,24},{24,20},{28,32},{32,2... | collective-permute-start | bytes 1572872 | tf_op jit(solution)/shard_map/ppermute | solution.py:228
  89.0 4.0 %collective-permute-start.6 = (bf16[1024,256]{1,0:T(8,128)(2,1)S(1)}, bf16[1024,256]{1,0:T(8,128)(2,1)S(1)}, u32[]{:S(2)}, u32[]{:S(2)}) collective-permute-start(bf16[1024,256]{1,0:T(8,128)(2,1)S(1)} %get-tuple-element.18), channel_id=1, source_target_pairs={{0,1016},{4,12},{8,0},{12,20},{16,8},{20,28},{24,16},{28,36},{32,2... | collective-permute-start | bytes 1572872 | tf_op jit(solution)/shard_map/ppermute | solution.py:229
  93.0 0.7 fold.1
  93.7 10.3 %all-to-all-start.1 = ((f32[16,8,128]{2,1,0:T(8,128)}), f32[16,8,128]{2,1,0:T(8,128)S(1)}, u32[]{:S(2)}, u32[]{:S(2)}) async-start(f32[16,8,128]{2,1,0:T(8,128)} %fold.1), calls=%async_computation.1 | async-start | bytes 131072 | tf_op jit(solution)/shard_map/all_to_all | solution.py:243
  104.0 23.7 %collective-permute-done.6.far = bf16[1024,256]{1,0:T(8,128)(2,1)S(1)} collective-permute-done((bf16[1024,256]{1,0:T(8,128)(2,1)S(1)}, bf16[1024,256]{1,0:T(8,128)(2,1)S(1)}, u32[]{:S(2)}, u32[]{:S(2)}) %collective-permute-start.6) | collective-permute-done | bytes 524320 | tf_op jit(solution)/shard_map/ppermute | solution.py:229
  127.7 0.7 meet.1
  128.4 0.5 all-to-all-done.1.folded
  128.9 0.7 spread.1
  129.5 4.9 %all-to-all-start.2 = ((bf16[64,8,128]{2,1,0:T(8,128)(2,1)}), bf16[64,8,128]{2,1,0:T(8,128)(2,1)S(1)}, u32[]{:S(2)}, u32[]{:S(2)}) async-start(bf16[64,8,128]{2,1,0:T(8,128)(2,1)} %spread.1), calls=%async_computation.2 | async-start | bytes 262144 | tf_op jit(solution)/shard_map/all_to_all | solution.py:265
  134.4 4.3 %collective-permute-start.7 = (bf16[256,256]{1,0:T(8,128)(2,1)S(1)}, bf16[256,256]{1,0:T(8,128)(2,1)S(1)}, u32[]{:S(2)}, u32[]{:S(2)}) collective-permute-start(bf16[256,256]{1,0:T(8,128)(2,1)S(1)} %get-tuple-element.20), channel_id=1, source_target_pairs={{0,1},{1,2},{2,3},{3,0},{4,5},{5,6},{6,7},{7,4},{8,9},{9,10},{10,1... | collective-permute-start | bytes 393224 | tf_op jit(solution)/shard_map/ppermute | solution.py:254
  138.7 3.8 %collective-permute-start.8 = (bf16[256,256]{1,0:T(8,128)(2,1)S(1)}, bf16[256,256]{1,0:T(8,128)(2,1)S(1)}, u32[]{:S(2)}, u32[]{:S(2)}) collective-permute-start(bf16[256,256]{1,0:T(8,128)(2,1)S(1)} %get-tuple-element.21), channel_id=1, source_target_pairs={{0,2},{1,3},{2,0},{3,1},{4,6},{5,7},{6,4},{7,5},{8,10},{9,11},{10,... | collective-permute-start | bytes 393224 | tf_op jit(solution)/shard_map/ppermute | solution.py:254
  142.5 3.0 %collective-permute-start.9 = (bf16[256,256]{1,0:T(8,128)(2,1)S(1)}, bf16[256,256]{1,0:T(8,128)(2,1)S(1)}, u32[]{:S(2)}, u32[]{:S(2)}) collective-permute-start(bf16[256,256]{1,0:T(8,128)(2,1)S(1)} %get-tuple-element.22), channel_id=1, source_target_pairs={{0,3},{1,0},{2,1},{3,2},{4,7},{5,4},{6,5},{7,6},{8,11},{9,8},{10,9... | collective-permute-start | bytes 393224 | tf_op jit(solution)/shard_map/ppermute | solution.py:254
  145.5 3.8 %collective-permute-done.8.turn2 = bf16[256,256]{1,0:T(8,128)(2,1)S(1)} collective-permute-done((bf16[256,256]{1,0:T(8,128)(2,1)S(1)}, bf16[256,256]{1,0:T(8,128)(2,1)S(1)}, u32[]{:S(2)}, u32[]{:S(2)}) %collective-permute-start.8) | collective-permute-done | bytes 131104 | tf_op jit(solution)/shard_map/ppermute | solution.py:254
  149.3 1.6 %collective-permute-done.9.turn3 = bf16[256,256]{1,0:T(8,128)(2,1)S(1)} collective-permute-done((bf16[256,256]{1,0:T(8,128)(2,1)S(1)}, bf16[256,256]{1,0:T(8,128)(2,1)S(1)}, u32[]{:S(2)}, u32[]{:S(2)}) %collective-permute-start.9) | collective-permute-done | bytes 131104 | tf_op jit(solution)/shard_map/ppermute | solution.py:254
  151.0 0.9 last.1
  (27 shorter events, 0.1 us)
Async XLA Ops:
  19.2 36.6 %collective-permute-start = (bf16[1024,256]{1,0:T(8,128)(2,1)S(1)}, bf16[1024,256]{1,0:T(8,128)(2,1)S(1)}, u32[]{:S(2)}, u32[]{:S(2)}) collective-permute-start(bf16[1024,256]{1,0:T(8,128)(2,1)S(1)} %all_gather.3.x0.after), channel_id=1, source_target_pairs={{0,1020},{4,8},{8,4},{12,16},{16,12},{20,24},{24,20},{28,32},{32,2... | collective-permute-start | bytes 1572872 | tf_op jit(solution)/shard_map/ppermute | solution.py:180
  26.7 1.3 copy-start
  28.0 0.9 copy-start.2
  28.9 0.7 copy-start.8
  29.6 0.7 copy-start.10
  30.2 30.6 %copy-start.3 = (bf16[256,256]{1,0:T(8,128)(2,1)S(1)}, bf16[256,256]{1,0:T(8,128)(2,1)}, u32[]{:S(2)}) copy-start(bf16[256,256]{1,0:T(8,128)(2,1)} %cotangent.5) | copy-start | bytes 393220
  30.2 30.6 %copy-start.6 = (bf16[256,256]{1,0:T(8,128)(2,1)S(1)}, bf16[256,256]{1,0:T(8,128)(2,1)}, u32[]{:S(2)}) copy-start(bf16[256,256]{1,0:T(8,128)(2,1)} %weight.3) | copy-start | bytes 393220
  30.2 30.6 %copy-start.11 = (s32[2]{0:T(128)S(1)}, s32[2]{0:T(128)}, u32[]{:S(2)}) copy-start(s32[2]{0:T(128)} %counts.5) | copy-start | bytes 28
  34.6 43.0 %copy-start.9 = (s32[2,20]{1,0:T(2,128)S(1)}, s32[2,20]{1,0:T(2,128)}, u32[]{:S(2)}) copy-start(s32[2,20]{1,0:T(2,128)} %cols.5) | copy-start | bytes 484
  34.6 42.0 %collective-permute-start.4 = (bf16[2048,256]{1,0:T(8,128)(2,1)}, bf16[2048,256]{1,0:T(8,128)(2,1)S(1)}, u32[]{:S(2)}, u32[]{:S(2)}) collective-permute-start(bf16[2048,256]{1,0:T(8,128)(2,1)} %send.1), channel_id=1, source_target_pairs={{0,4},{4,0},{1,5},{5,1},{2,6},{6,2},{3,7},{7,3},{8,12},{12,8},{9,1... | collective-permute-start | bytes 3145736 | tf_op jit(solution)/shard_map/ppermute | solution.py:195
  48.3 12.5 %collective-permute-start.1 = (bf16[1024,256]{1,0:T(8,128)(2,1)S(1)}, bf16[1024,256]{1,0:T(8,128)(2,1)S(1)}, u32[]{:S(2)}, u32[]{:S(2)}) collective-permute-start(bf16[1024,256]{1,0:T(8,128)(2,1)S(1)} %all_gather.3.x0.after), channel_id=1, source_target_pairs={{0,8},{4,1020},{8,16},{12,4},{16,24},{20,12},{24,32},{28,20},{32,4... | collective-permute-start | bytes 1572872 | tf_op jit(solution)/shard_map/ppermute | solution.py:181
  53.9 6.9 %collective-permute-start.2 = (bf16[1024,256]{1,0:T(8,128)(2,1)S(1)}, bf16[1024,256]{1,0:T(8,128)(2,1)S(1)}, u32[]{:S(2)}, u32[]{:S(2)}) collective-permute-start(bf16[1024,256]{1,0:T(8,128)(2,1)S(1)} %all_gather.3.x0.after), channel_id=1, source_target_pairs={{0,4},{4,0},{1,5},{5,1},{2,6},{6,2},{3,7},{7,3},{8,12},{12,8},{9,1... | collective-permute-start | bytes 1572872 | tf_op jit(solution)/shard_map/ppermute | solution.py:182
  55.8 5.0 %collective-permute-start.3 = (bf16[1024,256]{1,0:T(8,128)(2,1)S(1)}, bf16[1024,256]{1,0:T(8,128)(2,1)S(1)}, u32[]{:S(2)}, u32[]{:S(2)}) collective-permute-start(bf16[1024,256]{1,0:T(8,128)(2,1)S(1)} %collective-permute-done.x1), channel_id=1, source_target_pairs={{0,4},{4,0},{1,5},{5,1},{2,6},{6,2},{3,7},{7,3},{8,12},{12,8},{9,1... | collective-permute-start | bytes 1572872 | tf_op jit(solution)/shard_map/ppermute | solution.py:183
  60.8 16.7 %copy-start.1 = (bf16[2,20,128,128]{3,2,1,0:T(8,128)(2,1)S(1)}, bf16[2,20,128,128]{3,2,1,0:T(8,128)(2,1)}, u32[]{:S(2)}) copy-start(bf16[2,20,128,128]{3,2,1,0:T(8,128)(2,1)} %tiles.5) | copy-start | bytes 3932164
  63.1 29.8 %all-to-all-start = ((f32[64,8,128]{2,1,0:T(8,128)}), f32[64,8,128]{2,1,0:T(8,128)S(1)}, u32[]{:S(2)}, u32[]{:S(2)}) async-start(f32[64,8,128]{2,1,0:T(8,128)} %bitcast.2), calls=%async_computation | async-start | bytes 524288 | tf_op jit(solution)/shard_map/all_to_all | solution.py:233
  76.6 1.0 copy-start.4
  77.6 1.2 copy-start.5
  83.0 21.0 %collective-permute-start.5 = (bf16[1024,256]{1,0:T(8,128)(2,1)}, bf16[1024,256]{1,0:T(8,128)(2,1)S(1)}, u32[]{:S(2)}, u32[]{:S(2)}) collective-permute-start(bf16[1024,256]{1,0:T(8,128)(2,1)} %get-tuple-element.17), channel_id=1, source_target_pairs={{0,1020},{4,8},{8,4},{12,16},{16,12},{20,24},{24,20},{28,32},{32,2... | collective-permute-start | bytes 1572872 | tf_op jit(solution)/shard_map/ppermute | solution.py:228
  89.0 38.7 %collective-permute-start.6 = (bf16[1024,256]{1,0:T(8,128)(2,1)S(1)}, bf16[1024,256]{1,0:T(8,128)(2,1)S(1)}, u32[]{:S(2)}, u32[]{:S(2)}) collective-permute-start(bf16[1024,256]{1,0:T(8,128)(2,1)S(1)} %get-tuple-element.18), channel_id=1, source_target_pairs={{0,1016},{4,12},{8,0},{12,20},{16,8},{20,28},{24,16},{28,36},{32,2... | collective-permute-start | bytes 1572872 | tf_op jit(solution)/shard_map/ppermute | solution.py:229
  93.7 35.2 %all-to-all-start.1 = ((f32[16,8,128]{2,1,0:T(8,128)}), f32[16,8,128]{2,1,0:T(8,128)S(1)}, u32[]{:S(2)}, u32[]{:S(2)}) async-start(f32[16,8,128]{2,1,0:T(8,128)} %fold.1), calls=%async_computation.1 | async-start | bytes 131072 | tf_op jit(solution)/shard_map/all_to_all | solution.py:243
  127.7 23.3 %copy-start.7 = (bf16[256,256]{1,0:T(8,128)(2,1)S(1)}, bf16[256,256]{1,0:T(8,128)(2,1)}, u32[]{:S(2)}) copy-start(bf16[256,256]{1,0:T(8,128)(2,1)} %weight.3) | copy-start | bytes 393220
  129.5 21.4 %all-to-all-start.2 = ((bf16[64,8,128]{2,1,0:T(8,128)(2,1)}), bf16[64,8,128]{2,1,0:T(8,128)(2,1)S(1)}, u32[]{:S(2)}, u32[]{:S(2)}) async-start(bf16[64,8,128]{2,1,0:T(8,128)(2,1)} %spread.1), calls=%async_computation.2 | async-start | bytes 262144 | tf_op jit(solution)/shard_map/all_to_all | solution.py:265
  134.4 11.1 %collective-permute-start.7 = (bf16[256,256]{1,0:T(8,128)(2,1)S(1)}, bf16[256,256]{1,0:T(8,128)(2,1)S(1)}, u32[]{:S(2)}, u32[]{:S(2)}) collective-permute-start(bf16[256,256]{1,0:T(8,128)(2,1)S(1)} %get-tuple-element.20), channel_id=1, source_target_pairs={{0,1},{1,2},{2,3},{3,0},{4,5},{5,6},{6,7},{7,4},{8,9},{9,10},{10,1... | collective-permute-start | bytes 393224 | tf_op jit(solution)/shard_map/ppermute | solution.py:254
  138.7 10.6 %collective-permute-start.8 = (bf16[256,256]{1,0:T(8,128)(2,1)S(1)}, bf16[256,256]{1,0:T(8,128)(2,1)S(1)}, u32[]{:S(2)}, u32[]{:S(2)}) collective-permute-start(bf16[256,256]{1,0:T(8,128)(2,1)S(1)} %get-tuple-element.21), channel_id=1, source_target_pairs={{0,2},{1,3},{2,0},{3,1},{4,6},{5,7},{6,4},{7,5},{8,10},{9,11},{10,... | collective-permute-start | bytes 393224 | tf_op jit(solution)/shard_map/ppermute | solution.py:254
  142.5 8.5 %collective-permute-start.9 = (bf16[256,256]{1,0:T(8,128)(2,1)S(1)}, bf16[256,256]{1,0:T(8,128)(2,1)S(1)}, u32[]{:S(2)}, u32[]{:S(2)}) collective-permute-start(bf16[256,256]{1,0:T(8,128)(2,1)S(1)} %get-tuple-element.22), channel_id=1, source_target_pairs={{0,3},{1,0},{2,1},{3,2},{4,7},{5,4},{6,5},{7,6},{8,11},{9,8},{10,9... | collective-permute-start | bytes 393224 | tf_op jit(solution)/shard_map/ppermute | solution.py:254
